TPU v7x, 32 devices: a whole 2x2x4 slice. The times are simulated.
32 devices in a mesh: pop: 4 (over x, core), shard: 8 (over z, y).
Axes of the slice: x: 2, y: 2, z: 4, core: 2. Of those that a mesh axis runs over, the one named last changes fastest.
Arguments:
- tokens: bfloat16 [8, 480, 4096], P('pop'), may hold values from -6 to 6
- gate_weight_matrix: bfloat16 [4096, 14336], P('pop', 'shard'), may hold values from -0.09375 to 0.09375
- w_up: bfloat16 [4096, 14336], P('pop', 'shard'), may hold values from -0.09375 to 0.09375
- a_gate: bfloat16 [8, 4, 4096], P('pop'), may hold values from -5 to 5
- a_up: bfloat16 [8, 4, 4096], P('pop'), may hold values from -5 to 5
- gate_hidden_factors: bfloat16 [8, 4, 14336], P('pop', None, 'shard'), may hold values from -5 to 5
- up_hidden_factors: bfloat16 [8, 4, 14336], P('pop', None, 'shard'), may hold values from -5 to 5
- fitness: bfloat16 [8], P('pop'), may hold values from -1 to 1
- readout: float32 [14336], P('shard'), may hold values from -0.13363062 to 0.13363062
Outputs:
- scores: float32 [8, 480], P('pop')
- upd_gate: float32 [4096, 14336], P('pop', 'shard')
- up_update_direction: float32 [4096, 14336], P('pop', 'shard')
All inputs are finite; a program needn't handle non-finite values.
Results may differ from a plain program's by a relative error of at most 0.0003.
Values may be sent and summed in bfloat16 or wider, within the bound.
No kernel may reach another device: no remote copies, remote signals or barrier semaphores. Data moves between devices by JAX's collectives and lax.ppermute only.
A program may use at most 128 MiB of HBM per device.

v0:
```python
import math

import jax
import jax.numpy as jnp
from jax import lax
from jax.sharding import PartitionSpec as P


def direction(row_factor, col_factor, weighting):
    left_side = (row_factor.astype(jnp.float32) * weighting[:, None, None]).reshape(
        -1, row_factor.shape[2]
    )
    right_side = col_factor.astype(jnp.float32).reshape(-1, col_factor.shape[2])
    return lax.dot_general(
        left_side, right_side, (((0,), (0,)), ((), ())), precision=lax.Precision.HIGHEST
    )


def body(
    tokens,
    gate_weight_matrix,
    w_up,
    a_gate,
    a_up,
    gate_hidden_factors,
    up_hidden_factors,
    fitness,
    readout,
):
    members_dev, tok_count, model_width = tokens.shape
    row_count = members_dev * tok_count
    hidden_cols = gate_weight_matrix.shape[1]
    rank_count = a_gate.shape[1]
    noise_scale = 0.25 / math.sqrt(model_width * rank_count)
    flattened_rows = tokens.reshape(row_count, model_width)

    def add_rows(weight_rows):
        return jnp.dot(flattened_rows, weight_rows, preferred_element_type=jnp.float32)

    base_gate = add_rows(lax.all_gather(gate_weight_matrix, "pop", axis=0, tiled=True))
    base_up = add_rows(lax.all_gather(w_up, "pop", axis=0, tiled=True))
    gate_projected = jnp.einsum("mtd,mrd->mtr", tokens, a_gate, preferred_element_type=jnp.float32)
    up_projected = jnp.einsum("mtd,mrd->mtr", tokens, a_up, preferred_element_type=jnp.float32)
    noise_gate = jnp.einsum(
        "ygu,yup->ygp",
        gate_projected,
        gate_hidden_factors.astype(jnp.float32),
        precision=lax.Precision.HIGHEST,
    )
    noise_up = jnp.einsum(
        "ygu,yup->ygp",
        up_projected,
        up_hidden_factors.astype(jnp.float32),
        precision=lax.Precision.HIGHEST,
    )
    gate_pre = base_gate.reshape(members_dev, tok_count, hidden_cols) + noise_scale * noise_gate
    up_pre = base_up.reshape(members_dev, tok_count, hidden_cols) + noise_scale * noise_up
    hidden = jax.nn.silu(gate_pre) * up_pre
    partial_value = jnp.dot(
        hidden.reshape(row_count, hidden_cols), readout, precision=lax.Precision.HIGHEST
    ).reshape(members_dev, tok_count)
    scores = lax.psum(partial_value, "shard")
    col_gate, col_up, fitness_all = (
        lax.all_gather(gate_hidden_factors, "pop", axis=0, tiled=True),
        lax.all_gather(up_hidden_factors, "pop", axis=0, tiled=True),
        lax.all_gather(fitness, "pop", axis=0, tiled=True),
    )
    full_gate, full_up = (
        lax.all_gather(a_gate, "pop", axis=0, tiled=True),
        lax.all_gather(a_up, "pop", axis=0, tiled=True),
    )
    owned = model_width // lax.axis_size("pop")
    row_begin = lax.axis_index("pop") * owned
    row_gate = lax.dynamic_slice_in_dim(full_gate, row_begin, owned, 2)
    row_up = lax.dynamic_slice_in_dim(full_up, row_begin, owned, 2)
    total_members = fitness_all.shape[0]
    weighting = fitness_all.astype(jnp.float32) / math.sqrt(total_members * rank_count)
    upd_gate = direction(row_gate, col_gate, weighting)
    up_update_direction = direction(row_up, col_up, weighting)
    return (scores, upd_gate, up_update_direction)


def solution(mesh):
    placed = (
        P("pop", None, None),
        P("pop", "shard"),
        P("pop", "shard"),
        P("pop", None, None),
        P("pop", None, None),
        P("pop", None, "shard"),
        P("pop", None, "shard"),
        P("pop"),
        P("shard"),
    )
    return jax.shard_map(
        body,
        mesh=mesh,
        in_specs=placed,
        out_specs=(P("pop", None), P("pop", "shard"), P("pop", "shard")),
        check_vma=False,
    )
```

profile of v0, /device:TPU:0, one launch (start us, length us, event | category | flops | bytes accessed | tf_op | source)
XLA Modules:
  0.0 262.8 jit_solution(14272698410697424539)
XLA Ops:
  7.2 0.0 copy-start.7
  7.2 0.0 copy-start.6
  7.2 0.0 copy-start.5
  7.2 0.0 copy-start.4
  7.2 0.0 copy-start.3
  7.2 0.0 copy-start.2
  7.2 0.0 copy-start.1
  7.2 0.0 all-gather.3.cloned.1.call-start
  7.3 0.7 all-gather.3.cloned.1.call-update
  8.0 0.0 all-gather.5.cloned.1.call-start
  8.0 0.7 all-gather.5.cloned.1.call-update
  8.7 0.0 copy-done.7
  8.7 0.6 dynamic-slice
  10.0 0.0 copy-done.6
  10.0 0.2 dynamic-update-slice
  10.2 8.3 %all-reduce = bf16[8]{0:T(256)(128)(2,1)S(1)} all-reduce(bf16[8]{0:T(256)(128)(2,1)S(1)} %dynamic-update-slice), channel_id=1, replica_groups=mesh['pop'=4,'shard'=8] {'pop'}, use_global_device_ids=true, to_apply=%add | all-reduce | flops 8 | bytes 32
  18.6 0.0 copy-done.5
  18.6 0.0 copy-done.4
  18.6 5.4 %all_gather.25 = bf16[8,4,1792]{2,1,0:T(4,128)(2,1)S(1)} all-gather(bf16[2,4,1792]{2,1,0:T(4,128)(2,1)S(1)} %copy-done.4), channel_id=1, replica_groups=mesh['pop'=4,'shard'=8] {'pop'}, dimensions={0}, use_global_device_ids=true | all-gather | bytes 143360 | tf_op jit(solution)/shard_map/all_gather | solution.py:64
  24.0 0.0 copy-done.3
  24.0 6.0 %all_gather.27 = bf16[8,4,1792]{2,1,0:T(4,128)(2,1)S(1)} all-gather(bf16[2,4,1792]{2,1,0:T(4,128)(2,1)S(1)} %copy-done.3), channel_id=1, replica_groups=mesh['pop'=4,'shard'=8] {'pop'}, dimensions={0}, use_global_device_ids=true | all-gather | bytes 143360 | tf_op jit(solution)/shard_map/all_gather | solution.py:65
  30.0 0.0 copy-done.2
  30.0 7.6 %all_gather.23 = bf16[8,4,4096]{2,1,0:T(4,128)(2,1)S(1)} all-gather(bf16[2,4,4096]{2,1,0:T(4,128)(2,1)S(1)} %copy-done.2), channel_id=1, replica_groups=mesh['pop'=4,'shard'=8] {'pop'}, dimensions={0}, use_global_device_ids=true | all-gather | bytes 327680 | tf_op jit(solution)/shard_map/all_gather | solution.py:69
  37.6 0.0 copy-done.1
  37.6 7.6 %all_gather.26 = bf16[8,4,4096]{2,1,0:T(4,128)(2,1)S(1)} all-gather(bf16[2,4,4096]{2,1,0:T(4,128)(2,1)S(1)} %copy-done.1), channel_id=1, replica_groups=mesh['pop'=4,'shard'=8] {'pop'}, dimensions={0}, use_global_device_ids=true | all-gather | bytes 327680 | tf_op jit(solution)/shard_map/all_gather | solution.py:70
  45.3 0.0 slice-start
  45.4 5.3 %convolution_bitcast_fusion = f32[1024,1792]{1,0:T(8,128)} fusion(bf16[8,4,1792]{2,1,0:T(4,128)(2,1)S(1)} %all_gather.27, bf16[8,4,1024]{2,1,0:T(4,128)(2,1)S(1)} %constant_dynamic-slice_fusion, f32[8]{0:T(128)S(1)} %convert_multiply_fusion), kind=kOutput, calls=%fused_computation.15 | convolution fusion | flops 704708608 | bytes 7520288 | tf_op jit(solution)/shard_map/dot_general | solution.py:14
  50.6 0.0 slice-start.1
  50.6 5.3 %convolution_bitcast_fusion.1 = f32[1024,1792]{1,0:T(8,128)} fusion(bf16[8,4,1792]{2,1,0:T(4,128)(2,1)S(1)} %all_gather.25, bf16[8,4,1024]{2,1,0:T(4,128)(2,1)S(1)} %constant_dynamic-slice_fusion.1, f32[8]{0:T(128)S(1)} %convert_multiply_fusion), kind=kOutput, calls=%fused_computation.16 | convolution fusion | flops 704708608 | bytes 7520288 | tf_op jit(solution)/shard_map/dot_general | solution.py:14
  55.9 0.0 slice-done
  55.9 0.0 slice-done.1
  55.9 2.1 fusion.31
  58.0 5.0 %fusion.32 = f32[2,480,1792]{2,1,0:T(8,128)} fusion(f32[2,480,4]{1,2,0:T(4,128)S(1)} %fusion.31, bf16[2,4,1792]{2,1,0:T(4,128)(2,1)S(1)} %copy-done.3), kind=kOutput, calls=%fused_computation.38 | convolution fusion | flops 82575360 | bytes 6925312 | tf_op jit(solution)/shard_map/ygu,yup->ygp/dot_general | solution.py:50
  63.0 2.1 fusion.29
  65.1 4.9 %fusion.30 = f32[2,480,1792]{2,1,0:T(8,128)} fusion(f32[2,480,4]{1,2,0:T(4,128)S(1)} %fusion.29, bf16[2,4,1792]{2,1,0:T(4,128)(2,1)S(1)} %copy-done.4), kind=kOutput, calls=%fused_computation.36 | convolution fusion | flops 82575360 | bytes 6925312 | tf_op jit(solution)/shard_map/ygu,yup->ygp/dot_general | solution.py:44
  70.1 39.7 %all-gather.3.cloned.1.call-done = bf16[4096,1792]{1,0:T(8,128)(2,1)} async-done(((bf16[1024,1792]{1,0:T(8,128)(2,1)}), bf16[4096,1792]{1,0:T(8,128)(2,1)}) %all-gather.3.cloned.1.call-update) | async-done | bytes 14680080 | tf_op jit(solution)/shard_map/all_gather | solution.py:40
  109.8 20.5 %fusion.2 = f32[2,480,1792]{2,1,0:T(8,128)} fusion(bf16[2,480,4096]{2,1,0:T(8,128)(2,1)} %param.9, bf16[4096,1792]{1,0:T(8,128)(2,1)} %all-gather.3.cloned.1.call-done), kind=kOutput, calls=%fused_computation.2 | convolution fusion | flops 14092861440 | bytes 29425664 | tf_op jit(solution)/shard_map/dot_general | solution.py:38
  130.3 75.1 %all-gather.5.cloned.1.call-done = bf16[4096,1792]{1,0:T(8,128)(2,1)} async-done(((bf16[1024,1792]{1,0:T(8,128)(2,1)}), bf16[4096,1792]{1,0:T(8,128)(2,1)}) %all-gather.5.cloned.1.call-update) | async-done | bytes 14680080 | tf_op jit(solution)/shard_map/all_gather | solution.py:41
  205.4 0.0 copy-start
  205.4 0.0 copy-start.8
  205.4 18.1 %fusion = f32[2,480,1792]{2,1,0:T(8,128)S(1)} fusion(bf16[2,480,4096]{2,1,0:T(8,128)(2,1)} %param.9, bf16[4096,1792]{1,0:T(8,128)(2,1)} %all-gather.5.cloned.1.call-done), kind=kOutput, calls=%fused_computation | convolution fusion | flops 14092861440 | bytes 29425664 | tf_op jit(solution)/shard_map/dot_general | solution.py:38
  223.5 0.0 copy-done
  223.5 0.0 copy-done.8
  223.5 10.5 %fusion.4 = f32[1,2,480]{2,0,1:T(1,128)S(1)} fusion(f32[1792,1,1]{0,1,2:T(1,128)S(1)} %reshape.29, f32[2,480,1792]{2,1,0:T(8,128)S(1)} %fusion, f32[2,480,1792]{2,1,0:T(8,128)} %fusion.32, f32[2,480,1792]{2,1,0:T(8,128)S(1)} %copy-done.8, f32[2,480,1792]{2,1,0:T(8,128)S(1)} %copy-done), kind=kOutput, calls=%fused_computation.4 | convolution fusion | flops 36126720 | bytes 27536128 | tf_op jit(solution)/shard_map/dot_general | solution.py:59
  234.0 21.9 %psum.7 = f32[2,480]{1,0:T(2,128)} all-reduce(f32[2,480]{1,0:T(2,128)S(1)} %bitcast.27), channel_id=1, replica_groups=mesh['pop'=4,'shard'=8] {'shard'}, use_global_device_ids=true, to_apply=%region_0.1 | all-reduce | flops 960 | bytes 7680 | tf_op jit(solution)/shard_map/psum | solution.py:62
  (7 shorter events, 0.1 us)
Async XLA Ops:
  7.2 1.6 copy-start.7
  7.2 2.8 %copy-start.6 = (bf16[2]{0:T(256)(128)(2,1)S(1)}, bf16[2]{0:T(256)(128)(2,1)}, u32[]{:S(2)}) copy-start(bf16[2]{0:T(256)(128)(2,1)} %param.16) | copy-start | bytes 16
  7.2 11.4 %copy-start.5 = (f32[1792]{0:T(1024)S(1)}, f32[1792]{0:T(1024)}, u32[]{:S(2)}) copy-start(f32[1792]{0:T(1024)} %param.17) | copy-start | bytes 21508
  7.2 11.4 %copy-start.4 = (bf16[2,4,1792]{2,1,0:T(4,128)(2,1)S(1)}, bf16[2,4,1792]{2,1,0:T(4,128)(2,1)}, u32[]{:S(2)}) copy-start(bf16[2,4,1792]{2,1,0:T(4,128)(2,1)} %param.14) | copy-start | bytes 86020
  7.2 16.8 %copy-start.3 = (bf16[2,4,1792]{2,1,0:T(4,128)(2,1)S(1)}, bf16[2,4,1792]{2,1,0:T(4,128)(2,1)}, u32[]{:S(2)}) copy-start(bf16[2,4,1792]{2,1,0:T(4,128)(2,1)} %param.15) | copy-start | bytes 86020
  7.2 22.8 %copy-start.2 = (bf16[2,4,4096]{2,1,0:T(4,128)(2,1)S(1)}, bf16[2,4,4096]{2,1,0:T(4,128)(2,1)}, u32[]{:S(2)}) copy-start(bf16[2,4,4096]{2,1,0:T(4,128)(2,1)} %param.12) | copy-start | bytes 196612
  7.2 30.4 %copy-start.1 = (bf16[2,4,4096]{2,1,0:T(4,128)(2,1)S(1)}, bf16[2,4,4096]{2,1,0:T(4,128)(2,1)}, u32[]{:S(2)}) copy-start(bf16[2,4,4096]{2,1,0:T(4,128)(2,1)} %param.13) | copy-start | bytes 196612
  7.2 102.6 %all-gather.3.cloned.1.call-start = ((), (), s32[]{:S(2)}) async-start(), calls=%async_computation | async-start | bytes 18350080 | tf_op jit(solution)/shard_map/all_gather | solution.py:40
  8.0 197.4 %all-gather.5.cloned.1.call-start = ((), (), s32[]{:S(2)}) async-start(), calls=%async_computation.1 | async-start | bytes 18350080 | tf_op jit(solution)/shard_map/all_gather | solution.py:41
  45.3 10.6 %slice-start = ((s8[7864320]{0:T(1024)(128)(4,1)}), s8[4194304]{0:T(1024)(128)(4,1)S(1)}, s32[]{:S(2)}) async-start(s8[7864320]{0:T(1024)(128)(4,1)} %bitcast.25), calls=%async_computation.2 | async-start | bytes 8388608
  50.6 5.3 %slice-start.1 = ((s8[7864320]{0:T(1024)(128)(4,1)}), s8[3670016]{0:T(1024)(128)(4,1)S(1)}, s32[]{:S(2)}) async-start(s8[7864320]{0:T(1024)(128)(4,1)} %bitcast.25), calls=%async_computation.3 | async-start | bytes 7340032
  205.4 18.1 %copy-start = (f32[2,480,1792]{2,1,0:T(8,128)S(1)}, f32[2,480,1792]{2,1,0:T(8,128)}, u32[]{:S(2)}) copy-start(f32[2,480,1792]{2,1,0:T(8,128)} %fusion.30) | copy-start | bytes 20643844
  205.4 18.1 %copy-start.8 = (f32[2,480,1792]{2,1,0:T(8,128)S(1)}, f32[2,480,1792]{2,1,0:T(8,128)}, u32[]{:S(2)}) copy-start(f32[2,480,1792]{2,1,0:T(8,128)} %fusion.2) | copy-start | bytes 20643844
Sparse Core Ops, SparseCore 0:
  9.6 100.1 all-gather.2
  111.4 94.0 all-gather.4
where the time goes:
time: 263 us
  waiting for transfers between devices  116 us (44%)
  matrix products  73.8 us (28%)
  blocking collectives  56.9 us (22%)
  between operations  14.9 us (6%)
    all_gather x1, waiting for transfers between devices, body(): base_up = add_rows(lax.all_gather(w_up, 'pop', axis=0, tiled=True))  75.1 us
    all_gather x1, waiting for transfers between devices, body(): lax.all_gather(gate_weight_matrix, 'pop', axis=0, tiled=True)  39.7 us
    dot_general x2, matrix products, add_rows(): jnp.dot(flattened_rows, weight_rows, preferred_element_type=jnp.float32)  38.6 us
    psum x1, blocking collectives, body(): scores = lax.psum(partial_value, 'shard')  21.9 us
    dot_general x2, matrix products, direction(): lax.dot_general(left_side, right_side, (((0,), (0,)), ((), ())), precisio...  10.5 us
    dot_general x1, matrix products, body(): jnp.dot(hidden.reshape(row_count, hidden_cols), readout, precision=lax.Pr...  10.5 us
    unnamed x1, blocking collectives  8.31 us
    all_gather x1, blocking collectives, body(): lax.all_gather(a_gate, 'pop', axis=0, tiled=True)  7.63 us
  transfers between devices with their start and end apart: 2, of which 2 were waited for; matrix products, arithmetic and copies ran while one was open for 18% of the time, Pallas kernels for 0%

commit v1 on v0

v1 whole, which is shorter than its diff:
```python
import functools
import math

import jax
import jax.numpy as jnp
from jax import lax
from jax.experimental import pallas as pl
from jax.experimental.pallas import tpu as pltpu
from jax.sharding import PartitionSpec as P

F32 = jnp.float32
BF16 = jnp.bfloat16


def split3(value):
    top = lax.reduce_precision(value, 8, 7)
    rest = value - top
    middle = lax.reduce_precision(rest, 8, 7)
    return [term.astype(BF16) for term in (top, middle, rest - middle)]


def column_chunks(width):
    cuts, begin = [], 0
    while begin < width:
        size = min(256, width - begin)
        cuts.append((begin, size))
        begin += size
    return cuts


def line_sizes(total):
    outer = 4 if total % 4 == 0 else 1
    return outer, total // outer


def swap_pairs(total, partner):
    return [(index, partner(index)) for index in range(total)]


def line_gather(own, size, coord, permute):
    if size == 1:
        return [(own, coord)]
    if size == 2:
        return [(own, coord), (permute(own, lambda c: c ^ 1), coord ^ 1)]
    if size == 4:
        even = lambda c: c ^ 1
        odd = lambda c: 3 - c if c in (1, 2) else c
        edge = jnp.logical_or(coord == 0, coord == 3)
        first = permute(own, even)
        across = permute(own, odd)
        second = jnp.where(edge, permute(across, even), across)
        across = permute(first, odd)
        third = jnp.where(edge, permute(across, even), across)
        place = [
            jnp.where(coord == 0, a, jnp.where(coord == 1, b, jnp.where(coord == 2, c, d)))
            for a, b, c, d in ((1, 0, 3, 2), (2, 2, 1, 1), (3, 3, 0, 0))
        ]
        return [(own, coord)] + list(zip((first, second, third), place))
    return [
        (own if step == 0 else permute(own, lambda c, step=step: (c + step) % size), (coord + size - step) % size)
        for step in range(size)
    ]


def gated_scores(ids, chunks, groups, pairs, readout, rows_per_block):
    arrays, specs = [ids, readout], [pl.BlockSpec(memory_space=pltpu.SMEM), pl.BlockSpec(memory_space=pltpu.VMEM)]

    def add(array, space):
        for index, seen in enumerate(arrays):
            if seen is array:
                return index
        arrays.append(array)
        specs.append(pl.BlockSpec(memory_space=space))
        return len(arrays) - 1

    used_chunks = sorted({pair[1] for pair in pairs})
    used_groups = sorted({pair[0] for pair in pairs})
    model_width = rows_per_block * sum(1 for _ in chunks[0][2])
    chunk_refs = {
        j: [(add(array, pl.ANY), lane, place) for array, lane, place in chunks[j][2]] for j in used_chunks
    }
    group_refs, shapes, scratch = {}, [], []
    for g in used_groups:
        sources, tile, noise_rows, noise_cols = groups[g]
        group_refs[g] = (
            [(add(array, pl.ANY), place) for array, place in sources],
            tile,
            add(noise_rows, pltpu.VMEM),
            add(noise_cols, pltpu.VMEM),
        )
        shapes.append(jax.ShapeDtypeStruct((noise_rows.shape[0], tile), F32))
    copies = 0
    for g in used_groups:
        rows = groups[g][0][0][0].shape[0]
        scratch.append(pltpu.VMEM((rows, model_width), BF16))
        copies += len(groups[g][0])
    for j in used_chunks:
        scratch.append(pltpu.VMEM((model_width, 2 * chunks[j][1]), BF16))
        copies += len(chunks[j][2])
    scratch.append(pltpu.SemaphoreType.DMA((copies,)))
    inputs, outputs = len(arrays), len(shapes)

    def kernel(*refs):
        ids_ref, readout_ref = refs[0], refs[1]
        outs = dict(zip(used_groups, refs[inputs : inputs + outputs]))
        held = refs[inputs + outputs :]
        tokens = dict(zip(used_groups, held[: len(used_groups)]))
        weights = dict(zip(used_chunks, held[len(used_groups) : -1]))
        sems = held[-1]
        pending, count = {}, 0

        def fetch(key):
            nonlocal count
            if key in pending:
                return
            started = []
            if key[0] == "w":
                width = 2 * chunks[key[1]][1]
                for index, lane, place in chunk_refs[key[1]]:
                    first = pl.multiple_of(ids_ref[place] * rows_per_block, rows_per_block)
                    started.append(
                        pltpu.make_async_copy(
                            refs[index].at[:, pl.ds(lane, width)],
                            weights[key[1]].at[pl.ds(first, rows_per_block), :],
                            sems.at[count],
                        )
                    )
                    count += 1
            else:
                for index, place in group_refs[key[1]][0]:
                    source, target = refs[index], tokens[key[1]]
                    if place is not None:
                        lanes = source.shape[1]
                        target = target.at[:, pl.ds(pl.multiple_of(ids_ref[place] * lanes, lanes), lanes)]
                    started.append(pltpu.make_async_copy(source, target, sems.at[count]))
                    count += 1
            for copy in started:
                copy.start()
            pending[key] = started

        for g, j in pairs:
            fetch(("w", j))
            fetch(("t", g))
        fresh = set()
        for g, j in pairs:
            for key in (("w", j), ("t", g)):
                for copy in pending[key]:
                    copy.wait()
                pending[key] = []
            begin, size, _ = chunks[j]
            _, tile, noise_rows, noise_cols = group_refs[g]
            first = g not in fresh
            fresh.add(g)

            def step(t, carry, g=g, j=j, begin=begin, size=size, tile=tile, noise_rows=noise_rows, noise_cols=noise_cols, first=first):
                rows = pl.ds(pl.multiple_of(t * tile, 16), tile)
                total = jnp.dot(tokens[g][rows, :], weights[j][...], preferred_element_type=F32)
                total += lax.dot_general(
                    refs[noise_rows][t],
                    refs[noise_cols][:, 2 * begin : 2 * begin + 2 * size],
                    (((0,), (0,)), ((), ())),
                    preferred_element_type=F32,
                )
                gate, up = total[:, :size], total[:, size:]
                value = gate / (1.0 + jnp.exp(-gate)) * up * readout_ref[:, begin : begin + size]
                if size == 256:
                    value = value[:, :128] + value[:, 128:]
                line = jnp.sum(value.T, axis=0, keepdims=True)
                at = pl.ds(t, 1)
                outs[g][at, :] = line if first else outs[g][at, :] + line
                return carry

            lax.fori_loop(0, groups[g][2].shape[0], step, 0)

    flops = sum(4 * groups[g][0][0][0].shape[0] * model_width * chunks[j][1] for g, j in pairs)
    return dict(
        zip(
            used_groups,
            pl.pallas_call(
                kernel,
                out_shape=shapes,
                in_specs=specs,
                out_specs=[pl.BlockSpec(memory_space=pltpu.VMEM)] * len(shapes),
                scratch_shapes=scratch,
                compiler_params=pltpu.CompilerParams(vmem_limit_bytes=48 * 1024 * 1024),
                cost_estimate=pl.CostEstimate(flops=flops, bytes_accessed=8 * 1024 * 1024, transcendentals=0),
            )(*arrays),
        )
    )


def row_chunks(rows):
    last = rows // 5
    return [(0, rows - last, (rows - last) // 2), (rows - last, last, last)]


def body(
    pop_size,
    shard_size,
    tokens,
    gate_weight_matrix,
    w_up,
    a_gate,
    a_up,
    gate_hidden_factors,
    up_hidden_factors,
    fitness,
    readout,
):
    members, tok_count, model_width = tokens.shape
    rank = a_gate.shape[1]
    rows = members * tok_count
    block_rows, hidden = gate_weight_matrix.shape
    half = hidden // 2
    lo_size = pop_size // 2
    outer, inner = line_sizes(shard_size)
    noise_scale = 0.25 / math.sqrt(model_width * rank)
    pop, shard = lax.axis_index("pop"), lax.axis_index("shard")
    hi, lo = pop // lo_size, pop % lo_size
    flat = tokens.reshape(rows, model_width)
    chunks = column_chunks(half)

    across_pairs = [(p, (p + lo_size) % pop_size) for p in range(pop_size)]

    def across(value):
        return lax.ppermute(value, "pop", across_pairs)

    def along(value, step):
        pairs = [(p, p // lo_size * lo_size + (p + step) % lo_size) for p in range(pop_size)]
        return lax.ppermute(value, "pop", pairs)

    def outer_permute(value, target):
        return lax.ppermute(
            value, "shard", [(s, target(s // inner) * inner + s % inner) for s in range(shard_size)]
        )

    def inner_permute(value, target):
        return lax.ppermute(
            value, "shard", [(s, s // inner * inner + target(s % inner)) for s in range(shard_size)]
        )

    piece_width = model_width // shard_size
    cuts = row_chunks(rows)
    sent = [
        across(lax.dynamic_slice(flat, (begin, shard * piece_width), (size, piece_width))) for begin, size, _ in cuts
    ]

    def pick(which):
        start = which * half
        gate = lax.dynamic_slice_in_dim(gate_weight_matrix, start, half, 1)
        up = lax.dynamic_slice_in_dim(w_up, start, half, 1)
        return [
            jnp.concatenate([gate[:, begin : begin + size], up[:, begin : begin + size]], 1) for begin, size in chunks
        ]

    passed = [across(block) for block in pick(1 - hi)]
    kept = jnp.concatenate(pick(hi), 1)
    near = [along(kept, step) for step in range(1, lo_size)]
    far = [[block] + [along(block, step) for step in range(1, lo_size)] for block in passed]

    gathered = []
    for index, block in enumerate(sent):
        pieces = []
        if index == 0:
            for piece, z in line_gather(block, outer, shard // inner, outer_permute):
                for part, y in line_gather(piece, inner, shard % inner, inner_permute):
                    pieces.append((part, z * inner + y))
        else:
            for piece, y in line_gather(block, inner, shard % inner, inner_permute):
                for part, z in line_gather(piece, outer, shard // inner, outer_permute):
                    pieces.append((part, z * inner + y))
        gathered.append(pieces)

    places = [hi * lo_size + (lo + lo_size - step) % lo_size for step in range(lo_size)]
    places += [(1 - hi) * lo_size + (lo + lo_size - step) % lo_size for step in range(lo_size)]
    for pieces in gathered:
        places += [place for _, place in pieces]
    ids = jnp.stack([jnp.asarray(place, jnp.int32) for place in places])

    chunk_list = []
    for index, (begin, size) in enumerate(chunks):
        sources = [(kept, 2 * begin, 0)] + [(block, 2 * begin, 1 + n) for n, block in enumerate(near)]
        sources += [(block, 0, lo_size + n) for n, block in enumerate(far[index])]
        chunk_list.append((begin, size, sources))

    factors = jnp.concatenate([a_gate, a_up], 1)
    columns = jnp.concatenate([gate_hidden_factors, up_hidden_factors], 1)
    lines = 2 * members * rank
    projected = noise_scale * jnp.einsum("mrd,mtd->mrt", factors, tokens, preferred_element_type=F32)
    other_projected = across(projected)
    block_half = model_width // 2
    bundle = jnp.concatenate(
        [
            columns.reshape(lines, hidden),
            lax.dynamic_slice_in_dim(factors.reshape(lines, model_width), (1 - hi) * block_half, block_half, 1),
            jnp.broadcast_to(fitness[:, None], (members, 2 * rank * 128)).reshape(lines, 128),
        ],
        1,
    )
    other_bundle = across(bundle)
    other_columns = other_bundle[:, :hidden].reshape(members, 2 * rank, hidden)

    def noise_lines(value):
        same = jnp.eye(members, dtype=BF16)[None, :, None, :, None]
        terms = jnp.stack(split3(value))[:, :, :, None, :]
        return (terms * same).reshape(3 * lines, rows)

    def noise_columns(value):
        value = lax.dynamic_slice_in_dim(value, hi * half, half, 2)
        zero = jnp.zeros((members, rank, half), BF16)
        gate = jnp.concatenate([value[:, :rank], zero], 1).reshape(lines, half)
        up = jnp.concatenate([zero, value[:, rank:]], 1).reshape(lines, half)
        blocks = []
        for begin, size in chunks:
            blocks += [gate[:, begin : begin + size], up[:, begin : begin + size]]
        return jnp.tile(jnp.concatenate(blocks, 1), (3, 1))

    def tiled(value, tile):
        return value.reshape(value.shape[0], value.shape[1] // tile, tile).transpose(1, 0, 2)

    own_lines, other_lines = noise_lines(projected), noise_lines(other_projected)
    own_columns, far_columns = noise_columns(columns), noise_columns(other_columns)
    groups = [([(flat, None)], tok_count, tiled(own_lines, tok_count), own_columns)]
    at = 2 * lo_size
    for pieces, (begin, size, tile) in zip(gathered, cuts):
        sources = [(piece, at + n) for n, (piece, _) in enumerate(pieces)]
        at += len(pieces)
        groups.append((sources, tile, tiled(other_lines[:, begin : begin + size], tile), far_columns))
    half_readout = lax.dynamic_slice_in_dim(readout, hi * half, half, 0)[None, :]

    last = len(chunks) - 1
    plan = [[(0, j)] for j in range(last - 1)]
    plan.append([(0, last - 1)] + [(1, j) for j in range(last)])
    plan.append([(0, last), (1, last)] + [(2, j) for j in range(last + 1)])
    results = [
        gated_scores(ids, chunk_list, groups, pairs, half_readout, block_rows) for pairs in plan if pairs
    ]
    totals = [
        sum(result[g] for result in results if g in result).reshape(-1) for g in range(len(groups))
    ]
    own_total, other_total = totals[0], jnp.concatenate(totals[1:])

    scores = own_total + across(other_total)
    scores = scores + sum(inner_permute(scores, lambda c, s=s: (c + s) % inner) for s in range(1, inner))
    scores = scores + sum(outer_permute(scores, lambda c, s=s: (c + s) % outer) for s in range(1, outer))

    both = jnp.stack([bundle, other_bundle])
    heads = jnp.stack([both[:, :, :hidden], both[:, :, :hidden]])[0]
    marks = both[:, :, hidden + block_half :]
    factor_parts = jnp.stack(
        [
            lax.dynamic_slice_in_dim(factors.reshape(lines, model_width), hi * block_half, block_half, 1),
            other_bundle[:, hidden : hidden + block_half],
        ]
    )

    def packed(target):
        return jnp.concatenate(
            [heads, lax.dynamic_slice_in_dim(factor_parts, target * block_rows, block_rows, 2), marks], 2
        )

    every = [packed(lo)]
    for step in range(1, lo_size):
        every.append(along(packed((lo + step) % lo_size), step))
    every = jnp.stack(every).reshape(pop_size, members, 2, rank, hidden + block_rows + 128)
    weighting = every[..., -1:].astype(F32) / math.sqrt(pop_size * members * rank)

    def direction(kind):
        part = every[:, :, kind].reshape(pop_size * members * rank, -1)
        weight = weighting[:, :, kind].reshape(-1, 1)
        left = jnp.concatenate(split3(part[:, hidden : hidden + block_rows].astype(F32) * weight))
        right = jnp.tile(part[:, :hidden], (3, 1))
        return lax.dot_general(left, right, (((0,), (0,)), ((), ())), preferred_element_type=F32)

    return scores.reshape(members, tok_count), direction(0), direction(1)


def solution(mesh):
    placed = (
        P("pop", None, None),
        P("pop", "shard"),
        P("pop", "shard"),
        P("pop", None, None),
        P("pop", None, None),
        P("pop", None, "shard"),
        P("pop", None, "shard"),
        P("pop"),
        P("shard"),
    )
    return jax.shard_map(
        functools.partial(body, mesh.shape["pop"], mesh.shape["shard"]),
        mesh=mesh,
        in_specs=placed,
        out_specs=(P("pop", None), P("pop", "shard"), P("pop", "shard")),
        check_vma=False,
    )
```

time: 263 us -> 285 us (1.084)
  starting transfers between devices: 0.08 us -> 74.5 us
  matrix products: 73.8 us -> 14.4 us
  blocking collectives: 56.9 us -> 0 us
  Pallas kernels: 0 us -> 56.1 us
  local copies, waits for them, and re-layouts: 0.96 us -> 28.1 us
  waiting for transfers between devices: 116 us -> 91.9 us
  other arithmetic: 0.01 us -> 17.3 us
  between operations: 14.9 us -> 1.48 us
    all_gather x2 -> x0, waiting for transfers between devices: 115 us -> none  [the longest x1 75.1 us: body(): base_up = add_rows(lax.all_gather(w_up, 'pop', axis=0, tiled=True))]
    ppermute x0 -> x39, waiting for transfers between devices: none -> 91.9 us  [the longest x6 48.1 us: inner_permute(): lax.ppermute(value, 'shard', [(s, s // inner * inner + target(s % inner))...]
    ppermute x0 -> x39, starting transfers between devices: none -> 74.5 us  [the longest x18 54.4 us: outer_permute(): lax.ppermute(value, 'shard', [(s, target(s // inner) * inner + s % inner)...]
    dot_general x9 -> x3, matrix products: 73.8 us -> 14.4 us  [the longest x2 8.4 us: direction(): lax.dot_general(left, right, (((0,), (0,)), ((), ())), preferred_element_...]
    pallas_call x0 -> x4, Pallas kernels: none -> 56.1 us  [gated_scores(): pl.pallas_call(kernel, out_shape=shapes, in_specs=specs, out_specs=[pl.Bl...]
    all_gather x4 -> x0, blocking collectives: 26.7 us -> none  [the longest x1 7.63 us: body(): lax.all_gather(a_gate, 'pop', axis=0, tiled=True)]
    psum x1 -> x0, blocking collectives: 21.9 us -> none  [body(): scores = lax.psum(partial_value, 'shard')]
    unnamed x1 -> x0, blocking collectives: 8.31 us -> none
  transfers between devices with their start and end apart: 2 -> 39, of which waited for: 2 -> 12; matrix products, arithmetic and copies ran while one was open for 18% -> 16% of each run, Pallas kernels for 0% -> 15%
where the time goes in v1:
time: 285 us; the launch traced here: 284 us
  waiting for transfers between devices  91.9 us (32%)
  starting transfers between devices  74.5 us (26%)
  Pallas kernels  56.1 us (20%)
  local copies, waits for them, and re-layouts  28.1 us (10%)
  other arithmetic  17.3 us (6%)
  matrix products  14.4 us (5%)
    pallas_call x4, Pallas kernels, gated_scores(): pl.pallas_call(kernel, out_shape=shapes, in_specs=specs, out_specs=[pl.Bl...  56.1 us
    ppermute x18, starting transfers between devices, outer_permute(): lax.ppermute(value, 'shard', [(s, target(s // inner) * inner + s % inner)...  54.4 us
    ppermute x6, waiting for transfers between devices, inner_permute(): lax.ppermute(value, 'shard', [(s, s // inner * inner + target(s % inner))...  48.1 us
    ppermute x9, waiting for transfers between devices, across(): return lax.ppermute(value, 'pop', across_pairs)  33.2 us
    ppermute x9, starting transfers between devices, across(): return lax.ppermute(value, 'pop', across_pairs)  12.2 us
    ppermute x18, waiting for transfers between devices, outer_permute(): lax.ppermute(value, 'shard', [(s, target(s // inner) * inner + s % inner)...  10.6 us
    dot_general x2, matrix products, direction(): lax.dot_general(left, right, (((0,), (0,)), ((), ())), preferred_element_...  8.4 us
    unnamed x91, local copies, waits for them, and re-layouts  7.98 us
  transfers between devices with their start and end apart: 39, of which 12 were waited for; matrix products, arithmetic and copies ran while one was open for 16% of the time, Pallas kernels for 15%

profile of v1, /device:TPU:0, one launch (start us, length us, event | category | flops | bytes accessed | tf_op | source)
XLA Modules:
  0.0 283.7 jit_solution(3308948291923848286)
XLA Ops:
  0.7 2.0 dynamic-slice_dynamic-update-slice_fusion.5
  2.7 2.0 dynamic-slice_dynamic-update-slice_fusion.4
  4.7 1.9 dynamic-slice_dynamic-update-slice_fusion.3
  6.6 1.9 dynamic-slice_dynamic-update-slice_fusion.2
  13.2 2.9 %collective-permute-start.19 = (bf16[1024,256]{1,0:T(8,128)(2,1)}, bf16[1024,256]{1,0:T(8,128)(2,1)S(1)}, u32[]{:S(2)}, u32[]{:S(2)}) collective-permute-start(bf16[1024,256]{1,0:T(8,128)(2,1)} %pad_maximum_fusion.3), channel_id=1, source_target_pairs={{0,16},{8,24},{16,0},{24,8},{1,17},{9,25},{17,1},{25,9},{2,18},{10... | collective-permute-start | bytes 1572872 | tf_op jit(solution)/shard_map/ppermute | solution.py:226
  17.8 2.1 constant_dynamic-slice_fusion.7
  19.9 2.0 collective-permute-start.7
  21.9 6.0 %convolution_multiply_fusion = f32[2,8,480]{2,1,0:T(8,128)} fusion(bf16[2,480,4096]{2,1,0:T(8,128)(2,1)} %param.9, bf16[2,4,4096]{2,1,0:T(4,128)(2,1)S(1)} %copy-done.21, bf16[2,4,4096]{2,1,0:T(4,128)(2,1)S(1)} %copy-done.22), kind=kOutput, calls=%fused_computation | convolution fusion | flops 63184384 | bytes 8026112 | tf_op jit(solution)/shard_map/mrd,mtd->mrt/dot_general | solution.py:289
  27.9 1.6 constant_dynamic-slice_fusion.11
  29.5 2.0 collective-permute-start.21
  32.5 2.3 pad_maximum_fusion
  34.8 2.1 pad_maximum_fusion.1
  38.3 11.1 %collective-permute-done.17 = f32[2,8,480]{2,1,0:T(8,128)} collective-permute-done((f32[2,8,480]{2,1,0:T(8,128)}, f32[2,8,480]{2,1,0:T(8,128)}, u32[]{:S(2)}, u32[]{:S(2)}) %collective-permute-start.17) | collective-permute-done | bytes 30752 | tf_op jit(solution)/shard_map/ppermute | solution.py:226
  53.2 2.2 collective-permute-start.22
  56.2 1.6 collective-permute-start.27
  57.7 3.3 %collective-permute-done.22.refs_26_ = bf16[192,512]{1,0:T(8,128)(2,1)S(1)} collective-permute-done((bf16[192,512]{1,0:T(8,128)(2,1)S(1)}, bf16[192,512]{1,0:T(8,128)(2,1)S(1)}, u32[]{:S(2)}, u32[]{:S(2)}) %collective-permute-start.22) | collective-permute-done | bytes 196640 | tf_op jit(solution)/shard_map/ppermute | solution.py:233
  61.0 4.7 %collective-permute-start.24 = (bf16[192,512]{1,0:T(8,128)(2,1)S(1)}, bf16[192,512]{1,0:T(8,128)(2,1)S(1)}, u32[]{:S(2)}, u32[]{:S(2)}) collective-permute-start(bf16[192,512]{1,0:T(8,128)(2,1)S(1)} %collective-permute-done.23), channel_id=1, source_target_pairs={{0,2},{1,3},{2,0},{3,1},{4,6},{5,7},{6,4},{7,5},{8,10},{9,11},{10,... | collective-permute-start | bytes 589832 | tf_op jit(solution)/shard_map/ppermute | solution.py:233
  66.5 3.1 %collective-permute-start.28 = (bf16[192,512]{1,0:T(8,128)(2,1)S(1)}, bf16[192,512]{1,0:T(8,128)(2,1)S(1)}, u32[]{:S(2)}, u32[]{:S(2)}) collective-permute-start(bf16[192,512]{1,0:T(8,128)(2,1)S(1)} %collective-permute-done.27.refs_29_), channel_id=1, source_target_pairs={{0,2},{1,3},{2,0},{3,1},{4,6},{5,7},{6,4},{7,5},{8,10},{9,11},{10,... | collective-permute-start | bytes 589832 | tf_op jit(solution)/shard_map/ppermute | solution.py:233
  69.6 1.8 collective-permute-done.24
  72.1 4.5 %collective-permute-start.26 = (bf16[192,512]{1,0:T(8,128)(2,1)S(1)}, bf16[192,512]{1,0:T(8,128)(2,1)S(1)}, u32[]{:S(2)}, u32[]{:S(2)}) collective-permute-start(bf16[192,512]{1,0:T(8,128)(2,1)S(1)} %collective-permute-done.25), channel_id=1, source_target_pairs={{0,2},{1,3},{2,0},{3,1},{4,6},{5,7},{6,4},{7,5},{8,10},{9,11},{10,... | collective-permute-start | bytes 589832 | tf_op jit(solution)/shard_map/ppermute | solution.py:233
  76.6 4.1 %collective-permute-start.30 = (bf16[192,512]{1,0:T(8,128)(2,1)S(1)}, bf16[192,512]{1,0:T(8,128)(2,1)}, u32[]{:S(2)}, u32[]{:S(2)}) collective-permute-start(bf16[192,512]{1,0:T(8,128)(2,1)S(1)} %collective-permute-done.29), channel_id=1, source_target_pairs={{0,2},{1,3},{2,0},{3,1},{4,6},{5,7},{6,4},{7,5},{8,10},{9,11},{10,... | collective-permute-start | bytes 589832 | tf_op jit(solution)/shard_map/ppermute | solution.py:233
  82.0 2.1 collective-permute-start.9
  88.8 1.9 fusion.38
  90.7 13.1 %collective-permute-start.12 = (bf16[768,512]{1,0:T(8,128)(2,1)}, bf16[768,512]{1,0:T(8,128)(2,1)}, u32[]{:S(2)}, u32[]{:S(2)}) collective-permute-start(bf16[768,512]{1,0:T(8,128)(2,1)} %collective-permute-done.11), channel_id=1, source_target_pairs={{0,2},{1,3},{2,0},{3,1},{4,6},{5,7},{6,4},{7,5},{8,10},{9,11},{10,... | collective-permute-start | bytes 2359304 | tf_op jit(solution)/shard_map/ppermute | solution.py:233
  103.9 7.4 %collective-permute-start.14 = (bf16[768,512]{1,0:T(8,128)(2,1)}, bf16[768,512]{1,0:T(8,128)(2,1)}, u32[]{:S(2)}, u32[]{:S(2)}) collective-permute-start(bf16[768,512]{1,0:T(8,128)(2,1)} %collective-permute-done.9.refs_15_.refs_17_), channel_id=1, source_target_pairs={{0,0},{1,1},{2,4},{3,5},{4,2},{5,3},{6,6},{7,7},{8,8},{9,9},{10,12... | collective-permute-start | bytes 2359304 | tf_op jit(solution)/shard_map/ppermute | solution.py:233
  112.7 1.6 reshape_squeeze.8
  114.3 1.6 slice.225
  120.2 4.2 %fusion.4 = f32[1024,1792]{1,0:T(8,128)} fusion(bf16[96,1792]{1,0:T(8,128)(2,1)S(1)} %bitcast.87, bf16[32,1024]{1,0:T(8,128)(2,1)S(1)} %get-tuple-element.38, bf16[32,1024]{1,0:T(8,128)(2,1)S(1)} %get-tuple-element.37, bf16[32,1024]{1,0:T(8,128)(2,1)S(1)} %get-tuple-element.36), kind=kOutput, calls=%fused_computation.22 | convolution fusion | flops 352911360 | bytes 7880704 | tf_op jit(solution)/shard_map/dot_general | solution.py:373
  124.4 1.6 reshape_squeeze.9
  126.2 9.3 %collective-permute-done.3.refs_4_.refs_6_ = bf16[1024,512]{1,0:T(8,128)(2,1)S(1)} collective-permute-done((bf16[1024,512]{1,0:T(8,128)(2,1)}, bf16[1024,512]{1,0:T(8,128)(2,1)S(1)}, u32[]{:S(2)}, u32[]{:S(2)}) %collective-permute-start.3) | collective-permute-done | bytes 1048608 | tf_op jit(solution)/shard_map/ppermute | solution.py:226
  136.0 2.0 collective-permute-start.15
  142.1 10.7 %collective-permute-done.5.refs_8_ = bf16[1024,512]{1,0:T(8,128)(2,1)} collective-permute-done((bf16[1024,512]{1,0:T(8,128)(2,1)}, bf16[1024,512]{1,0:T(8,128)(2,1)}, u32[]{:S(2)}, u32[]{:S(2)}) %collective-permute-start.5) | collective-permute-done | bytes 1048608 | tf_op jit(solution)/shard_map/ppermute | solution.py:226
  152.8 1.8 collective-permute-start.32
  154.6 1.9 collective-permute-done.15
  156.7 3.5 %collective-permute-done.32 = bf16[192,512]{1,0:T(8,128)(2,1)S(1)} collective-permute-done((bf16[192,512]{1,0:T(8,128)(2,1)}, bf16[192,512]{1,0:T(8,128)(2,1)S(1)}, u32[]{:S(2)}, u32[]{:S(2)}) %collective-permute-start.32) | collective-permute-done | bytes 196640 | tf_op jit(solution)/shard_map/ppermute | solution.py:233
  164.3 9.6 %shard_map.112 = f32[2,480]{1,0:T(2,128)S(1)} custom-call(s32[20]{0:T(128)S(1)} %stack.110.refs_0_, f32[1,896]{1,0:T(1,128)S(1)} %broadcast_in_dim.8.refs_1_, bf16[1024,1792]{1,0:T(8,128)(2,1)} %get-tuple-element.20.refs_2_, bf16[1024,1792]{1,0:T(8,128)(2,1)} %collective-permute-done.refs_3_, bf16[1024,512]{1,0:T(8,128)(2,1)S(1)} %collective-permute-done.1.refs_4_, ...), custom_call_target="tpu_custom_call" | custom-call | flops 4026531840 | bytes 8388608 | tf_op jit(solution)/shard_map/pallas_call | solution.py:179
  173.9 9.5 %shard_map.113 = f32[2,480]{1,0:T(2,128)S(1)} custom-call(s32[20]{0:T(128)S(1)} %stack.110.refs_0_, f32[1,896]{1,0:T(1,128)S(1)} %broadcast_in_dim.8.refs_1_, bf16[1024,1792]{1,0:T(8,128)(2,1)} %get-tuple-element.20.refs_2_, bf16[1024,1792]{1,0:T(8,128)(2,1)} %collective-permute-done.refs_3_, bf16[1024,512]{1,0:T(8,128)(2,1)S(1)} %collective-permute-done.3.refs_4_.refs_6_, ...), custom_call_target="tpu_custom_call" | custom-call | flops 4026531840 | bytes 8388608 | tf_op jit(solution)/shard_map/pallas_call | solution.py:179
  183.6 13.9 %collective-permute-done.10.refs_16_.refs_18_ = bf16[768,512]{1,0:T(8,128)(2,1)S(1)} collective-permute-done((bf16[768,512]{1,0:T(8,128)(2,1)}, bf16[768,512]{1,0:T(8,128)(2,1)S(1)}, u32[]{:S(2)}, u32[]{:S(2)}) %collective-permute-start.10) | collective-permute-done | bytes 786464 | tf_op jit(solution)/shard_map/ppermute | solution.py:238
  197.5 16.9 %collective-permute-done.13.refs_18_.refs_20_ = bf16[768,512]{1,0:T(8,128)(2,1)S(1)} collective-permute-done((bf16[768,512]{1,0:T(8,128)(2,1)S(1)}, bf16[768,512]{1,0:T(8,128)(2,1)S(1)}, u32[]{:S(2)}, u32[]{:S(2)}) %collective-permute-start.13) | collective-permute-done | bytes 786464 | tf_op jit(solution)/shard_map/ppermute | solution.py:238
  214.3 15.3 %collective-permute-done.16.refs_20_.refs_22_ = bf16[768,512]{1,0:T(8,128)(2,1)} collective-permute-done((bf16[768,512]{1,0:T(8,128)(2,1)S(1)}, bf16[768,512]{1,0:T(8,128)(2,1)}, u32[]{:S(2)}, u32[]{:S(2)}) %collective-permute-start.16) | collective-permute-done | bytes 786464 | tf_op jit(solution)/shard_map/ppermute | solution.py:238
  229.8 22.4 %shard_map.114 = (f32[2,480]{1,0:T(2,128)S(1)}, f32[2,384]{1,0:T(2,128)S(1)}) custom-call(s32[20]{0:T(128)S(1)} %stack.110.refs_0_, f32[1,896]{1,0:T(1,128)S(1)} %broadcast_in_dim.8.refs_1_, bf16[1024,1792]{1,0:T(8,128)(2,1)} %get-tuple-element.20.refs_2_, bf16[1024,1792]{1,0:T(8,128)(2,1)} %collective-permute-done.refs_3_, bf16[1024,512]{1,0:T(8,128)(2,1)} %copy-done, ...), custom_call_target="tpu_custom_call" | custom-call | flops 13690208256 | bytes 8388608 | tf_op jit(solution)/shard_map/pallas_call | solution.py:179
  252.3 14.7 %shard_map.115 = (f32[2,480]{1,0:T(2,128)S(1)}, f32[2,384]{1,0:T(2,128)S(1)}, f32[1,192]{1,0:T(1,128)S(1)}) custom-call(s32[20]{0:T(128)S(1)} %stack.110.refs_0_, f32[1,896]{1,0:T(1,128)S(1)} %broadcast_in_dim.8.refs_1_, bf16[1024,1792]{1,0:T(8,128)(2,1)} %get-tuple-element.20.refs_2_, bf16[1024,1792]{1,0:T(8,128)(2,1)} %collective-permute-done.refs_3_, ...), custom_call_target="tpu_custom_call" | custom-call | flops 6442450944 | bytes 8388608 | tf_op jit(solution)/shard_map/pallas_call | solution.py:179
  267.0 1.6 collective-permute-start.33
  268.6 2.0 collective-permute-done.33
  272.3 2.0 collective-permute-done.34
  274.3 2.5 collective-permute-start.37
  276.7 2.0 collective-permute-start.36
  278.8 4.2 %fusion.10 = f32[1024,1792]{1,0:T(8,128)} fusion(bf16[96,1792]{1,0:T(8,128)(2,1)S(1)} %bitcast.88, bf16[32,1024]{1,0:T(8,128)(2,1)S(1)} %get-tuple-element.35, bf16[32,1024]{1,0:T(8,128)(2,1)S(1)} %get-tuple-element.34, bf16[32,1024]{1,0:T(8,128)(2,1)S(1)} %get-tuple-element.33), kind=kOutput, calls=%fused_computation.28 | convolution fusion | flops 352911360 | bytes 7880704 | tf_op jit(solution)/shard_map/dot_general | solution.py:373
  (206 shorter events, 37.6 us)
Async XLA Ops:
  13.2 53.3 %collective-permute-start.19 = (bf16[1024,256]{1,0:T(8,128)(2,1)}, bf16[1024,256]{1,0:T(8,128)(2,1)S(1)}, u32[]{:S(2)}, u32[]{:S(2)}) collective-permute-start(bf16[1024,256]{1,0:T(8,128)(2,1)} %pad_maximum_fusion.3), channel_id=1, source_target_pairs={{0,16},{8,24},{16,0},{24,8},{1,17},{9,25},{17,1},{25,9},{2,18},{10... | collective-permute-start | bytes 1572872 | tf_op jit(solution)/shard_map/ppermute | solution.py:226
  17.8 33.4 %collective-permute-start.18 = (bf16[16,3968]{1,0:T(8,128)(2,1)}, bf16[16,3968]{1,0:T(8,128)(2,1)S(1)}, u32[]{:S(2)}, u32[]{:S(2)}) collective-permute-start(bf16[16,3968]{1,0:T(8,128)(2,1)} %get-tuple-element.44), channel_id=1, source_target_pairs={{0,16},{8,24},{16,0},{24,8},{1,17},{9,25},{17,1},{25,9},{2,18},{10... | collective-permute-start | bytes 380936 | tf_op jit(solution)/shard_map/ppermute | solution.py:226
  19.9 62.1 %collective-permute-start.7 = (bf16[768,512]{1,0:T(8,128)(2,1)}, bf16[768,512]{1,0:T(8,128)(2,1)S(1)}, u32[]{:S(2)}, u32[]{:S(2)}) collective-permute-start(bf16[768,512]{1,0:T(8,128)(2,1)} %constant_dynamic-slice_fusion.7), channel_id=1, source_target_pairs={{0,16},{8,24},{16,0},{24,8},{1,17},{9,25},{17,1},{25,9},{2,18},{10... | collective-permute-start | bytes 2359304 | tf_op jit(solution)/shard_map/ppermute | solution.py:226
  27.9 21.6 %collective-permute-start.17 = (f32[2,8,480]{2,1,0:T(8,128)}, f32[2,8,480]{2,1,0:T(8,128)}, u32[]{:S(2)}, u32[]{:S(2)}) collective-permute-start(f32[2,8,480]{2,1,0:T(8,128)} %convolution_multiply_fusion), channel_id=1, source_target_pairs={{0,16},{8,24},{16,0},{24,8},{1,17},{9,25},{17,1},{25,9},{2,18},{10... | collective-permute-start | bytes 92168 | tf_op jit(solution)/shard_map/ppermute | solution.py:226
  29.5 23.7 %collective-permute-start.21 = (bf16[192,512]{1,0:T(8,128)(2,1)}, bf16[192,512]{1,0:T(8,128)(2,1)S(1)}, u32[]{:S(2)}, u32[]{:S(2)}) collective-permute-start(bf16[192,512]{1,0:T(8,128)(2,1)} %constant_dynamic-slice_fusion.11), channel_id=1, source_target_pairs={{0,16},{8,24},{16,0},{24,8},{1,17},{9,25},{17,1},{25,9},{2,18},{10... | collective-permute-start | bytes 589832 | tf_op jit(solution)/shard_map/ppermute | solution.py:226
  53.1 3.0 %collective-permute-start.38 = (bf16[2,16,2944]{2,1,0:T(8,128)(2,1)S(1)}, bf16[2,16,2944]{2,1,0:T(8,128)(2,1)S(1)}, u32[]{:S(2)}, u32[]{:S(2)}) collective-permute-start(bf16[2,16,2944]{2,1,0:T(8,128)(2,1)S(1)} %get-tuple-element.32), channel_id=1, source_target_pairs={{0,8},{8,0},{16,24},{24,16},{1,9},{9,1},{17,25},{25,17},{2,10},{10... | collective-permute-start | bytes 565256 | tf_op jit(solution)/shard_map/ppermute | solution.py:230
  53.2 7.8 %collective-permute-start.22 = (bf16[192,512]{1,0:T(8,128)(2,1)S(1)}, bf16[192,512]{1,0:T(8,128)(2,1)S(1)}, u32[]{:S(2)}, u32[]{:S(2)}) collective-permute-start(bf16[192,512]{1,0:T(8,128)(2,1)S(1)} %collective-permute-done.21.refs_25_), channel_id=1, source_target_pairs={{0,2},{1,3},{2,0},{3,1},{4,6},{5,7},{6,4},{7,5},{8,10},{9,11},{10,... | collective-permute-start | bytes 589832 | tf_op jit(solution)/shard_map/ppermute | solution.py:233
  55.5 5.5 %collective-permute-start.23 = (bf16[192,512]{1,0:T(8,128)(2,1)S(1)}, bf16[192,512]{1,0:T(8,128)(2,1)S(1)}, u32[]{:S(2)}, u32[]{:S(2)}) collective-permute-start(bf16[192,512]{1,0:T(8,128)(2,1)S(1)} %collective-permute-done.21.refs_25_), channel_id=1, source_target_pairs={{0,0},{1,1},{2,4},{3,5},{4,2},{5,3},{6,6},{7,7},{8,8},{9,9},{10,12... | collective-permute-start | bytes 589832 | tf_op jit(solution)/shard_map/ppermute | solution.py:233
  56.2 9.6 %collective-permute-start.27 = (bf16[192,512]{1,0:T(8,128)(2,1)S(1)}, bf16[192,512]{1,0:T(8,128)(2,1)S(1)}, u32[]{:S(2)}, u32[]{:S(2)}) collective-permute-start(bf16[192,512]{1,0:T(8,128)(2,1)S(1)} %collective-permute-done.21.refs_25_), channel_id=1, source_target_pairs={{0,1},{1,0},{2,3},{3,2},{4,5},{5,4},{6,7},{7,6},{8,9},{9,8},{10,11... | collective-permute-start | bytes 589832 | tf_op jit(solution)/shard_map/ppermute | solution.py:238
  61.0 102.7 %collective-permute-start = (bf16[1024,1792]{1,0:T(8,128)(2,1)}, bf16[1024,1792]{1,0:T(8,128)(2,1)}, u32[]{:S(2)}, u32[]{:S(2)}) collective-permute-start(bf16[1024,1792]{1,0:T(8,128)(2,1)} %get-tuple-element.20.refs_2_), channel_id=1, source_target_pairs={{0,8},{8,0},{16,24},{24,16},{1,9},{9,1},{17,25},{25,17},{2,10},{10... | collective-permute-start | bytes 11010056 | tf_op jit(solution)/shard_map/ppermute | solution.py:230
  61.0 10.4 %collective-permute-start.24 = (bf16[192,512]{1,0:T(8,128)(2,1)S(1)}, bf16[192,512]{1,0:T(8,128)(2,1)S(1)}, u32[]{:S(2)}, u32[]{:S(2)}) collective-permute-start(bf16[192,512]{1,0:T(8,128)(2,1)S(1)} %collective-permute-done.23), channel_id=1, source_target_pairs={{0,2},{1,3},{2,0},{3,1},{4,6},{5,7},{6,4},{7,5},{8,10},{9,11},{10,... | collective-permute-start | bytes 589832 | tf_op jit(solution)/shard_map/ppermute | solution.py:233
  65.8 6.3 %collective-permute-start.25 = (bf16[192,512]{1,0:T(8,128)(2,1)S(1)}, bf16[192,512]{1,0:T(8,128)(2,1)S(1)}, u32[]{:S(2)}, u32[]{:S(2)}) collective-permute-start(bf16[192,512]{1,0:T(8,128)(2,1)S(1)} %collective-permute-done.22.refs_26_), channel_id=1, source_target_pairs={{0,0},{1,1},{2,4},{3,5},{4,2},{5,3},{6,6},{7,7},{8,8},{9,9},{10,12... | collective-permute-start | bytes 589832 | tf_op jit(solution)/shard_map/ppermute | solution.py:233
  66.5 14.2 %collective-permute-start.28 = (bf16[192,512]{1,0:T(8,128)(2,1)S(1)}, bf16[192,512]{1,0:T(8,128)(2,1)S(1)}, u32[]{:S(2)}, u32[]{:S(2)}) collective-permute-start(bf16[192,512]{1,0:T(8,128)(2,1)S(1)} %collective-permute-done.27.refs_29_), channel_id=1, source_target_pairs={{0,2},{1,3},{2,0},{3,1},{4,6},{5,7},{6,4},{7,5},{8,10},{9,11},{10,... | collective-permute-start | bytes 589832 | tf_op jit(solution)/shard_map/ppermute | solution.py:233
  71.4 5.2 %collective-permute-start.29 = (bf16[192,512]{1,0:T(8,128)(2,1)S(1)}, bf16[192,512]{1,0:T(8,128)(2,1)S(1)}, u32[]{:S(2)}, u32[]{:S(2)}) collective-permute-start(bf16[192,512]{1,0:T(8,128)(2,1)S(1)} %collective-permute-done.27.refs_29_), channel_id=1, source_target_pairs={{0,0},{1,1},{2,4},{3,5},{4,2},{5,3},{6,6},{7,7},{8,8},{9,9},{10,12... | collective-permute-start | bytes 589832 | tf_op jit(solution)/shard_map/ppermute | solution.py:233
  72.1 12.0 %collective-permute-start.26 = (bf16[192,512]{1,0:T(8,128)(2,1)S(1)}, bf16[192,512]{1,0:T(8,128)(2,1)S(1)}, u32[]{:S(2)}, u32[]{:S(2)}) collective-permute-start(bf16[192,512]{1,0:T(8,128)(2,1)S(1)} %collective-permute-done.25), channel_id=1, source_target_pairs={{0,2},{1,3},{2,0},{3,1},{4,6},{5,7},{6,4},{7,5},{8,10},{9,11},{10,... | collective-permute-start | bytes 589832 | tf_op jit(solution)/shard_map/ppermute | solution.py:233
  76.6 10.0 %collective-permute-start.30 = (bf16[192,512]{1,0:T(8,128)(2,1)S(1)}, bf16[192,512]{1,0:T(8,128)(2,1)}, u32[]{:S(2)}, u32[]{:S(2)}) collective-permute-start(bf16[192,512]{1,0:T(8,128)(2,1)S(1)} %collective-permute-done.29), channel_id=1, source_target_pairs={{0,2},{1,3},{2,0},{3,1},{4,6},{5,7},{6,4},{7,5},{8,10},{9,11},{10,... | collective-permute-start | bytes 589832 | tf_op jit(solution)/shard_map/ppermute | solution.py:233
  80.7 7.4 %collective-permute-start.31 = (bf16[192,512]{1,0:T(8,128)(2,1)S(1)}, bf16[192,512]{1,0:T(8,128)(2,1)}, u32[]{:S(2)}, u32[]{:S(2)}) collective-permute-start(bf16[192,512]{1,0:T(8,128)(2,1)S(1)} %collective-permute-done.28.refs_30_), channel_id=1, source_target_pairs={{0,0},{1,1},{2,4},{3,5},{4,2},{5,3},{6,6},{7,7},{8,8},{9,9},{10,12... | collective-permute-start | bytes 589832 | tf_op jit(solution)/shard_map/ppermute | solution.py:233
  82.0 21.8 %collective-permute-start.9 = (bf16[768,512]{1,0:T(8,128)(2,1)S(1)}, bf16[768,512]{1,0:T(8,128)(2,1)}, u32[]{:S(2)}, u32[]{:S(2)}) collective-permute-start(bf16[768,512]{1,0:T(8,128)(2,1)S(1)} %collective-permute-done.7.refs_13_.refs_15_), channel_id=1, source_target_pairs={{0,2},{1,3},{2,0},{3,1},{4,6},{5,7},{6,4},{7,5},{8,10},{9,11},{10,... | collective-permute-start | bytes 2359304 | tf_op jit(solution)/shard_map/ppermute | solution.py:233
  84.1 6.6 %collective-permute-start.11 = (bf16[768,512]{1,0:T(8,128)(2,1)S(1)}, bf16[768,512]{1,0:T(8,128)(2,1)}, u32[]{:S(2)}, u32[]{:S(2)}) collective-permute-start(bf16[768,512]{1,0:T(8,128)(2,1)S(1)} %collective-permute-done.7.refs_13_.refs_15_), channel_id=1, source_target_pairs={{0,0},{1,1},{2,4},{3,5},{4,2},{5,3},{6,6},{7,7},{8,8},{9,9},{10,12... | collective-permute-start | bytes 2359304 | tf_op jit(solution)/shard_map/ppermute | solution.py:233
  86.6 31.1 %collective-permute-start.1 = (bf16[1024,512]{1,0:T(8,128)(2,1)}, bf16[1024,512]{1,0:T(8,128)(2,1)S(1)}, u32[]{:S(2)}, u32[]{:S(2)}) collective-permute-start(bf16[1024,512]{1,0:T(8,128)(2,1)} %pad_maximum_fusion), channel_id=1, source_target_pairs={{0,16},{8,24},{16,0},{24,8},{1,17},{9,25},{17,1},{25,9},{2,18},{10... | collective-permute-start | bytes 3145736 | tf_op jit(solution)/shard_map/ppermute | solution.py:226
  88.2 47.3 %collective-permute-start.3 = (bf16[1024,512]{1,0:T(8,128)(2,1)}, bf16[1024,512]{1,0:T(8,128)(2,1)S(1)}, u32[]{:S(2)}, u32[]{:S(2)}) collective-permute-start(bf16[1024,512]{1,0:T(8,128)(2,1)} %pad_maximum_fusion.1), channel_id=1, source_target_pairs={{0,16},{8,24},{16,0},{24,8},{1,17},{9,25},{17,1},{25,9},{2,18},{10... | collective-permute-start | bytes 3145736 | tf_op jit(solution)/shard_map/ppermute | solution.py:226
  90.7 44.7 %collective-permute-start.12 = (bf16[768,512]{1,0:T(8,128)(2,1)}, bf16[768,512]{1,0:T(8,128)(2,1)}, u32[]{:S(2)}, u32[]{:S(2)}) collective-permute-start(bf16[768,512]{1,0:T(8,128)(2,1)} %collective-permute-done.11), channel_id=1, source_target_pairs={{0,2},{1,3},{2,0},{3,1},{4,6},{5,7},{6,4},{7,5},{8,10},{9,11},{10,... | collective-permute-start | bytes 2359304 | tf_op jit(solution)/shard_map/ppermute | solution.py:233
  103.9 32.1 %collective-permute-start.14 = (bf16[768,512]{1,0:T(8,128)(2,1)}, bf16[768,512]{1,0:T(8,128)(2,1)}, u32[]{:S(2)}, u32[]{:S(2)}) collective-permute-start(bf16[768,512]{1,0:T(8,128)(2,1)} %collective-permute-done.9.refs_15_.refs_17_), channel_id=1, source_target_pairs={{0,0},{1,1},{2,4},{3,5},{4,2},{5,3},{6,6},{7,7},{8,8},{9,9},{10,12... | collective-permute-start | bytes 2359304 | tf_op jit(solution)/shard_map/ppermute | solution.py:233
  117.8 46.6 %copy-start = (bf16[1024,512]{1,0:T(8,128)(2,1)}, bf16[1024,512]{1,0:T(8,128)(2,1)S(1)}, u32[]{:S(2)}) copy-start(bf16[1024,512]{1,0:T(8,128)(2,1)S(1)} %collective-permute-done.1.refs_4_) | copy-start | bytes 3145732
  117.8 35.1 %collective-permute-start.5 = (bf16[1024,512]{1,0:T(8,128)(2,1)}, bf16[1024,512]{1,0:T(8,128)(2,1)}, u32[]{:S(2)}, u32[]{:S(2)}) collective-permute-start(bf16[1024,512]{1,0:T(8,128)(2,1)} %pad_maximum_fusion.2), channel_id=1, source_target_pairs={{0,16},{8,24},{16,0},{24,8},{1,17},{9,25},{17,1},{25,9},{2,18},{10... | collective-permute-start | bytes 3145736 | tf_op jit(solution)/shard_map/ppermute | solution.py:226
  126.2 38.1 %copy-start.33 = (bf16[16,1792]{1,0:T(8,128)(2,1)S(1)}, bf16[16,1792]{1,0:T(8,128)(2,1)}, u32[]{:S(2)}) copy-start(bf16[16,1792]{1,0:T(8,128)(2,1)} %copy-done.32) | copy-start | bytes 172036
  135.4 38.4 %copy-start.1 = (bf16[1024,512]{1,0:T(8,128)(2,1)}, bf16[1024,512]{1,0:T(8,128)(2,1)S(1)}, u32[]{:S(2)}) copy-start(bf16[1024,512]{1,0:T(8,128)(2,1)S(1)} %collective-permute-done.3.refs_4_.refs_6_) | copy-start | bytes 3145732
  135.5 26.2 %collective-permute-start.2 = (bf16[1024,512]{1,0:T(8,128)(2,1)S(1)}, bf16[1024,512]{1,0:T(8,128)(2,1)S(1)}, u32[]{:S(2)}, u32[]{:S(2)}) collective-permute-start(bf16[1024,512]{1,0:T(8,128)(2,1)S(1)} %collective-permute-done.1.refs_4_), channel_id=1, source_target_pairs={{0,8},{8,0},{16,24},{24,16},{1,9},{9,1},{17,25},{25,17},{2,10},{10... | collective-permute-start | bytes 3145736 | tf_op jit(solution)/shard_map/ppermute | solution.py:230
  135.5 26.8 %collective-permute-start.4 = (bf16[1024,512]{1,0:T(8,128)(2,1)S(1)}, bf16[1024,512]{1,0:T(8,128)(2,1)S(1)}, u32[]{:S(2)}, u32[]{:S(2)}) collective-permute-start(bf16[1024,512]{1,0:T(8,128)(2,1)S(1)} %collective-permute-done.3.refs_4_.refs_6_), channel_id=1, source_target_pairs={{0,8},{8,0},{16,24},{24,16},{1,9},{9,1},{17,25},{25,17},{2,10},{10... | collective-permute-start | bytes 3145736 | tf_op jit(solution)/shard_map/ppermute | solution.py:230
  136.0 20.6 %collective-permute-start.15 = (bf16[768,512]{1,0:T(8,128)(2,1)}, bf16[768,512]{1,0:T(8,128)(2,1)S(1)}, u32[]{:S(2)}, u32[]{:S(2)}) collective-permute-start(bf16[768,512]{1,0:T(8,128)(2,1)} %collective-permute-done.14), channel_id=1, source_target_pairs={{0,2},{1,3},{2,0},{3,1},{4,6},{5,7},{6,4},{7,5},{8,10},{9,11},{10,... | collective-permute-start | bytes 2359304 | tf_op jit(solution)/shard_map/ppermute | solution.py:233
  142.1 87.6 %copy-start.4 = (bf16[768,512]{1,0:T(8,128)(2,1)}, bf16[768,512]{1,0:T(8,128)(2,1)S(1)}, u32[]{:S(2)}) copy-start(bf16[768,512]{1,0:T(8,128)(2,1)S(1)} %broadcast_select_fusion.1.refs_17_.refs_19_) | copy-start | bytes 2359300
  152.8 7.3 %collective-permute-start.32 = (bf16[192,512]{1,0:T(8,128)(2,1)}, bf16[192,512]{1,0:T(8,128)(2,1)S(1)}, u32[]{:S(2)}, u32[]{:S(2)}) collective-permute-start(bf16[192,512]{1,0:T(8,128)(2,1)} %collective-permute-done.31), channel_id=1, source_target_pairs={{0,2},{1,3},{2,0},{3,1},{4,6},{5,7},{6,4},{7,5},{8,10},{9,11},{10,... | collective-permute-start | bytes 589832 | tf_op jit(solution)/shard_map/ppermute | solution.py:233
  156.5 27.0 %collective-permute-start.6 = (bf16[1024,512]{1,0:T(8,128)(2,1)}, bf16[1024,512]{1,0:T(8,128)(2,1)S(1)}, u32[]{:S(2)}, u32[]{:S(2)}) collective-permute-start(bf16[1024,512]{1,0:T(8,128)(2,1)} %collective-permute-done.5.refs_8_), channel_id=1, source_target_pairs={{0,8},{8,0},{16,24},{24,16},{1,9},{9,1},{17,25},{25,17},{2,10},{10... | collective-permute-start | bytes 3145736 | tf_op jit(solution)/shard_map/ppermute | solution.py:230
  156.6 73.1 %copy-start.5 = (bf16[768,512]{1,0:T(8,128)(2,1)}, bf16[768,512]{1,0:T(8,128)(2,1)S(1)}, u32[]{:S(2)}) copy-start(bf16[768,512]{1,0:T(8,128)(2,1)S(1)} %broadcast_select_fusion.refs_19_.refs_21_) | copy-start | bytes 2359300
  160.2 23.3 %collective-permute-start.8 = (bf16[768,512]{1,0:T(8,128)(2,1)S(1)}, bf16[768,512]{1,0:T(8,128)(2,1)S(1)}, u32[]{:S(2)}, u32[]{:S(2)}) collective-permute-start(bf16[768,512]{1,0:T(8,128)(2,1)S(1)} %collective-permute-done.7.refs_13_.refs_15_), channel_id=1, source_target_pairs={{0,1},{1,0},{2,3},{3,2},{4,5},{5,4},{6,7},{7,6},{8,9},{9,8},{10,11... | collective-permute-start | bytes 2359304 | tf_op jit(solution)/shard_map/ppermute | solution.py:238
  161.7 35.8 %collective-permute-start.10 = (bf16[768,512]{1,0:T(8,128)(2,1)}, bf16[768,512]{1,0:T(8,128)(2,1)S(1)}, u32[]{:S(2)}, u32[]{:S(2)}) collective-permute-start(bf16[768,512]{1,0:T(8,128)(2,1)} %collective-permute-done.9.refs_15_.refs_17_), channel_id=1, source_target_pairs={{0,1},{1,0},{2,3},{3,2},{4,5},{5,4},{6,7},{7,6},{8,9},{9,8},{10,11... | collective-permute-start | bytes 2359304 | tf_op jit(solution)/shard_map/ppermute | solution.py:238
  162.2 52.1 %collective-permute-start.13 = (bf16[768,512]{1,0:T(8,128)(2,1)S(1)}, bf16[768,512]{1,0:T(8,128)(2,1)S(1)}, u32[]{:S(2)}, u32[]{:S(2)}) collective-permute-start(bf16[768,512]{1,0:T(8,128)(2,1)S(1)} %broadcast_select_fusion.1.refs_17_.refs_19_), channel_id=1, source_target_pairs={{0,1},{1,0},{2,3},{3,2},{4,5},{5,4},{6,7},{7,6},{8,9},{9,8},{10,11... | collective-permute-start | bytes 2359304 | tf_op jit(solution)/shard_map/ppermute | solution.py:238
  163.7 65.9 %collective-permute-start.16 = (bf16[768,512]{1,0:T(8,128)(2,1)S(1)}, bf16[768,512]{1,0:T(8,128)(2,1)}, u32[]{:S(2)}, u32[]{:S(2)}) collective-permute-start(bf16[768,512]{1,0:T(8,128)(2,1)S(1)} %broadcast_select_fusion.refs_19_.refs_21_), channel_id=1, source_target_pairs={{0,1},{1,0},{2,3},{3,2},{4,5},{5,4},{6,7},{7,6},{8,9},{9,8},{10,11... | collective-permute-start | bytes 2359304 | tf_op jit(solution)/shard_map/ppermute | solution.py:238
  173.9 55.8 %copy-start.31 = (bf16[16,1792]{1,0:T(8,128)(2,1)S(1)}, bf16[16,1792]{1,0:T(8,128)(2,1)}, u32[]{:S(2)}) copy-start(bf16[16,1792]{1,0:T(8,128)(2,1)} %copy-done.30) | copy-start | bytes 172036
  173.9 55.8 %copy-start.8 = (bf16[6,2,8,384]{3,2,0,1:T(8,128)(2,1)S(1)}, bf16[6,2,8,384]{3,2,0,1:T(8,128)(2,1)}, u32[]{:S(2)}) copy-start(bf16[6,2,8,384]{3,2,0,1:T(8,128)(2,1)} %copy.22) | copy-start | bytes 221188
  183.5 68.8 %collective-permute-start.20 = (bf16[1024,256]{1,0:T(8,128)(2,1)S(1)}, bf16[1024,256]{1,0:T(8,128)(2,1)S(1)}, u32[]{:S(2)}, u32[]{:S(2)}) collective-permute-start(bf16[1024,256]{1,0:T(8,128)(2,1)S(1)} %collective-permute-done.19.refs_10_), channel_id=1, source_target_pairs={{0,8},{8,0},{16,24},{24,16},{1,9},{9,1},{17,25},{25,17},{2,10},{10... | collective-permute-start | bytes 1572872 | tf_op jit(solution)/shard_map/ppermute | solution.py:230
  183.5 46.1 %copy-start.19 = (bf16[1024,512]{1,0:T(8,128)(2,1)}, bf16[1024,512]{1,0:T(8,128)(2,1)S(1)}, u32[]{:S(2)}) copy-start(bf16[1024,512]{1,0:T(8,128)(2,1)S(1)} %collective-permute-done.6.refs_9_) | copy-start | bytes 3145732
  197.5 54.7 %copy-start.6 = (bf16[768,512]{1,0:T(8,128)(2,1)}, bf16[768,512]{1,0:T(8,128)(2,1)S(1)}, u32[]{:S(2)}) copy-start(bf16[768,512]{1,0:T(8,128)(2,1)S(1)} %collective-permute-done.10.refs_16_.refs_18_) | copy-start | bytes 2359300
  267.0 3.7 %collective-permute-start.33 = (f32[960]{0:T(1024)S(1)}, f32[960]{0:T(1024)S(1)}, u32[]{:S(2)}, u32[]{:S(2)}) collective-permute-start(f32[960]{0:T(1024)S(1)} %pad_maximum_fusion.11), channel_id=1, source_target_pairs={{0,16},{8,24},{16,0},{24,8},{1,17},{9,25},{17,1},{25,9},{2,18},{10... | collective-permute-start | bytes 11528 | tf_op jit(solution)/shard_map/ppermute | solution.py:226
  270.7 3.6 %collective-permute-start.34 = (f32[960]{0:T(1024)S(1)}, f32[960]{0:T(1024)S(1)}, u32[]{:S(2)}, u32[]{:S(2)}) collective-permute-start(f32[960]{0:T(1024)S(1)} %add.159), channel_id=1, source_target_pairs={{0,1},{1,0},{2,3},{3,2},{4,5},{5,4},{6,7},{7,6},{8,9},{9,8},{10,11... | collective-permute-start | bytes 11528 | tf_op jit(solution)/shard_map/ppermute | solution.py:238
  274.3 8.7 %collective-permute-start.37 = (f32[960]{0:T(1024)S(1)}, f32[960]{0:T(1024)S(1)}, u32[]{:S(2)}, u32[]{:S(2)}) collective-permute-start(f32[960]{0:T(1024)S(1)} %add.160), channel_id=1, source_target_pairs={{0,6},{1,7},{2,0},{3,1},{4,2},{5,3},{6,4},{7,5},{8,14},{9,15},{10,... | collective-permute-start | bytes 11528 | tf_op jit(solution)/shard_map/ppermute | solution.py:233
  276.7 6.2 %collective-permute-start.35 = (f32[960]{0:T(1024)S(1)}, f32[960]{0:T(1024)S(1)}, u32[]{:S(2)}, u32[]{:S(2)}) collective-permute-start(f32[960]{0:T(1024)S(1)} %add.160), channel_id=1, source_target_pairs={{0,2},{1,3},{2,4},{3,5},{4,6},{5,7},{6,0},{7,1},{8,10},{9,11},{10,... | collective-permute-start | bytes 11528 | tf_op jit(solution)/shard_map/ppermute | solution.py:233
  276.7 6.2 %collective-permute-start.36 = (f32[960]{0:T(1024)S(1)}, f32[960]{0:T(1024)S(1)}, u32[]{:S(2)}, u32[]{:S(2)}) collective-permute-start(f32[960]{0:T(1024)S(1)} %add.160), channel_id=1, source_target_pairs={{0,4},{1,5},{2,6},{3,7},{4,0},{5,1},{6,2},{7,3},{8,12},{9,13},{10,... | collective-permute-start | bytes 11528 | tf_op jit(solution)/shard_map/ppermute | solution.py:233
  (29 other events, 445.4 us)

commit v2 on v0

v2 whole, which is shorter than its diff:
```python
import functools
import math

import jax
import jax.numpy as jnp
from jax import lax
from jax.experimental import pallas as pl
from jax.experimental.pallas import tpu as pltpu
from jax.sharding import PartitionSpec as P

F32 = jnp.float32
BF16 = jnp.bfloat16
MIB = 1024 * 1024
VMEM_BYTES = 64 * MIB
SMALL = pl.CostEstimate(flops=1, bytes_accessed=1, transcendentals=0)


def split3(value):
    top = lax.reduce_precision(value, 8, 7)
    rest = value - top
    middle = lax.reduce_precision(rest, 8, 7)
    return [term.astype(BF16) for term in (top, middle, rest - middle)]


def column_chunks(width):
    cuts, begin = [], 0
    while begin < width:
        size = min(256, width - begin)
        cuts.append((begin, size))
        begin += size
    return cuts


def line_sizes(total):
    outer = 4 if total % 4 == 0 else 1
    return outer, total // outer


def swap_pairs(total, partner):
    return [(index, partner(index)) for index in range(total)]


def line_steps(own, size, coord, permute):
    if size != 4:
        for step in range(1, size):
            block = permute(own, lambda c, step=step: (c + step) % size)
            hold = yield
            yield hold(block), (coord + size - step) % size
        return
    even = lambda c: c ^ 1
    odd = lambda c: 3 - c if c in (1, 2) else None
    edge = jnp.logical_or(coord == 0, coord == 3)
    places = [
        jnp.where(coord == 0, a, jnp.where(coord == 1, b, jnp.where(coord == 2, c, d)))
        for a, b, c, d in ((1, 0, 3, 2), (2, 2, 1, 1), (3, 3, 0, 0))
    ]
    first, across = permute(own, even), permute(own, odd)
    hold = yield
    first, across = hold(first), hold(across)
    yield first, places[0]
    ahead, over = permute(across, even), permute(first, odd)
    hold = yield
    ahead, over = hold(ahead), hold(over)
    yield jnp.where(edge, ahead, across), places[1]
    ahead = permute(over, even)
    hold = yield
    yield jnp.where(edge, hold(ahead), over), places[2]


def line_gather(own, size, coord, permute):
    found, steps = [(own, coord)], line_steps(own, size, coord, permute)
    for _ in range(size - 1):
        next(steps)
        found.append(steps.send(lambda value: value))
    return found


def after(value, *others):
    anywhere = pl.BlockSpec(memory_space=pltpu.HBM)
    return pl.pallas_call(
        lambda *refs: None,
        out_shape=jax.ShapeDtypeStruct(value.shape, value.dtype),
        in_specs=[anywhere] * (1 + len(others)),
        out_specs=anywhere,
        input_output_aliases={0: 0},
        compiler_params=pltpu.CompilerParams(vmem_limit_bytes=VMEM_BYTES),
        cost_estimate=SMALL,
    )(value, *others)


def gated_scores(ids, chunks, own, blocks, parts, readout, waited=()):
    arrays, specs = [], []

    def add(array, space):
        for index, seen in enumerate(arrays):
            if seen is array:
                return index
        arrays.append(array)
        specs.append(pl.BlockSpec(memory_space=space))
        return len(arrays) - 1

    add(ids, pltpu.SMEM)
    add(readout, pltpu.VMEM)
    for array in waited:
        add(array, pltpu.HBM)
    lines = own[1].shape[1]
    tiles, tile, width = own[0].shape
    place_count, block_rows = blocks[1].shape[0], blocks[1].shape[2]
    chunk_rows = chunks[0][2][0][0].shape[0]
    sizes = sorted({size for _, size, _ in chunks}, reverse=True)
    used_chunks = sorted({j for part in parts for j in range(part[3], part[4])})
    used_tiles = sorted({t for part in parts if part[0] for t in range(part[1], part[2])})
    used_blocks = sorted({t for part in parts if not part[0] for t in range(part[1], part[2])})
    slots, scratch, shapes, copies = {}, [], [], 0
    size_at = {}
    for size in sizes:
        those = [j for j in used_chunks if chunks[j][1] == size]
        if those:
            size_at[size] = len(scratch)
            scratch.append(pltpu.VMEM((len(those), width, 2 * size), BF16))
            for slot, j in enumerate(those):
                slots[j] = slot
    chunk_refs = {j: [(add(source[0], pltpu.HBM),) + source[1:] for source in chunks[j][2]] for j in used_chunks}
    copies += sum(len(refs) for refs in chunk_refs.values())
    own_at = block_at = own_out = block_out = None
    if used_tiles:
        own_at, own_out = len(scratch), len(shapes)
        scratch.append(pltpu.VMEM((len(used_tiles), tile, width), BF16))
        shapes.append(jax.ShapeDtypeStruct((tiles, tile), F32))
        own_ref, own_lines, own_cols = add(own[0], pltpu.HBM), add(own[1], pltpu.VMEM), add(own[2], pltpu.VMEM)
        copies += len(used_tiles)
    if used_blocks:
        block_at, block_out = len(scratch), len(shapes)
        scratch.append(pltpu.VMEM((len(used_blocks), block_rows, width), BF16))
        shapes.append(jax.ShapeDtypeStruct((place_count, block_rows), F32))
        far_lines, far_cols = add(blocks[1], pltpu.VMEM), add(blocks[2], pltpu.VMEM)
        block_refs = {n: [(add(array, pltpu.HBM), place) for array, place in blocks[0][n][1]] for n in used_blocks}
        copies += sum(len(refs) for refs in block_refs.values())
    scratch.append(pltpu.SemaphoreType.DMA((copies,)))
    inputs, outputs = len(arrays), len(shapes)

    def kernel(*refs):
        ids_ref, readout_ref = refs[0], refs[1]
        outs, held = refs[inputs : inputs + outputs], refs[inputs + outputs :]
        sems = held[-1]
        pending, count = {}, 0

        def fetch(key):
            nonlocal count
            if key in pending:
                return
            pairs = []
            if key[0] == "chunk":
                target = held[size_at[chunks[key[1]][1]]].at[slots[key[1]]]
                for index, lane, shift, to, lanes, place in chunk_refs[key[1]]:
                    first = pl.multiple_of(ids_ref[place] * chunk_rows, chunk_rows)
                    if shift is not None:
                        lane = pl.multiple_of(ids_ref[shift] * 128 + lane, 128)
                    source = refs[index].at[:, pl.ds(lane, lanes)]
                    pairs.append((source, target.at[pl.ds(first, chunk_rows), pl.ds(to, lanes)]))
            elif key[0] == "own":
                pairs.append((refs[own_ref].at[key[1]], held[own_at].at[used_tiles.index(key[1])]))
            else:
                for index, place in block_refs[key[1]]:
                    lanes = refs[index].shape[1]
                    first = pl.multiple_of(ids_ref[place] * lanes, lanes)
                    target = held[block_at].at[used_blocks.index(key[1]), :, pl.ds(first, lanes)]
                    pairs.append((refs[index], target))
            pending[key] = []
            for source, target in pairs:
                pending[key].append(pltpu.make_async_copy(source, target, sems.at[count]))
                pending[key][-1].start()
                count += 1

        def keys(part):
            mine, begin, end, first, last = part
            found = [("chunk", j) for j in range(first, last)]
            return found + [("own" if mine else "block", n) for n in range(begin, end)]

        for part in parts[:2]:
            for key in keys(part):
                fetch(key)
        for out in outs:
            out[...] = jnp.zeros(out.shape, F32)
        for number, part in enumerate(parts):
            for key in keys(part):
                for copy in pending[key]:
                    copy.wait()
                pending[key] = []
            if number + 2 < len(parts):
                for key in keys(parts[number + 2]):
                    fetch(key)
            mine, begin, end, first, last = part
            size = chunks[first][1]
            span = last - first

            def step(n, carry, mine=mine, begin=begin, end=end, first=first, size=size, span=span):
                t, j = n // span, n % span
                weights = held[size_at[size]].at[slots[first] + j]
                if mine:
                    tokens = held[own_at].at[used_tiles.index(begin) + t]
                    noise, columns = refs[own_lines].at[begin + t], refs[own_cols]
                    out, row = outs[own_out], begin + t
                else:
                    tokens = held[block_at].at[used_blocks.index(begin) + t]
                    row = ids_ref[blocks[0][begin][0] + t]
                    noise, columns = refs[far_lines].at[row], refs[far_cols]
                    out = outs[block_out]
                total = jnp.dot(tokens[...], weights[...], preferred_element_type=F32)
                at = chunks[first][0] + j * size
                if size % 128 == 0:
                    at = pl.multiple_of(at, 128)
                total += lax.dot_general(
                    noise[...],
                    columns[:, pl.ds(2 * at, 2 * size)],
                    (((0,), (0,)), ((), ())),
                    preferred_element_type=F32,
                )
                gate, up = total[:, :size], total[:, size:]
                value = gate / (1.0 + jnp.exp(-gate)) * up * readout_ref[:, pl.ds(at, size)]
                if size == 256:
                    value = value[:, :128] + value[:, 128:]
                out[pl.ds(row, 1), :] += jnp.sum(value.T, axis=0, keepdims=True)
                return carry

            if (end - begin) * span == 1:
                step(0, 0)
            else:
                lax.fori_loop(0, (end - begin) * span, step, 0)

    results = pl.pallas_call(
        kernel,
        out_shape=shapes,
        in_specs=specs,
        out_specs=[pl.BlockSpec(memory_space=pltpu.VMEM)] * len(shapes),
        scratch_shapes=scratch,
        compiler_params=pltpu.CompilerParams(vmem_limit_bytes=VMEM_BYTES),
        cost_estimate=SMALL,
    )(*arrays)
    return (results[own_out] if used_tiles else None), (results[block_out] if used_blocks else None)


def noise_columns(gate, up, cuts):
    blocks = []
    for begin, size in cuts:
        blocks += [gate[:, begin : begin + size], up[:, begin : begin + size]]
    value = jnp.concatenate(blocks, 1).astype(BF16)
    return jnp.concatenate([value] * 3, 0)


def own_factors(tokens, a_gate, a_up, gate_cols, up_cols, gate_half, up_half, marks, start, scale, cuts, waited):
    members, tok_count, width = tokens.shape
    rank, hidden, half = a_gate.shape[1], gate_cols.shape[2], gate_half.shape[2]
    lines, block_half = 2 * members * rank, width // 2

    def kernel(start_ref, tok_ref, ag, au, gc, uc, gh, uh, marks_ref, waited_ref, bundle, rows, cols):
        def both(gate, up):
            found = []
            for m in range(members):
                found += [gate(m).astype(F32), up(m).astype(F32)]
            return jnp.concatenate(found, 0).astype(BF16)

        bundle[:, :hidden] = both(lambda m: gc[m], lambda m: uc[m])
        lanes = pl.ds(pl.multiple_of(start_ref[0] * 128, 128), block_half)
        bundle[:, hidden : hidden + block_half] = both(lambda m: ag[m, :, lanes], lambda m: au[m, :, lanes])
        bundle[:, hidden + block_half : hidden + block_half + 128] = marks_ref[...]
        terms = []
        for m in range(members):
            factors = jnp.concatenate([ag[m].astype(F32), au[m].astype(F32)], 0).astype(BF16)
            value = scale * lax.dot_general(
                factors, tok_ref[m], (((1,), (1,)), ((), ())), preferred_element_type=F32
            )
            found = []
            for _ in range(3):
                found.append(value.astype(BF16).astype(F32))
                value = value - found[-1]
            terms.append(found)
            zero = jnp.zeros_like(value)
            lines_of = [found[n] if other == m else zero for n in range(3) for other in range(members)]
            rows[m] = jnp.concatenate(lines_of, 0).astype(BF16)
        ends = jnp.concatenate([jnp.concatenate(found, 1) for found in terms], 0)
        bundle[:, hidden + block_half + 128 :] = ends.astype(BF16)
        gates, ups = [], []
        for m in range(members):
            gate, up = gh[m].astype(F32), uh[m].astype(F32)
            gates += [gate, jnp.zeros_like(gate)]
            ups += [jnp.zeros_like(up), up]
        cols[...] = noise_columns(jnp.concatenate(gates, 0), jnp.concatenate(ups, 0), cuts)

    vmem = pl.BlockSpec(memory_space=pltpu.VMEM)
    return pl.pallas_call(
        kernel,
        out_shape=[
            jax.ShapeDtypeStruct((lines, hidden + block_half + 128 + 3 * tok_count), BF16),
            jax.ShapeDtypeStruct((members, 3 * lines, tok_count), BF16),
            jax.ShapeDtypeStruct((3 * lines, 2 * half), BF16),
        ],
        in_specs=[pl.BlockSpec(memory_space=pltpu.SMEM)] + [vmem] * 8 + [pl.BlockSpec(memory_space=pltpu.HBM)],
        out_specs=[vmem] * 3,
        compiler_params=pltpu.CompilerParams(vmem_limit_bytes=VMEM_BYTES),
        cost_estimate=SMALL,
    )(start, tokens, a_gate, a_up, gate_cols, up_cols, gate_half, up_half, marks, waited)


def other_factors(bundle, half_cols, first, members, tok_count, tile, cuts):
    lines, half = half_cols.shape
    rank = lines // members // 2
    count = members * tok_count // tile

    def kernel(bundle_ref, half_ref, rows, cols):
        for block in range(count):
            m, at = block * tile // tok_count, block * tile % tok_count
            found = []
            for n in range(3):
                lane = first + n * tok_count + at
                value = bundle_ref[:, lane : lane + tile].astype(F32)
                line = lax.broadcasted_iota(jnp.int32, value.shape, 0)
                found.append(jnp.where(line // (2 * rank) == m, value, 0.0))
            rows[block] = jnp.concatenate(found, 0).astype(BF16)
        value = half_ref[...].astype(F32)
        is_gate = lax.broadcasted_iota(jnp.int32, value.shape, 0) % (2 * rank) < rank
        cols[...] = noise_columns(jnp.where(is_gate, value, 0.0), jnp.where(is_gate, 0.0, value), cuts)

    vmem = pl.BlockSpec(memory_space=pltpu.VMEM)
    return pl.pallas_call(
        kernel,
        out_shape=[
            jax.ShapeDtypeStruct((count, 3 * lines, tile), BF16),
            jax.ShapeDtypeStruct((3 * lines, 2 * half), BF16),
        ],
        in_specs=[vmem] * 2,
        out_specs=[vmem] * 2,
        compiler_params=pltpu.CompilerParams(vmem_limit_bytes=VMEM_BYTES),
        cost_estimate=SMALL,
    )(bundle, half_cols)


def cut_blocks(gate, up, shift, cuts, waited):
    rows = gate.shape[0]

    def kernel(shift_ref, gate_ref, up_ref, waited_ref, *refs):
        blocks, held, sems = refs[: len(cuts)], refs[len(cuts) : -1], refs[-1]
        first, second = [], []
        for n, (begin, size) in enumerate(cuts):
            lanes = pl.ds(pl.multiple_of(shift_ref[0] * 128 + begin, 128), size)
            first.append([])
            for kind, source in enumerate((gate_ref, up_ref)):
                target = held[n].at[:, pl.ds(kind * size, size)]
                first[n].append(pltpu.make_async_copy(source.at[:, lanes], target, sems.at[3 * n + kind]))
                first[n][kind].start()
            second.append(pltpu.make_async_copy(held[n], blocks[n], sems.at[3 * n + 2]))
        for n in range(len(cuts)):
            for copy in first[n]:
                copy.wait()
            second[n].start()
        for copy in second:
            copy.wait()

    anywhere = pl.BlockSpec(memory_space=pltpu.HBM)
    return pl.pallas_call(
        kernel,
        out_shape=[jax.ShapeDtypeStruct((rows, 2 * size), gate.dtype) for _, size in cuts],
        in_specs=[pl.BlockSpec(memory_space=pltpu.SMEM), anywhere, anywhere, anywhere],
        out_specs=[anywhere] * len(cuts),
        scratch_shapes=[pltpu.VMEM((rows, 2 * size), gate.dtype) for _, size in cuts]
        + [pltpu.SemaphoreType.DMA((3 * len(cuts),))],
        compiler_params=pltpu.CompilerParams(vmem_limit_bytes=VMEM_BYTES),
        cost_estimate=SMALL,
    )(shift, gate, up, waited)


def body(
    pop_size,
    shard_size,
    tokens,
    gate_weight_matrix,
    w_up,
    a_gate,
    a_up,
    gate_hidden_factors,
    up_hidden_factors,
    fitness,
    readout,
):
    members, tok_count, model_width = tokens.shape
    rank = a_gate.shape[1]
    rows = members * tok_count
    block_rows, hidden = gate_weight_matrix.shape
    half = hidden // 2
    lo_size = pop_size // 2
    outer, inner = line_sizes(shard_size)
    noise_scale = 0.25 / math.sqrt(model_width * rank)
    pop, shard = lax.axis_index("pop"), lax.axis_index("shard")
    hi, lo = pop // lo_size, pop % lo_size
    flat = tokens.reshape(rows, model_width)
    chunks = column_chunks(half)

    across_pairs = [(p, (p + lo_size) % pop_size) for p in range(pop_size)]

    def across(value):
        return lax.ppermute(value, "pop", across_pairs)

    def along(value, step):
        pairs = [(p, p // lo_size * lo_size + (p + step) % lo_size) for p in range(pop_size)]
        return lax.ppermute(value, "pop", pairs)

    def outer_permute(value, target):
        pairs = [(s, target(s // inner), s % inner) for s in range(shard_size)]
        return lax.ppermute(value, "shard", [(s, z * inner + y) for s, z, y in pairs if z is not None])

    def inner_permute(value, target):
        pairs = [(s, s // inner, target(s % inner)) for s in range(shard_size)]
        return lax.ppermute(value, "shard", [(s, z * inner + y) for s, z, y in pairs if y is not None])

    z, y = shard // inner, shard % inner
    size_z, size_y = rows // outer, model_width // inner
    block = lax.dynamic_slice(flat, (z * size_z, y * size_y), (size_z, size_y))
    sent = across(block)

    lines = 2 * members * rank
    block_half = model_width // 2
    marks = jnp.broadcast_to(fitness[:, None], (members, 2 * rank * 128)).reshape(lines, 128)

    def in_half(value):
        return lax.dynamic_slice_in_dim(value, hi * half, half, value.ndim - 1)

    bundle, own_lines, own_columns = own_factors(
        tokens,
        a_gate,
        a_up,
        gate_hidden_factors,
        up_hidden_factors,
        in_half(gate_hidden_factors),
        in_half(up_hidden_factors),
        marks,
        ((1 - hi) * (block_half // 128)).astype(jnp.int32)[None],
        noise_scale,
        chunks,
        block,
    )
    other_bundle = across(bundle)
    bundle_width = hidden + block_half + 128

    def pick(which):
        if half % 128 == 0:
            shift = (which * (half // 128)).astype(jnp.int32)[None]
            return cut_blocks(gate_weight_matrix, w_up, shift, chunks, bundle)
        gate = lax.dynamic_slice_in_dim(gate_weight_matrix, which * half, half, 1)
        up = lax.dynamic_slice_in_dim(w_up, which * half, half, 1)
        return [
            jnp.concatenate([gate[:, begin : begin + size], up[:, begin : begin + size]], 1) for begin, size in chunks
        ]

    cut = pick(1 - hi)
    if half % 128 == 0:
        near = [(along(gate_weight_matrix, step), along(w_up, step)) for step in range(1, lo_size)]
        near = [(gate_weight_matrix, w_up)] + near
    else:
        kept = jnp.concatenate(pick(hi), 1)
        near = [kept] + [along(kept, step) for step in range(1, lo_size)]

    sent = after(sent, *cut, *jax.tree.leaves(near[1:]))
    other_bundle = after(other_bundle, sent)

    both = jnp.stack([bundle[:, :bundle_width], other_bundle[:, :bundle_width]])
    heads = both[:, :, :hidden]
    marks = both[:, :, hidden + block_half :]
    factors = jnp.concatenate([a_gate, a_up], 1)
    factor_parts = jnp.stack(
        [
            lax.dynamic_slice_in_dim(factors.reshape(lines, model_width), hi * block_half, block_half, 1),
            other_bundle[:, hidden : hidden + block_half],
        ]
    )

    def packed(target):
        return jnp.concatenate(
            [heads, lax.dynamic_slice_in_dim(factor_parts, target * block_rows, block_rows, 2), marks], 2
        )

    every = [packed(lo)]
    for step in range(1, lo_size):
        every.append(along(packed((lo + step) % lo_size), step))
    every = jnp.stack(every).reshape(pop_size, members, 2, rank, hidden + block_rows + 128)
    weighting = every[..., -1:].astype(F32) / math.sqrt(pop_size * members * rank)

    def direction(kind):
        part = every[:, :, kind].reshape(pop_size * members * rank, -1)
        weight = weighting[:, :, kind].reshape(-1, 1)
        left = jnp.concatenate(split3(part[:, hidden : hidden + block_rows].astype(F32) * weight))
        right = jnp.tile(part[:, :hidden], (3, 1))
        return lax.dot_general(left, right, (((0,), (0,)), ((), ())), preferred_element_type=F32)

    directions = [direction(0), direction(1)]

    far_lines, far_columns = other_factors(
        other_bundle, in_half(other_bundle[:, :hidden]), bundle_width, members, tok_count, size_z, chunks
    )
    half_readout = lax.dynamic_slice_in_dim(readout, hi * half, half, 0)[None, :]
    own = (tokens, own_lines, own_columns)
    held_at = pop_size + 1
    part_at = held_at + outer

    steps = line_steps(sent, outer, z, outer_permute)
    held, spread, far, chunk_list = [(sent, z)], [line_gather(sent, inner, y, inner_permute)], [], []
    end = len(chunks)
    passed = [across(cut[0])] + [None] * (end - 1)
    own_total = other_total = 0.0
    done, barrier = [0] * outer, list(directions)

    def gather_next():
        next(steps)
        held.append(steps.send(lambda value: after(value, *barrier)))
        spread.append(line_gather(held[-1][0], inner, y, inner_permute))

    def bring(j):
        if passed[j] is None:
            passed[j] = across(after(cut[j], *(far[j - 2] if j > 1 else [every])))
        return passed[j]

    def score(parts):
        nonlocal own_total, other_total
        places = [hi * lo_size + (lo + lo_size - step) % lo_size for step in range(lo_size)]
        places += [(1 - hi) * lo_size + (lo + lo_size - step) % lo_size for step in range(lo_size)]
        places += [hi * (half // 128)]
        places += [held[n][1] if n < len(held) else 0 for n in range(outer)] + [place for _, place in spread[0]]
        ids = jnp.stack([jnp.asarray(place, jnp.int32) for place in places])
        blocks = [
            (held_at + n, [(piece, part_at + k) for k, (piece, _) in enumerate(pieces)])
            for n, pieces in enumerate(spread)
        ]
        mine, theirs = gated_scores(
            ids, chunk_list, own, (blocks, far_lines, far_columns), parts, half_readout
        )
        own_total = own_total if mine is None else own_total + mine.reshape(-1)
        other_total = other_total if theirs is None else other_total + theirs.reshape(-1)
        return [value for value in (mine, theirs) if value is not None]

    for j in range(end):
        block = bring(j)
        if len(held) < outer:
            recent = spread[-1][-1][0]
            gather_next()
            block = after(block, held[-1][0], recent)
        elif j:
            block = after(block, *barrier)
        far.append([block] + [along(block, step) for step in range(1, lo_size)])
        begin, size = chunks[j]
        sources = []
        for n, kept_block in enumerate(near):
            if half % 128 == 0:
                sources += [(value, begin, pop_size, k * size, size, n) for k, value in enumerate(kept_block)]
            else:
                sources.append((kept_block, 2 * begin, None, 0, 2 * size, n))
        sources += [(value, 0, None, 0, 2 * size, lo_size + n) for n, value in enumerate(far[j])]
        chunk_list.append((begin, size, sources))
        parts = [(True, t, t + 1, j, j + 1) for t in range(members)]
        for n in range(min(j, outer)):
            parts += [(False, n, n + 1, i, i + 1) for i in range(done[n], j + 1)]
            done[n] = j + 1
        barrier = score(parts)
    while len(held) < outer:
        gather_next()
    score([(False, n, n + 1, i, i + 1) for n in range(outer) for i in range(done[n], end)])

    scores = own_total + across(other_total)
    scores = scores + sum(inner_permute(scores, lambda c, s=s: (c + s) % inner) for s in range(1, inner))
    scores = scores + sum(outer_permute(scores, lambda c, s=s: (c + s) % outer) for s in range(1, outer))

    return scores.reshape(members, tok_count), directions[0], directions[1]


def solution(mesh):
    placed = (
        P("pop", None, None),
        P("pop", "shard"),
        P("pop", "shard"),
        P("pop", None, None),
        P("pop", None, None),
        P("pop", None, "shard"),
        P("pop", None, "shard"),
        P("pop"),
        P("shard"),
    )
    return jax.shard_map(
        functools.partial(body, mesh.shape["pop"], mesh.shape["shard"]),
        mesh=mesh,
        in_specs=placed,
        out_specs=(P("pop", None), P("pop", "shard"), P("pop", "shard")),
        check_vma=False,
    )
```

time: 263 us -> 185 us (0.70)
  Pallas kernels: 0 us -> 77.6 us
  waiting for transfers between devices: 116 us -> 45.1 us
  matrix products: 73.8 us -> 8.4 us
  blocking collectives: 56.9 us -> 0 us
  starting transfers between devices: 0.08 us -> 28 us
  local copies, waits for them, and re-layouts: 0.96 us -> 15.2 us
  between operations: 14.9 us -> 0.93 us
  other arithmetic: 0.01 us -> 9 us
    all_gather x2 -> x0, waiting for transfers between devices: 115 us -> none  [the longest x1 75.1 us: body(): base_up = add_rows(lax.all_gather(w_up, 'pop', axis=0, tiled=True))]
    pallas_call x0 -> x22, Pallas kernels: none -> 77.6 us  [the longest x5 66.5 us: gated_scores(): pl.pallas_call(kernel, out_shape=shapes, in_specs=specs, out_specs=[pl.Bl...]
    dot_general x9 -> x2, matrix products: 73.8 us -> 8.4 us  [direction(): lax.dot_general(left, right, (((0,), (0,)), ((), ())), preferred_element_...]
    ppermute x0 -> x27, waiting for transfers between devices: none -> 45.1 us  [the longest x8 23.9 us: outer_permute(): lax.ppermute(value, 'shard', [(s, z * inner + y) for s, z, y in pairs if...]
    ppermute x0 -> x27, starting transfers between devices: none -> 28 us  [the longest x8 15.2 us: outer_permute(): lax.ppermute(value, 'shard', [(s, z * inner + y) for s, z, y in pairs if...]
    all_gather x4 -> x0, blocking collectives: 26.7 us -> none  [the longest x1 7.63 us: body(): lax.all_gather(a_gate, 'pop', axis=0, tiled=True)]
    psum x1 -> x0, blocking collectives: 21.9 us -> none  [body(): scores = lax.psum(partial_value, 'shard')]
    unnamed x1 -> x0, blocking collectives: 8.31 us -> none
  transfers between devices with their start and end apart: 2 -> 27, of which waited for: 2 -> 12; matrix products, arithmetic and copies ran while one was open for 18% -> 15% of each run, Pallas kernels for 0% -> 36%
where the time goes in v2:
time: 185 us; the launch traced here: 184 us
  Pallas kernels  77.6 us (42%)
  waiting for transfers between devices  45.1 us (24%)
  starting transfers between devices  28 us (15%)
  local copies, waits for them, and re-layouts  15.2 us (8%)
  other arithmetic  9 us (5%)
  matrix products  8.4 us (5%)
    pallas_call x5, Pallas kernels, gated_scores(): pl.pallas_call(kernel, out_shape=shapes, in_specs=specs, out_specs=[pl.Bl...  66.5 us
    ppermute x8, waiting for transfers between devices, outer_permute(): lax.ppermute(value, 'shard', [(s, z * inner + y) for s, z, y in pairs if...  23.9 us
    ppermute x8, starting transfers between devices, outer_permute(): lax.ppermute(value, 'shard', [(s, z * inner + y) for s, z, y in pairs if...  15.2 us
    ppermute x7, waiting for transfers between devices, across(): return lax.ppermute(value, 'pop', across_pairs)  13.6 us
    dot_general x2, matrix products, direction(): lax.dot_general(left, right, (((0,), (0,)), ((), ())), preferred_element_...  8.4 us
    ppermute x7, starting transfers between devices, across(): return lax.ppermute(value, 'pop', across_pairs)  7.36 us
    pallas_call x1, Pallas kernels, own_factors(): pl.pallas_call(kernel, out_shape=[jax.ShapeDtypeStruct((lines, hidden + b...  6.24 us
    ppermute x5, starting transfers between devices, inner_permute(): lax.ppermute(value, 'shard', [(s, z * inner + y) for s, z, y in pairs if...  4.56 us
  transfers between devices with their start and end apart: 27, of which 12 were waited for; matrix products, arithmetic and copies ran while one was open for 15% of the time, Pallas kernels for 36%

profile of v2, /device:TPU:0, one launch (start us, length us, event | category | flops | bytes accessed | tf_op | source)
XLA Modules:
  0.0 184.4 jit_solution(17572727667230415058)
XLA Ops:
  1.2 2.2 %dynamic_slice.27.waited_ref = bf16[240,2048]{1,0:T(8,128)(2,1)} dynamic-slice(bf16[960,4096]{1,0:T(8,128)(2,1)} %bitcast.33, s32[]{:T(128)S(6)} %select_n.137, s32[]{:T(128)S(6)} %select_n.138), dynamic_slice_sizes={240,2048} | dynamic-slice | bytes 1966084 | tf_op jit(solution)/shard_map/dynamic_slice | solution.py:417
  3.5 2.9 %collective-permute-start.3 = (bf16[240,2048]{1,0:T(8,128)(2,1)}, bf16[240,2048]{1,0:T(8,128)(2,1)}, u32[]{:S(2)}, u32[]{:S(2)}) collective-permute-start(bf16[240,2048]{1,0:T(8,128)(2,1)} %dynamic_slice.27.waited_ref), channel_id=1, source_target_pairs={{0,16},{8,24},{16,0},{24,8},{1,17},{9,25},{17,1},{25,9},{2,18},{10... | collective-permute-start | bytes 2949128 | tf_op jit(solution)/shard_map/ppermute | solution.py:401
  6.4 0.7 broadcast_in_dim.22
  7.2 1.3 constant_dynamic-slice_fusion.1
  9.2 6.2 %shard_map.112 = (bf16[16,5408]{1,0:T(8,128)(2,1)}, bf16[2,48,480]{2,1,0:T(8,128)(2,1)}, bf16[48,1792]{1,0:T(8,128)(2,1)}) custom-call(s32[1]{0:T(128)} %bitcast.10.start_ref, bf16[2,480,4096]{2,1,0:T(8,128)(2,1)} %refs_14_.1, bf16[2,4,4096]{2,1,0:T(4,128)(2,1)} %ag.1, bf16[2,4,4096]{2,1,0:T(4,128)(2,1)} %au.1, bf16[2,4,1792]{2,1,0:T(4,128)(2,1)} %gc.1, ...), custom_call_target="tpu_custom_call" | custom-call | flops 1 | bytes 1 | tf_op jit(solution)/shard_map/pallas_call | solution.py:291
  15.5 3.2 %shard_map.113 = (bf16[1024,512]{1,0:T(8,128)(2,1)}, bf16[1024,512]{1,0:T(8,128)(2,1)}, bf16[1024,512]{1,0:T(8,128)(2,1)}, bf16[1024,256]{1,0:T(8,128)(2,1)}) custom-call(s32[1]{0:T(128)} %bitcast.9.shift_ref, bf16[1024,1792]{1,0:T(8,128)(2,1)} %refs_2_.9, bf16[1024,1792]{1,0:T(8,128)(2,1)} %refs_3_.9, bf16[16,5408]{1,0:T(8,128)(2,1)} %get-tuple-element.18.waited_ref), custom_call_target="tpu_custom_call" | custom-call | flops 1 | bytes 1 | tf_op jit(solution)/shard_map/pallas_call | solution.py:360
  18.7 0.9 maximum_bitcast_fusion.1
  19.6 1.6 slice_bitcast_fusion.1
  21.8 7.4 %collective-permute-done.3.refs_0_ = bf16[240,2048]{1,0:T(8,128)(2,1)} collective-permute-done((bf16[240,2048]{1,0:T(8,128)(2,1)}, bf16[240,2048]{1,0:T(8,128)(2,1)}, u32[]{:S(2)}, u32[]{:S(2)}) %collective-permute-start.3) | collective-permute-done | bytes 983072 | tf_op jit(solution)/shard_map/ppermute | solution.py:401
  29.3 3.2 %collective-permute-done.5.refs_0_ = bf16[16,5408]{1,0:T(8,128)(2,1)} collective-permute-done((bf16[16,5408]{1,0:T(8,128)(2,1)}, bf16[16,5408]{1,0:T(8,128)(2,1)}, u32[]{:S(2)}, u32[]{:S(2)}) %collective-permute-start.5) | collective-permute-done | bytes 173088 | tf_op jit(solution)/shard_map/ppermute | solution.py:401
  32.5 0.8 slice_bitcast_fusion.2
  33.3 0.9 slice_bitcast_fusion
  34.2 0.8 fusion.21
  35.0 1.0 maximum_bitcast_fusion
  36.1 1.8 collective-permute-start.2
  37.9 1.6 collective-permute-start.4
  39.5 1.5 collective-permute-start.7
  41.0 1.6 collective-permute-start.10
  43.7 4.2 %fusion.4.refs_1_ = f32[1024,1792]{1,0:T(8,128)} fusion(bf16[96,1792]{1,0:T(8,128)(2,1)S(1)} %bitcast.34, bf16[32,1024]{1,0:T(8,128)(2,1)S(1)} %get-tuple-element.44, bf16[32,1024]{1,0:T(8,128)(2,1)S(1)} %get-tuple-element.43, bf16[32,1024]{1,0:T(8,128)(2,1)S(1)} %get-tuple-element.42), kind=kOutput, calls=%fused_computation.9 | convolution fusion | flops 352911360 | bytes 7880704 | tf_op jit(solution)/shard_map/dot_general | solution.py:492
  47.9 4.2 %fusion.10.refs_2_ = f32[1024,1792]{1,0:T(8,128)} fusion(bf16[96,1792]{1,0:T(8,128)(2,1)S(1)} %bitcast.35, bf16[32,1024]{1,0:T(8,128)(2,1)S(1)} %get-tuple-element.41, bf16[32,1024]{1,0:T(8,128)(2,1)S(1)} %get-tuple-element.40, bf16[32,1024]{1,0:T(8,128)(2,1)S(1)} %get-tuple-element.39), kind=kOutput, calls=%fused_computation.15 | convolution fusion | flops 352911360 | bytes 7880704 | tf_op jit(solution)/shard_map/dot_general | solution.py:492
  52.1 9.9 %collective-permute-done.4.refs_0_ = bf16[240,2048]{1,0:T(8,128)(2,1)} collective-permute-done((bf16[240,2048]{1,0:T(8,128)(2,1)}, bf16[240,2048]{1,0:T(8,128)(2,1)}, u32[]{:S(2)}, u32[]{:S(2)}) %collective-permute-start.4) | collective-permute-done | bytes 983072 | tf_op jit(solution)/shard_map/ppermute | solution.py:409
  62.1 1.3 collective-permute-done.7.refs_2_.refs_16_.refs_18_.refs_20_
  63.4 4.5 %collective-permute-start.11 = (bf16[240,2048]{1,0:T(8,128)(2,1)}, bf16[240,2048]{1,0:T(8,128)(2,1)}, u32[]{:S(2)}, u32[]{:S(2)}) collective-permute-start(bf16[240,2048]{1,0:T(8,128)(2,1)} %shard_map.120), channel_id=1, source_target_pairs={{0,2},{1,3},{2,0},{3,1},{4,6},{5,7},{6,4},{7,5},{8,10},{9,11},{10,... | collective-permute-start | bytes 2949128 | tf_op jit(solution)/shard_map/ppermute | solution.py:409
  68.9 1.6 collective-permute-start.15
  70.6 0.8 dynamic_slice.24
  72.6 10.1 %shard_map.118.refs_1_ = f32[2,480]{1,0:T(2,128)} custom-call(s32[11]{0:T(128)} %stack.55.refs_0_, f32[1,896]{1,0:T(1,128)} %broadcast_in_dim.19.refs_1_, bf16[1024,1792]{1,0:T(8,128)(2,1)} %refs_2_.9, bf16[1024,1792]{1,0:T(8,128)(2,1)} %refs_3_.9, bf16[1024,1792]{1,0:T(8,128)(2,1)} %collective-permute-done.refs_5_.refs_4_, ...), custom_call_target="tpu_custom_call" | custom-call | flops 1 | bytes 1 | tf_op jit(solution)/shard_map/pallas_call | solution.py:231
  82.6 6.5 %collective-permute-done.11.refs_0_ = bf16[240,2048]{1,0:T(8,128)(2,1)} collective-permute-done((bf16[240,2048]{1,0:T(8,128)(2,1)}, bf16[240,2048]{1,0:T(8,128)(2,1)}, u32[]{:S(2)}, u32[]{:S(2)}) %collective-permute-start.11) | collective-permute-done | bytes 983072 | tf_op jit(solution)/shard_map/ppermute | solution.py:409
  89.2 2.3 %broadcast_select_fusion.1.refs_1_.refs_23_ = bf16[240,2048]{1,0:T(8,128)(2,1)} fusion(bf16[240,2048]{1,0:T(8,128)(2,1)} %shard_map.121, bf16[240,2048]{1,0:T(8,128)(2,1)} %shard_map.120, pred[]{:T(512)S(6)} %or.3), kind=kLoop, calls=%fused_computation.1 | loop fusion | flops 491520 | bytes 2949121 | tf_op jit(solution)/shard_map/jit(_where)/select_n | solution.py:64
  92.0 1.8 collective-permute-start.16
  93.8 0.9 collective-permute-start.14
  94.8 1.5 collective-permute-start.17
  96.3 0.8 slice.71
  98.3 1.7 shard_map.123
  100.1 12.7 %shard_map.124 = (f32[2,480]{1,0:T(2,128)}, f32[4,240]{1,0:T(4,128)}) custom-call(s32[11]{0:T(128)} %stack.132.refs_0_, f32[1,896]{1,0:T(1,128)} %broadcast_in_dim.19.refs_1_, bf16[1024,1792]{1,0:T(8,128)(2,1)} %refs_2_.9, bf16[1024,1792]{1,0:T(8,128)(2,1)} %refs_3_.9, bf16[1024,1792]{1,0:T(8,128)(2,1)} %collective-permute-done.refs_5_.refs_4_, ...), custom_call_target="tpu_custom_call" | custom-call | flops 1 | bytes 1 | tf_op jit(solution)/shard_map/pallas_call | solution.py:231
  112.8 3.7 %collective-permute-done.16.refs_0_ = bf16[240,2048]{1,0:T(8,128)(2,1)} collective-permute-done((bf16[240,2048]{1,0:T(8,128)(2,1)}, bf16[240,2048]{1,0:T(8,128)(2,1)}, u32[]{:S(2)}, u32[]{:S(2)}) %collective-permute-start.16) | collective-permute-done | bytes 983072 | tf_op jit(solution)/shard_map/ppermute | solution.py:409
  116.5 2.3 %broadcast_select_fusion.refs_1_.refs_16_ = bf16[240,2048]{1,0:T(8,128)(2,1)} fusion(bf16[240,2048]{1,0:T(8,128)(2,1)} %shard_map.127, bf16[240,2048]{1,0:T(8,128)(2,1)} %shard_map.126, pred[]{:T(512)S(6)} %or.3), kind=kLoop, calls=%fused_computation | loop fusion | flops 491520 | bytes 2949121 | tf_op jit(solution)/shard_map/jit(_where)/select_n | solution.py:67
  120.7 1.2 collective-permute-done.18.refs_11_
  121.9 15.8 %shard_map.129 = (f32[2,480]{1,0:T(2,128)}, f32[4,240]{1,0:T(4,128)}) custom-call(s32[11]{0:T(128)} %stack.134.refs_0_, f32[1,896]{1,0:T(1,128)} %broadcast_in_dim.19.refs_1_, bf16[1024,1792]{1,0:T(8,128)(2,1)} %refs_2_.9, bf16[1024,1792]{1,0:T(8,128)(2,1)} %refs_3_.9, bf16[1024,1792]{1,0:T(8,128)(2,1)} %collective-permute-done.refs_5_.refs_4_, ...), custom_call_target="tpu_custom_call" | custom-call | flops 1 | bytes 1 | tf_op jit(solution)/shard_map/pallas_call | solution.py:231
  137.9 2.1 %collective-permute-done.20.refs_13_ = bf16[1024,256]{1,0:T(8,128)(2,1)} collective-permute-done((bf16[1024,256]{1,0:T(8,128)(2,1)}, bf16[1024,256]{1,0:T(8,128)(2,1)}, u32[]{:S(2)}, u32[]{:S(2)}) %collective-permute-start.20) | collective-permute-done | bytes 524320 | tf_op jit(solution)/shard_map/ppermute | solution.py:405
  140.0 17.3 %shard_map.132 = (f32[2,480]{1,0:T(2,128)}, f32[4,240]{1,0:T(4,128)}) custom-call(s32[11]{0:T(128)} %stack.134.refs_0_, f32[1,896]{1,0:T(1,128)} %broadcast_in_dim.19.refs_1_, bf16[1024,1792]{1,0:T(8,128)(2,1)} %refs_2_.9, bf16[1024,1792]{1,0:T(8,128)(2,1)} %refs_3_.9, bf16[1024,1792]{1,0:T(8,128)(2,1)} %collective-permute-done.refs_5_.refs_4_, ...), custom_call_target="tpu_custom_call" | custom-call | flops 1 | bytes 1 | tf_op jit(solution)/shard_map/pallas_call | solution.py:231
  157.3 10.6 %shard_map.133 = f32[4,240]{1,0:T(4,128)} custom-call(s32[11]{0:T(128)} %stack.134.refs_0_, f32[1,896]{1,0:T(1,128)} %broadcast_in_dim.19.refs_1_, bf16[1024,1792]{1,0:T(8,128)(2,1)} %refs_2_.9, bf16[1024,1792]{1,0:T(8,128)(2,1)} %refs_3_.9, bf16[1024,1792]{1,0:T(8,128)(2,1)} %collective-permute-done.refs_5_.refs_4_, ...), custom_call_target="tpu_custom_call" | custom-call | flops 1 | bytes 1 | tf_op jit(solution)/shard_map/pallas_call | solution.py:231
  167.9 0.7 add_add_fusion.1
  169.3 0.7 add_add_fusion.2
  170.1 2.3 %collective-permute-done.22 = f32[960]{0:T(1024)S(1)} collective-permute-done((f32[960]{0:T(1024)S(1)}, f32[960]{0:T(1024)S(1)}, u32[]{:S(2)}, u32[]{:S(2)}) %collective-permute-start.22) | collective-permute-done | bytes 3872 | tf_op jit(solution)/shard_map/ppermute | solution.py:401
  172.8 3.1 %collective-permute-done.23 = f32[960]{0:T(1024)S(1)} collective-permute-done((f32[960]{0:T(1024)S(1)}, f32[960]{0:T(1024)S(1)}, u32[]{:S(2)}, u32[]{:S(2)}) %collective-permute-start.23) | collective-permute-done | bytes 3872 | tf_op jit(solution)/shard_map/ppermute | solution.py:413
  175.9 2.3 %collective-permute-start.26 = (f32[960]{0:T(1024)S(1)}, f32[960]{0:T(1024)S(1)}, u32[]{:S(2)}, u32[]{:S(2)}) collective-permute-start(f32[960]{0:T(1024)S(1)} %add.184), channel_id=1, source_target_pairs={{0,6},{1,7},{2,0},{3,1},{4,2},{5,3},{6,4},{7,5},{8,14},{9,15},{10,... | collective-permute-start | bytes 11528 | tf_op jit(solution)/shard_map/ppermute | solution.py:409
  178.3 1.7 collective-permute-start.25
  180.0 3.6 %collective-permute-done.24 = f32[960]{0:T(1024)S(1)} collective-permute-done((f32[960]{0:T(1024)S(1)}, f32[960]{0:T(1024)S(1)}, u32[]{:S(2)}, u32[]{:S(2)}) %collective-permute-start.24) | collective-permute-done | bytes 3872 | tf_op jit(solution)/shard_map/ppermute | solution.py:409
  (77 shorter events, 11.2 us)
Async XLA Ops:
  0.6 28.6 %collective-permute-start = (bf16[1024,1792]{1,0:T(8,128)(2,1)}, bf16[1024,1792]{1,0:T(8,128)(2,1)}, u32[]{:S(2)}, u32[]{:S(2)}) collective-permute-start(bf16[1024,1792]{1,0:T(8,128)(2,1)} %refs_2_.9), channel_id=1, source_target_pairs={{0,8},{8,0},{16,24},{24,16},{1,9},{9,1},{17,25},{25,17},{2,10},{10... | collective-permute-start | bytes 11010056 | tf_op jit(solution)/shard_map/ppermute | solution.py:405
  1.1 28.1 %collective-permute-start.1 = (bf16[1024,1792]{1,0:T(8,128)(2,1)}, bf16[1024,1792]{1,0:T(8,128)(2,1)}, u32[]{:S(2)}, u32[]{:S(2)}) collective-permute-start(bf16[1024,1792]{1,0:T(8,128)(2,1)} %refs_3_.9), channel_id=1, source_target_pairs={{0,8},{8,0},{16,24},{24,16},{1,9},{9,1},{17,25},{25,17},{2,10},{10... | collective-permute-start | bytes 11010056 | tf_op jit(solution)/shard_map/ppermute | solution.py:405
  3.5 25.8 %collective-permute-start.3 = (bf16[240,2048]{1,0:T(8,128)(2,1)}, bf16[240,2048]{1,0:T(8,128)(2,1)}, u32[]{:S(2)}, u32[]{:S(2)}) collective-permute-start(bf16[240,2048]{1,0:T(8,128)(2,1)} %dynamic_slice.27.waited_ref), channel_id=1, source_target_pairs={{0,16},{8,24},{16,0},{24,8},{1,17},{9,25},{17,1},{25,9},{2,18},{10... | collective-permute-start | bytes 2949128 | tf_op jit(solution)/shard_map/ppermute | solution.py:401
  15.5 17.0 %collective-permute-start.5 = (bf16[16,5408]{1,0:T(8,128)(2,1)}, bf16[16,5408]{1,0:T(8,128)(2,1)}, u32[]{:S(2)}, u32[]{:S(2)}) collective-permute-start(bf16[16,5408]{1,0:T(8,128)(2,1)} %get-tuple-element.18.waited_ref), channel_id=1, source_target_pairs={{0,16},{8,24},{16,0},{24,8},{1,17},{9,25},{17,1},{25,9},{2,18},{10... | collective-permute-start | bytes 519176 | tf_op jit(solution)/shard_map/ppermute | solution.py:401
  36.0 6.6 %collective-permute-start.6 = (bf16[2,16,2944]{2,1,0:T(8,128)(2,1)S(1)}, bf16[2,16,2944]{2,1,0:T(8,128)(2,1)S(1)}, u32[]{:S(2)}, u32[]{:S(2)}) collective-permute-start(bf16[2,16,2944]{2,1,0:T(8,128)(2,1)S(1)} %get-tuple-element.38), channel_id=1, source_target_pairs={{0,8},{8,0},{16,24},{24,16},{1,9},{9,1},{17,25},{25,17},{2,10},{10... | collective-permute-start | bytes 565256 | tf_op jit(solution)/shard_map/ppermute | solution.py:405
  36.1 26.0 %collective-permute-start.2 = (bf16[1024,512]{1,0:T(8,128)(2,1)}, bf16[1024,512]{1,0:T(8,128)(2,1)}, u32[]{:S(2)}, u32[]{:S(2)}) collective-permute-start(bf16[1024,512]{1,0:T(8,128)(2,1)} %get-tuple-element.19.refs_1_), channel_id=1, source_target_pairs={{0,16},{8,24},{16,0},{24,8},{1,17},{9,25},{17,1},{25,9},{2,18},{10... | collective-permute-start | bytes 3145736 | tf_op jit(solution)/shard_map/ppermute | solution.py:401
  37.9 24.1 %collective-permute-start.4 = (bf16[240,2048]{1,0:T(8,128)(2,1)}, bf16[240,2048]{1,0:T(8,128)(2,1)}, u32[]{:S(2)}, u32[]{:S(2)}) collective-permute-start(bf16[240,2048]{1,0:T(8,128)(2,1)} %shard_map.114.refs_1_.refs_15_.refs_17_.refs_19_), channel_id=1, source_target_pairs={{0,2},{1,3},{2,0},{3,1},{4,6},{5,7},{6,4},{7,5},{8,10},{9,11},{10,... | collective-permute-start | bytes 2949128 | tf_op jit(solution)/shard_map/ppermute | solution.py:409
  39.5 23.9 %collective-permute-start.7 = (bf16[240,2048]{1,0:T(8,128)(2,1)}, bf16[240,2048]{1,0:T(8,128)(2,1)}, u32[]{:S(2)}, u32[]{:S(2)}) collective-permute-start(bf16[240,2048]{1,0:T(8,128)(2,1)} %shard_map.114.refs_1_.refs_15_.refs_17_.refs_19_), channel_id=1, source_target_pairs={{0,1},{1,0},{2,3},{3,2},{4,5},{5,4},{6,7},{7,6},{8,9},{9,8},{10,11... | collective-permute-start | bytes 2949128 | tf_op jit(solution)/shard_map/ppermute | solution.py:413
  41.0 22.3 %collective-permute-start.10 = (bf16[240,2048]{1,0:T(8,128)(2,1)}, bf16[240,2048]{1,0:T(8,128)(2,1)}, u32[]{:S(2)}, u32[]{:S(2)}) collective-permute-start(bf16[240,2048]{1,0:T(8,128)(2,1)} %shard_map.114.refs_1_.refs_15_.refs_17_.refs_19_), channel_id=1, source_target_pairs={{2,4},{3,5},{4,2},{5,3},{10,12},{11,13},{12,10},{13,11},{18,20},{1... | collective-permute-start | bytes 2949128 | tf_op jit(solution)/shard_map/ppermute | solution.py:409
  42.8 5.1 %copy-start = (bf16[4,2,2,4,2944]{4,3,2,1,0:T(4,128)(2,1)}, bf16[4,2,2,4,2944]{4,3,2,1,0:T(4,128)(2,1)S(1)}, u32[]{:S(2)}) copy-start(bf16[4,2,2,4,2944]{4,3,2,1,0:T(4,128)(2,1)S(1)} %reshape.47.refs_1_) | copy-start | bytes 1130500
  63.4 9.2 %collective-permute-start.8 = (bf16[1024,512]{1,0:T(8,128)(2,1)}, bf16[1024,512]{1,0:T(8,128)(2,1)}, u32[]{:S(2)}, u32[]{:S(2)}) collective-permute-start(bf16[1024,512]{1,0:T(8,128)(2,1)} %shard_map.117.refs_6_.refs_1_), channel_id=1, source_target_pairs={{0,8},{8,0},{16,24},{24,16},{1,9},{9,1},{17,25},{25,17},{2,10},{10... | collective-permute-start | bytes 3145736 | tf_op jit(solution)/shard_map/ppermute | solution.py:405
  63.4 25.8 %collective-permute-start.11 = (bf16[240,2048]{1,0:T(8,128)(2,1)}, bf16[240,2048]{1,0:T(8,128)(2,1)}, u32[]{:S(2)}, u32[]{:S(2)}) collective-permute-start(bf16[240,2048]{1,0:T(8,128)(2,1)} %shard_map.120), channel_id=1, source_target_pairs={{0,2},{1,3},{2,0},{3,1},{4,6},{5,7},{6,4},{7,5},{8,10},{9,11},{10,... | collective-permute-start | bytes 2949128 | tf_op jit(solution)/shard_map/ppermute | solution.py:409
  67.9 24.1 %collective-permute-start.9 = (bf16[1024,512]{1,0:T(8,128)(2,1)}, bf16[1024,512]{1,0:T(8,128)(2,1)}, u32[]{:S(2)}, u32[]{:S(2)}) collective-permute-start(bf16[1024,512]{1,0:T(8,128)(2,1)} %shard_map.119), channel_id=1, source_target_pairs={{0,16},{8,24},{16,0},{24,8},{1,17},{9,25},{17,1},{25,9},{2,18},{10... | collective-permute-start | bytes 3145736 | tf_op jit(solution)/shard_map/ppermute | solution.py:401
  68.4 23.6 %collective-permute-start.12 = (bf16[240,2048]{1,0:T(8,128)(2,1)}, bf16[240,2048]{1,0:T(8,128)(2,1)}, u32[]{:S(2)}, u32[]{:S(2)}) collective-permute-start(bf16[240,2048]{1,0:T(8,128)(2,1)} %shard_map.116.refs_1_.refs_19_.refs_21_), channel_id=1, source_target_pairs={{0,1},{1,0},{2,3},{3,2},{4,5},{5,4},{6,7},{7,6},{8,9},{9,8},{10,11... | collective-permute-start | bytes 2949128 | tf_op jit(solution)/shard_map/ppermute | solution.py:413
  68.9 23.1 %collective-permute-start.15 = (bf16[240,2048]{1,0:T(8,128)(2,1)}, bf16[240,2048]{1,0:T(8,128)(2,1)}, u32[]{:S(2)}, u32[]{:S(2)}) collective-permute-start(bf16[240,2048]{1,0:T(8,128)(2,1)} %shard_map.116.refs_1_.refs_19_.refs_21_), channel_id=1, source_target_pairs={{2,4},{3,5},{4,2},{5,3},{10,12},{11,13},{12,10},{13,11},{18,20},{1... | collective-permute-start | bytes 2949128 | tf_op jit(solution)/shard_map/ppermute | solution.py:409
  92.0 8.0 %collective-permute-start.13 = (bf16[1024,512]{1,0:T(8,128)(2,1)}, bf16[1024,512]{1,0:T(8,128)(2,1)}, u32[]{:S(2)}, u32[]{:S(2)}) collective-permute-start(bf16[1024,512]{1,0:T(8,128)(2,1)} %shard_map.122.refs_8_.refs_1_), channel_id=1, source_target_pairs={{0,8},{8,0},{16,24},{24,16},{1,9},{9,1},{17,25},{25,17},{2,10},{10... | collective-permute-start | bytes 3145736 | tf_op jit(solution)/shard_map/ppermute | solution.py:405
  92.0 24.5 %collective-permute-start.16 = (bf16[240,2048]{1,0:T(8,128)(2,1)}, bf16[240,2048]{1,0:T(8,128)(2,1)}, u32[]{:S(2)}, u32[]{:S(2)}) collective-permute-start(bf16[240,2048]{1,0:T(8,128)(2,1)} %shard_map.126), channel_id=1, source_target_pairs={{0,2},{1,3},{2,0},{3,1},{4,6},{5,7},{6,4},{7,5},{8,10},{9,11},{10,... | collective-permute-start | bytes 2949128 | tf_op jit(solution)/shard_map/ppermute | solution.py:409
  93.8 25.0 %collective-permute-start.14 = (bf16[1024,512]{1,0:T(8,128)(2,1)}, bf16[1024,512]{1,0:T(8,128)(2,1)}, u32[]{:S(2)}, u32[]{:S(2)}) collective-permute-start(bf16[1024,512]{1,0:T(8,128)(2,1)} %shard_map.125), channel_id=1, source_target_pairs={{0,16},{8,24},{16,0},{24,8},{1,17},{9,25},{17,1},{25,9},{2,18},{10... | collective-permute-start | bytes 3145736 | tf_op jit(solution)/shard_map/ppermute | solution.py:401
  94.8 24.0 %collective-permute-start.17 = (bf16[240,2048]{1,0:T(8,128)(2,1)}, bf16[240,2048]{1,0:T(8,128)(2,1)}, u32[]{:S(2)}, u32[]{:S(2)}) collective-permute-start(bf16[240,2048]{1,0:T(8,128)(2,1)} %broadcast_select_fusion.1.refs_1_.refs_23_), channel_id=1, source_target_pairs={{0,1},{1,0},{2,3},{3,2},{4,5},{5,4},{6,7},{7,6},{8,9},{9,8},{10,11... | collective-permute-start | bytes 2949128 | tf_op jit(solution)/shard_map/ppermute | solution.py:413
  118.8 3.0 %collective-permute-start.18 = (bf16[1024,512]{1,0:T(8,128)(2,1)}, bf16[1024,512]{1,0:T(8,128)(2,1)}, u32[]{:S(2)}, u32[]{:S(2)}) collective-permute-start(bf16[1024,512]{1,0:T(8,128)(2,1)} %shard_map.128.refs_10_), channel_id=1, source_target_pairs={{0,8},{8,0},{16,24},{24,16},{1,9},{9,1},{17,25},{25,17},{2,10},{10... | collective-permute-start | bytes 3145736 | tf_op jit(solution)/shard_map/ppermute | solution.py:405
  118.9 18.8 %collective-permute-start.19 = (bf16[1024,256]{1,0:T(8,128)(2,1)}, bf16[1024,256]{1,0:T(8,128)(2,1)}, u32[]{:S(2)}, u32[]{:S(2)}) collective-permute-start(bf16[1024,256]{1,0:T(8,128)(2,1)} %shard_map.130), channel_id=1, source_target_pairs={{0,16},{8,24},{16,0},{24,8},{1,17},{9,25},{17,1},{25,9},{2,18},{10... | collective-permute-start | bytes 1572872 | tf_op jit(solution)/shard_map/ppermute | solution.py:401
  119.5 37.8 %collective-permute-start.21 = (bf16[240,2048]{1,0:T(8,128)(2,1)}, bf16[240,2048]{1,0:T(8,128)(2,1)}, u32[]{:S(2)}, u32[]{:S(2)}) collective-permute-start(bf16[240,2048]{1,0:T(8,128)(2,1)} %broadcast_select_fusion.refs_1_.refs_16_), channel_id=1, source_target_pairs={{0,1},{1,0},{2,3},{3,2},{4,5},{5,4},{6,7},{7,6},{8,9},{9,8},{10,11... | collective-permute-start | bytes 2949128 | tf_op jit(solution)/shard_map/ppermute | solution.py:413
  137.7 2.3 %collective-permute-start.20 = (bf16[1024,256]{1,0:T(8,128)(2,1)}, bf16[1024,256]{1,0:T(8,128)(2,1)}, u32[]{:S(2)}, u32[]{:S(2)}) collective-permute-start(bf16[1024,256]{1,0:T(8,128)(2,1)} %shard_map.131.refs_12_), channel_id=1, source_target_pairs={{0,8},{8,0},{16,24},{24,16},{1,9},{9,1},{17,25},{25,17},{2,10},{10... | collective-permute-start | bytes 1572872 | tf_op jit(solution)/shard_map/ppermute | solution.py:405
  168.7 3.6 %collective-permute-start.22 = (f32[960]{0:T(1024)S(1)}, f32[960]{0:T(1024)S(1)}, u32[]{:S(2)}, u32[]{:S(2)}) collective-permute-start(f32[960]{0:T(1024)S(1)} %add.182), channel_id=1, source_target_pairs={{0,16},{8,24},{16,0},{24,8},{1,17},{9,25},{17,1},{25,9},{2,18},{10... | collective-permute-start | bytes 11528 | tf_op jit(solution)/shard_map/ppermute | solution.py:401
  172.3 3.6 %collective-permute-start.23 = (f32[960]{0:T(1024)S(1)}, f32[960]{0:T(1024)S(1)}, u32[]{:S(2)}, u32[]{:S(2)}) collective-permute-start(f32[960]{0:T(1024)S(1)} %add.183), channel_id=1, source_target_pairs={{0,1},{1,0},{2,3},{3,2},{4,5},{5,4},{6,7},{7,6},{8,9},{9,8},{10,11... | collective-permute-start | bytes 11528 | tf_op jit(solution)/shard_map/ppermute | solution.py:413
  175.9 4.1 %collective-permute-start.26 = (f32[960]{0:T(1024)S(1)}, f32[960]{0:T(1024)S(1)}, u32[]{:S(2)}, u32[]{:S(2)}) collective-permute-start(f32[960]{0:T(1024)S(1)} %add.184), channel_id=1, source_target_pairs={{0,6},{1,7},{2,0},{3,1},{4,2},{5,3},{6,4},{7,5},{8,14},{9,15},{10,... | collective-permute-start | bytes 11528 | tf_op jit(solution)/shard_map/ppermute | solution.py:409
  178.3 5.4 %collective-permute-start.24 = (f32[960]{0:T(1024)S(1)}, f32[960]{0:T(1024)S(1)}, u32[]{:S(2)}, u32[]{:S(2)}) collective-permute-start(f32[960]{0:T(1024)S(1)} %add.184), channel_id=1, source_target_pairs={{0,2},{1,3},{2,4},{3,5},{4,6},{5,7},{6,0},{7,1},{8,10},{9,11},{10,... | collective-permute-start | bytes 11528 | tf_op jit(solution)/shard_map/ppermute | solution.py:409
  178.3 5.4 %collective-permute-start.25 = (f32[960]{0:T(1024)S(1)}, f32[960]{0:T(1024)S(1)}, u32[]{:S(2)}, u32[]{:S(2)}) collective-permute-start(f32[960]{0:T(1024)S(1)} %add.184), channel_id=1, source_target_pairs={{0,4},{1,5},{2,6},{3,7},{4,0},{5,1},{6,2},{7,3},{8,12},{9,13},{10,... | collective-permute-start | bytes 11528 | tf_op jit(solution)/shard_map/ppermute | solution.py:409

commit v3 on v2

v3 whole, which is shorter than its diff:
```python
import functools
import math

import jax
import jax.numpy as jnp
from jax import lax
from jax.experimental import pallas as pl
from jax.experimental.pallas import tpu as pltpu
from jax.sharding import PartitionSpec as P

F32 = jnp.float32
BF16 = jnp.bfloat16
MIB = 1024 * 1024
VMEM_BYTES = 64 * MIB
SMALL = pl.CostEstimate(flops=1, bytes_accessed=1, transcendentals=0)


def split3(value):
    top = lax.reduce_precision(value, 8, 7)
    rest = value - top
    middle = lax.reduce_precision(rest, 8, 7)
    return [term.astype(BF16) for term in (top, middle, rest - middle)]


def column_chunks(width):
    return [[(begin, min(256, width - begin))] for begin in range(0, width, 256)]


def line_sizes(total):
    outer = 4 if total % 4 == 0 else 1
    return outer, total // outer


def swap_pairs(total, partner):
    return [(index, partner(index)) for index in range(total)]


def line_steps(own, size, coord, permute):
    if size != 4:
        for step in range(1, size):
            block = permute(own, lambda c, step=step: (c + step) % size)
            hold = yield
            yield hold(block)
        return
    even = lambda c: c ^ 1
    odd = lambda c: 3 - c if c in (1, 2) else None
    edge = jnp.logical_or(coord == 0, coord == 3)
    first, across = permute(own, even), permute(own, odd)
    hold = yield
    first, across = hold(first), hold(across)
    yield first
    ahead, over = permute(across, even), permute(first, odd)
    hold = yield
    ahead, over = hold(ahead), hold(over)
    yield jnp.where(edge, ahead, across)
    ahead = permute(over, even)
    hold = yield
    yield jnp.where(edge, hold(ahead), over)


def line_places(size, coord):
    if size != 4:
        return [coord] + [(coord + size - step) % size for step in range(1, size)]
    return [coord] + [
        jnp.where(coord == 0, a, jnp.where(coord == 1, b, jnp.where(coord == 2, c, d)))
        for a, b, c, d in ((1, 0, 3, 2), (2, 2, 1, 1), (3, 3, 0, 0))
    ]


def line_gather(own, size, coord, permute):
    found, steps = [own], line_steps(own, size, coord, permute)
    for _ in range(size - 1):
        next(steps)
        found.append(steps.send(lambda value: value))
    return found


def after(value, *others):
    anywhere = pl.BlockSpec(memory_space=pltpu.HBM)
    return pl.pallas_call(
        lambda *refs: None,
        out_shape=jax.ShapeDtypeStruct(value.shape, value.dtype),
        in_specs=[anywhere] * (1 + len(others)),
        out_specs=anywhere,
        input_output_aliases={0: 0},
        compiler_params=pltpu.CompilerParams(vmem_limit_bytes=VMEM_BYTES),
        cost_estimate=SMALL,
    )(value, *others)


def gated_scores(ids, chunks, own, blocks, parts, readout):
    arrays, specs, scratch, shapes, copies = [], [], [], [], 0

    def add(array, space):
        for index, seen in enumerate(arrays):
            if seen is array:
                return index
        arrays.append(array)
        specs.append(pl.BlockSpec(memory_space=space))
        return len(arrays) - 1

    add(ids, pltpu.SMEM)
    small = []

    def add_small(array):
        small.append((add(array, pltpu.HBM), len(scratch)))
        scratch.append(pltpu.VMEM(array.shape, array.dtype))
        return small[-1][1]

    lines = own[1].shape[1]
    tiles, tile, width = own[0].shape
    place_count, block_rows = blocks[1].shape[0], blocks[1].shape[2]
    chunk_rows = chunks[0][2][0][0].shape[0]
    used_chunks = sorted({j for part in parts for j in range(part[3], part[4])})
    used_tiles = sorted({t for part in parts if part[0] for t in range(part[1], part[2])})
    used_blocks = sorted({t for part in parts if not part[0] for t in range(part[1], part[2])})
    lane_at, total_lanes = {}, 0
    for j in used_chunks:
        lane_at[j] = total_lanes
        total_lanes += 2 * chunks[j][1]
    weights_at = len(scratch)
    scratch.append(pltpu.VMEM((width, total_lanes), BF16))
    chunk_refs = {j: [(add(source[0], pltpu.HBM),) + source[1:] for source in chunks[j][2]] for j in used_chunks}
    copies += sum(len(refs) for refs in chunk_refs.values())
    own_at = block_at = own_out = block_out = None
    if used_tiles:
        own_at, own_out = len(scratch), len(shapes)
        scratch.append(pltpu.VMEM((len(used_tiles) * tile, width), BF16))
        shapes.append(jax.ShapeDtypeStruct((tiles, tile), F32))
        own_ref, own_lines, own_cols = add(own[0], pltpu.HBM), add_small(own[1]), add_small(own[2])
        copies += len(used_tiles)
    if used_blocks:
        block_at, block_out = len(scratch), len(shapes)
        scratch.append(pltpu.VMEM((len(used_blocks) * block_rows, width), BF16))
        shapes.append(jax.ShapeDtypeStruct((place_count, block_rows), F32))
        far_lines, far_cols = add_small(blocks[1]), add_small(blocks[2])
        block_refs = {n: [(add(array, pltpu.HBM), place) for array, place in blocks[0][n][1]] for n in used_blocks}
        copies += sum(len(refs) for refs in block_refs.values())
    readout_at = add_small(readout)
    scratch.append(pltpu.SemaphoreType.DMA((copies + len(small),)))
    inputs, outputs = len(arrays), len(shapes)

    def kernel(*refs):
        ids_ref = refs[0]
        outs, held = refs[inputs : inputs + outputs], refs[inputs + outputs :]
        sems, readout_ref = held[-1], held[readout_at]
        pending, count = {}, 0

        def fetch(key):
            nonlocal count
            if key in pending:
                return
            pairs = []
            if key[0] == "chunk":
                for index, lane, shift, to, lanes, place in chunk_refs[key[1]]:
                    first = pl.multiple_of(ids_ref[place] * chunk_rows, chunk_rows)
                    if shift is not None:
                        lane = pl.multiple_of(ids_ref[shift] * 128 + lane, 128)
                    source = refs[index].at[:, pl.ds(lane, lanes)]
                    target = held[weights_at].at[pl.ds(first, chunk_rows), pl.ds(lane_at[key[1]] + to, lanes)]
                    pairs.append((source, target))
            elif key[0] == "own":
                rows = pl.ds(used_tiles.index(key[1]) * tile, tile)
                pairs.append((refs[own_ref].at[key[1]], held[own_at].at[rows, :]))
            else:
                for index, place in block_refs[key[1]]:
                    lanes = refs[index].shape[1]
                    first = pl.multiple_of(ids_ref[place] * lanes, lanes)
                    rows = pl.ds(used_blocks.index(key[1]) * block_rows, block_rows)
                    target = held[block_at].at[rows, pl.ds(first, lanes)]
                    pairs.append((refs[index], target))
            pending[key] = []
            for source, target in pairs:
                pending[key].append(pltpu.make_async_copy(source, target, sems.at[count]))
                pending[key][-1].start()
                count += 1

        def keys(part):
            mine, begin, end, first, last = part
            found = [("chunk", j) for j in range(first, last)]
            return found + [("own" if mine else "block", n) for n in range(begin, end)]

        first_copies = []
        for n, (index, place) in enumerate(small):
            first_copies.append(pltpu.make_async_copy(refs[index], held[place], sems.at[copies + n]))
            first_copies[-1].start()
        for part in parts[:2]:
            for key in keys(part):
                fetch(key)
        for out in outs:
            out[...] = jnp.zeros(out.shape, F32)
        for copy in first_copies:
            copy.wait()
        for number, part in enumerate(parts):
            for key in keys(part):
                for copy in pending[key]:
                    copy.wait()
                pending[key] = []
            if number + 2 < len(parts):
                for key in keys(parts[number + 2]):
                    fetch(key)
            mine, begin, end, first, last = part
            if mine:
                held_rows, height, at = held[own_at], tile, used_tiles.index(begin)
            else:
                held_rows, height, at = held[block_at], block_rows, used_blocks.index(begin)
            lanes = slice(lane_at[first], lane_at[last - 1] + 2 * chunks[last - 1][1])
            top, tall = at * height, (end - begin) * height
            piece = 240 if lanes.stop - lanes.start <= 256 and tall % 240 == 0 else tall
            pieces = [
                jnp.dot(held_rows[top + k : top + k + piece, :], held[weights_at][:, lanes], preferred_element_type=F32)
                for k in range(0, tall, piece)
            ]
            total = jnp.concatenate(pieces, 0) if len(pieces) > 1 else pieces[0]
            for t in range(end - begin):
                if mine:
                    row, noise, columns = begin + t, held[own_lines].at[begin + t], held[own_cols]
                else:
                    row = ids_ref[blocks[0][begin + t][0]]
                    noise, columns = held[far_lines].at[row], held[far_cols]
                begin_lane = 2 * chunks[first][0]
                part_total = total[t * height : (t + 1) * height, :] + lax.dot_general(
                    noise[...],
                    columns[:, begin_lane : begin_lane + lanes.stop - lanes.start],
                    (((0,), (0,)), ((), ())),
                    preferred_element_type=F32,
                )
                line = 0.0
                for j in range(first, last):
                    start, size, _ = chunks[j]
                    lane = lane_at[j] - lane_at[first]
                    gate, up = part_total[:, lane : lane + size], part_total[:, lane + size : lane + 2 * size]
                    value = gate / (1.0 + jnp.exp(-gate)) * up * readout_ref[:, start : start + size]
                    if size % 128 == 0:
                        value = sum(value[:, k : k + 128] for k in range(0, size, 128))
                    line += jnp.sum(value.T, axis=0, keepdims=True)
                out = outs[own_out if mine else block_out]
                out[pl.ds(row, 1), :] += line

    results = pl.pallas_call(
        kernel,
        out_shape=shapes,
        in_specs=specs,
        out_specs=[pl.BlockSpec(memory_space=pltpu.VMEM)] * len(shapes),
        scratch_shapes=scratch,
        compiler_params=pltpu.CompilerParams(vmem_limit_bytes=VMEM_BYTES),
        cost_estimate=SMALL,
    )(*arrays)
    return (results[own_out] if used_tiles else None), (results[block_out] if used_blocks else None)


def noise_columns(gate, up, cuts):
    blocks = []
    for begin, size in cuts:
        blocks += [gate[:, begin : begin + size], up[:, begin : begin + size]]
    value = jnp.concatenate(blocks, 1).astype(BF16)
    return jnp.concatenate([value] * 3, 0)


def lanes_from(ref, start, width, row=None):
    if start is None:
        return ref[...] if row is None else ref[row]
    lanes = pl.ds(pl.multiple_of(start * 128, 128), width)
    return ref[:, lanes] if row is None else ref[row, :, lanes]


def own_factors(starts, tokens, a_gate, a_up, gate_cols, up_cols, gate_half, up_half, fitness, scale, cuts, waited):
    members, tok_count, width = tokens.shape
    rank, hidden = a_gate.shape[1], gate_cols.shape[2]
    half, lines, block_half = hidden // 2, 2 * members * rank, width // 2
    halves = [] if gate_half is None else [gate_half, up_half]

    def kernel(starts_ref, tok_ref, ag, au, gc, uc, fit, waited_ref, *refs):
        bundle, rows, cols = refs[-3:]

        def both(gate, up):
            found = []
            for m in range(members):
                found += [gate(m).astype(F32), up(m).astype(F32)]
            return jnp.concatenate(found, 0).astype(BF16)

        bundle[:, :hidden] = both(lambda m: gc[m], lambda m: uc[m])
        bundle[:, hidden : hidden + block_half] = both(
            lambda m: lanes_from(ag, starts_ref[0], block_half, m), lambda m: lanes_from(au, starts_ref[0], block_half, m)
        )
        marks = [jnp.broadcast_to(fit[:, m : m + 1].astype(F32), (2 * rank, 128)) for m in range(members)]
        bundle[:, hidden + block_half : hidden + block_half + 128] = jnp.concatenate(marks, 0).astype(BF16)
        terms = []
        for m in range(members):
            factors = jnp.concatenate([ag[m].astype(F32), au[m].astype(F32)], 0).astype(BF16)
            value = scale * lax.dot_general(
                factors, tok_ref[m], (((1,), (1,)), ((), ())), preferred_element_type=F32
            )
            found = []
            for _ in range(3):
                found.append(value.astype(BF16).astype(F32))
                value = value - found[-1]
            terms.append(found)
            zero = jnp.zeros_like(value)
            lines_of = [found[n] if other == m else zero for n in range(3) for other in range(members)]
            rows[m] = jnp.concatenate(lines_of, 0).astype(BF16)
        ends = jnp.concatenate([jnp.concatenate(found, 1) for found in terms], 0)
        bundle[:, hidden + block_half + 128 :] = ends.astype(BF16)
        gates, ups = [], []
        for m in range(members):
            if halves:
                gate, up = refs[0][m].astype(F32), refs[1][m].astype(F32)
            else:
                gate = lanes_from(gc, starts_ref[1], half, m).astype(F32)
                up = lanes_from(uc, starts_ref[1], half, m).astype(F32)
            gates += [gate, jnp.zeros_like(gate)]
            ups += [jnp.zeros_like(up), up]
        cols[...] = noise_columns(jnp.concatenate(gates, 0), jnp.concatenate(ups, 0), cuts)

    vmem = pl.BlockSpec(memory_space=pltpu.VMEM)
    return pl.pallas_call(
        kernel,
        out_shape=[
            jax.ShapeDtypeStruct((lines, hidden + block_half + 128 + 3 * tok_count), BF16),
            jax.ShapeDtypeStruct((members, 3 * lines, tok_count), BF16),
            jax.ShapeDtypeStruct((3 * lines, 2 * half), BF16),
        ],
        in_specs=[pl.BlockSpec(memory_space=pltpu.SMEM)]
        + [vmem] * 6
        + [pl.BlockSpec(memory_space=pltpu.HBM)]
        + [vmem] * len(halves),
        out_specs=[vmem] * 3,
        compiler_params=pltpu.CompilerParams(vmem_limit_bytes=VMEM_BYTES),
        cost_estimate=SMALL,
    )(starts, tokens, a_gate, a_up, gate_cols, up_cols, fitness, waited, *halves)


def other_factors(starts, bundle, own_bundle, a_gate, a_up, half_cols, hidden, tok_count, tile, block_rows, cuts):
    members, rank, width = a_gate.shape
    lines, half, block_half = 2 * members * rank, hidden // 2, width // 2
    first = hidden + block_half + 128
    count, targets = members * tok_count // tile, (starts.shape[0] - 1) // 2
    halves = [] if half_cols is None else [half_cols]

    def kernel(starts_ref, bundle_ref, own_ref, ag, au, *refs):
        rows, cols = refs[len(halves) : len(halves) + 2]
        for block in range(count):
            m, at = block * tile // tok_count, block * tile % tok_count
            found = []
            for n in range(3):
                lane = first + n * tok_count + at
                value = bundle_ref[:, lane : lane + tile].astype(F32)
                line = lax.broadcasted_iota(jnp.int32, value.shape, 0)
                found.append(jnp.where(line // (2 * rank) == m, value, 0.0))
            rows[block] = jnp.concatenate(found, 0).astype(BF16)
        value = (refs[0][...] if halves else lanes_from(bundle_ref, starts_ref[0], half)).astype(F32)
        is_gate = lax.broadcasted_iota(jnp.int32, value.shape, 0) % (2 * rank) < rank
        cols[...] = noise_columns(jnp.where(is_gate, value, 0.0), jnp.where(is_gate, 0.0, value), cuts)
        for target in range(targets):
            pack = refs[len(halves) + 2 + target]
            pack[:lines, :hidden] = own_ref[:, :hidden]
            pack[lines:, :hidden] = bundle_ref[:, :hidden]
            mine = []
            for m in range(members):
                for source in (ag, au):
                    mine.append(lanes_from(source, starts_ref[2 + 2 * target], block_rows, m).astype(F32))
            pack[:lines, hidden : hidden + block_rows] = jnp.concatenate(mine, 0).astype(BF16)
            pack[lines:, hidden : hidden + block_rows] = lanes_from(
                bundle_ref, hidden // 128 + starts_ref[1 + 2 * target], block_rows
            )
            pack[:lines, hidden + block_rows :] = own_ref[:, first - 128 : first]
            pack[lines:, hidden + block_rows :] = bundle_ref[:, first - 128 : first]

    vmem = pl.BlockSpec(memory_space=pltpu.VMEM)
    return pl.pallas_call(
        kernel,
        out_shape=[
            jax.ShapeDtypeStruct((count, 3 * lines, tile), BF16),
            jax.ShapeDtypeStruct((3 * lines, 2 * half), BF16),
        ]
        + [jax.ShapeDtypeStruct((2 * lines, hidden + block_rows + 128), BF16)] * targets,
        in_specs=[pl.BlockSpec(memory_space=pltpu.SMEM)] + [vmem] * (4 + len(halves)),
        out_specs=[vmem] * (2 + targets),
        compiler_params=pltpu.CompilerParams(vmem_limit_bytes=VMEM_BYTES),
        cost_estimate=SMALL,
    )(starts, bundle, own_bundle, a_gate, a_up, *halves)


def update_directions(packs, hidden, block_rows, rank, total):
    step = 128

    def kernel(*refs):
        gate_out, up_out = refs[len(packs) :]
        lanes = pl.ds(pl.multiple_of(hidden + pl.program_id(0) * step, 128), step)
        left, right = [], []
        for ref in refs[: len(packs)]:
            value = ref[:, lanes].astype(F32) * (ref[:, hidden + block_rows : hidden + block_rows + 1].astype(F32) / math.sqrt(total))
            for _ in range(3):
                term = value.astype(BF16)
                left.append(term)
                value = value - term.astype(F32)
            right += [ref[:, :hidden]] * 3
        left, right = jnp.concatenate(left, 0), jnp.concatenate(right, 0)
        is_gate = lax.broadcasted_iota(jnp.int32, left.shape, 0) % (2 * rank) < rank
        for out, mask in ((gate_out, is_gate), (up_out, jnp.logical_not(is_gate))):
            part = jnp.where(mask, left.astype(F32), 0.0).astype(BF16)
            out[...] = lax.dot_general(part, right, (((0,), (0,)), ((), ())), preferred_element_type=F32)

    return pl.pallas_call(
        kernel,
        grid=(block_rows // step,),
        out_shape=[jax.ShapeDtypeStruct((block_rows, hidden), F32)] * 2,
        in_specs=[pl.BlockSpec(pack.shape, lambda i: (0, 0)) for pack in packs],
        out_specs=[pl.BlockSpec((step, hidden), lambda i: (i, 0))] * 2,
        compiler_params=pltpu.CompilerParams(vmem_limit_bytes=VMEM_BYTES),
        cost_estimate=SMALL,
    )(*packs)


def cut_blocks(gate, up, shift, groups, waited):
    rows = gate.shape[0]
    widths = [2 * sum(size for _, size in group) for group in groups]
    count = sum(2 * len(group) for group in groups)

    def kernel(shift_ref, gate_ref, up_ref, waited_ref, *refs):
        blocks, held, sems = refs[: len(groups)], refs[len(groups) : -1], refs[-1]
        first, used = [], 0
        for n, group in enumerate(groups):
            first.append([])
            for begin, size in group:
                lanes = pl.ds(pl.multiple_of(shift_ref[0] * 128 + begin, 128), size)
                to = 2 * (begin - group[0][0])
                for kind, source in enumerate((gate_ref, up_ref)):
                    target = held[n].at[:, pl.ds(to + kind * size, size)]
                    first[n].append(pltpu.make_async_copy(source.at[:, lanes], target, sems.at[used]))
                    first[n][-1].start()
                    used += 1
        second = []
        for n in range(len(groups)):
            for copy in first[n]:
                copy.wait()
            second.append(pltpu.make_async_copy(held[n], blocks[n], sems.at[used + n]))
            second[n].start()
        for copy in second:
            copy.wait()

    anywhere = pl.BlockSpec(memory_space=pltpu.HBM)
    return pl.pallas_call(
        kernel,
        out_shape=[jax.ShapeDtypeStruct((rows, width), gate.dtype) for width in widths],
        in_specs=[pl.BlockSpec(memory_space=pltpu.SMEM), anywhere, anywhere, anywhere],
        out_specs=[anywhere] * len(groups),
        scratch_shapes=[pltpu.VMEM((rows, width), gate.dtype) for width in widths]
        + [pltpu.SemaphoreType.DMA((count + len(groups),))],
        compiler_params=pltpu.CompilerParams(vmem_limit_bytes=VMEM_BYTES),
        cost_estimate=SMALL,
    )(shift, gate, up, waited)


def body(
    pop_size,
    shard_size,
    tokens,
    gate_weight_matrix,
    w_up,
    a_gate,
    a_up,
    gate_hidden_factors,
    up_hidden_factors,
    fitness,
    readout,
):
    members, tok_count, model_width = tokens.shape
    rank = a_gate.shape[1]
    rows = members * tok_count
    block_rows, hidden = gate_weight_matrix.shape
    half = hidden // 2
    lo_size = pop_size // 2
    outer, inner = line_sizes(shard_size)
    noise_scale = 0.25 / math.sqrt(model_width * rank)
    pop, shard = lax.axis_index("pop"), lax.axis_index("shard")
    hi, lo = pop // lo_size, pop % lo_size
    flat = tokens.reshape(rows, model_width)
    crossing = column_chunks(half)
    chunks = [chunk for group in crossing for chunk in group]

    across_pairs = [(p, (p + lo_size) % pop_size) for p in range(pop_size)]

    def across(value):
        return lax.ppermute(value, "pop", across_pairs)

    def along(value, step):
        pairs = [(p, p // lo_size * lo_size + (p + step) % lo_size) for p in range(pop_size)]
        return lax.ppermute(value, "pop", pairs)

    def outer_permute(value, target):
        pairs = [(s, target(s // inner), s % inner) for s in range(shard_size)]
        return lax.ppermute(value, "shard", [(s, z * inner + y) for s, z, y in pairs if z is not None])

    def inner_permute(value, target):
        pairs = [(s, s // inner, target(s % inner)) for s in range(shard_size)]
        return lax.ppermute(value, "shard", [(s, z * inner + y) for s, z, y in pairs if y is not None])

    z, y = shard // inner, shard % inner
    size_z, size_y = rows // outer, model_width // inner
    block = lax.dynamic_slice(flat, (z * size_z, y * size_y), (size_z, size_y))
    sent = across(block)

    block_half = model_width // 2
    by_start = half % 128 == 0

    def in_half(value):
        return None if by_start else lax.dynamic_slice_in_dim(value, hi * half, half, value.ndim - 1)

    def numbers(*values):
        return jnp.stack([jnp.asarray(value, jnp.int32) for value in values])

    half_start = hi * (half // 128)
    bundle, own_lines, own_columns = own_factors(
        numbers((1 - hi) * (block_half // 128), half_start),
        tokens,
        a_gate,
        a_up,
        gate_hidden_factors,
        up_hidden_factors,
        in_half(gate_hidden_factors),
        in_half(up_hidden_factors),
        fitness[None, :],
        noise_scale,
        chunks,
        block,
    )
    other_bundle = across(bundle)

    def pick(which):
        if half % 128 == 0:
            return cut_blocks(gate_weight_matrix, w_up, numbers(which * (half // 128)), crossing, bundle)
        gate = lax.dynamic_slice_in_dim(gate_weight_matrix, which * half, half, 1)
        up = lax.dynamic_slice_in_dim(w_up, which * half, half, 1)
        return [
            jnp.concatenate([part[:, begin : begin + size] for begin, size in group for part in (gate, up)], 1)
            for group in crossing
        ]

    cut = pick(1 - hi)
    if half % 128 == 0:
        near = [(along(gate_weight_matrix, step), along(w_up, step)) for step in range(1, lo_size)]
        near = [(gate_weight_matrix, w_up)] + near
    else:
        kept = jnp.concatenate(pick(hi), 1)
        near = [kept] + [along(kept, step) for step in range(1, lo_size)]

    sent = after(sent, *cut, *jax.tree.leaves(near[1:]))

    starts = [half_start]
    for step in range(lo_size):
        target = (lo + step) % lo_size
        starts += [target * (block_rows // 128), hi * (block_half // 128) + target * (block_rows // 128)]
    far_lines, far_columns, *packs = other_factors(
        numbers(*starts),
        other_bundle,
        bundle,
        a_gate,
        a_up,
        in_half(other_bundle[:, :hidden]),
        hidden,
        tok_count,
        size_z,
        block_rows,
        chunks,
    )
    packs = packs[:1] + [along(pack, step) for step, pack in enumerate(packs[1:], 1)]
    directions = update_directions(packs, hidden, block_rows, rank, pop_size * members * rank)

    half_readout = lax.dynamic_slice_in_dim(readout, hi * half, half, 0)[None, :]
    own = (tokens, own_lines, own_columns)
    held_at = pop_size + 1
    part_at = held_at + outer
    ids = numbers(
        *[hi * lo_size + (lo + lo_size - step) % lo_size for step in range(lo_size)],
        *[(1 - hi) * lo_size + (lo + lo_size - step) % lo_size for step in range(lo_size)],
        half_start,
        *line_places(outer, z),
        *line_places(inner, y),
    )

    steps = line_steps(sent, outer, z, outer_permute)
    held, spread, far, chunk_list = [sent], [line_gather(sent, inner, y, inner_permute)], [], []
    end = len(chunks)
    passed = [across(after(cut[0], other_bundle))] + [None] * (len(crossing) - 1)
    own_total = other_total = 0.0
    done, barrier = [0] * outer, list(directions)

    def gather_next():
        next(steps)
        held.append(steps.send(lambda value: after(value, *barrier)))
        spread.append(line_gather(held[-1], inner, y, inner_permute))

    def bring(j):
        if passed[j] is None:
            passed[j] = across(after(cut[j], *(far[j - 2] if j > 1 else packs)))
        return passed[j]

    def score(parts):
        nonlocal own_total, other_total
        blocks = [
            (held_at + n, [(piece, part_at + k) for k, piece in enumerate(pieces)])
            for n, pieces in enumerate(spread)
        ]
        mine, theirs = gated_scores(
            ids, chunk_list, own, (blocks, far_lines, far_columns), parts, half_readout
        )
        own_total = own_total if mine is None else own_total + mine.reshape(-1)
        other_total = other_total if theirs is None else other_total + theirs.reshape(-1)
        return [value for value in (mine, theirs) if value is not None]

    for j, group in enumerate(crossing):
        block = bring(j)
        if len(held) < outer:
            recent = spread[-1][-1]
            gather_next()
            block = after(block, held[-1], recent)
        elif j:
            block = after(block, *barrier)
        far.append([block] + [along(block, step) for step in range(1, lo_size)])
        for begin, size in group:
            sources = []
            for n, kept_block in enumerate(near):
                if half % 128 == 0:
                    sources += [(value, begin, pop_size, k * size, size, n) for k, value in enumerate(kept_block)]
                else:
                    sources.append((kept_block, 2 * begin, None, 0, 2 * size, n))
            at = 2 * (begin - group[0][0])
            sources += [(value, at, None, 0, 2 * size, lo_size + n) for n, value in enumerate(far[j])]
            chunk_list.append((begin, size, sources))
        there = len(chunk_list)
        parts = [(True, t, t + 1, i, i + 1) for i in range(there - len(group), there) for t in range(members)]
        if j < len(crossing) - 1:
            ready = min(j + 1, outer - 1)
            old = [n for n in range(ready) if done[n] == there - 1]
            if old:
                parts.append((False, old[0], old[-1] + 1, there - 1, there))
            for n in range(ready):
                parts += [(False, n, n + 1, i, i + 1) for i in range(done[n], there) if n not in old]
                done[n] = there
            barrier = score(parts)
    while len(held) < outer:
        gather_next()
    rest = [(False, n, n + 1, i, i + 1) for n in range(outer) for i in range(done[n], end - 1)]
    score(rest + [(False, 0, outer, end - 1, end)] + parts)

    crossed = across(other_total)
    near_own = [inner_permute(own_total, lambda c, s=s: (c + s) % inner) for s in range(1, inner)]
    near_other = [
        lax.ppermute(
            other_total,
            ("pop", "shard"),
            [
                (p * shard_size + s, (p + lo_size) % pop_size * shard_size + s // inner * inner + (s + step) % inner)
                for p in range(pop_size)
                for s in range(shard_size)
            ],
        )
        for step in range(1, inner)
    ]
    scores = own_total + crossed + sum(near_own) + sum(near_other)
    scores = scores + sum(outer_permute(scores, lambda c, s=s: (c + s) % outer) for s in range(1, outer))
    return scores.reshape(members, tok_count), directions[0], directions[1]


def solution(mesh):
    placed = (
        P("pop", None, None),
        P("pop", "shard"),
        P("pop", "shard"),
        P("pop", None, None),
        P("pop", None, None),
        P("pop", None, "shard"),
        P("pop", None, "shard"),
        P("pop"),
        P("shard"),
    )
    return jax.shard_map(
        functools.partial(body, mesh.shape["pop"], mesh.shape["shard"]),
        mesh=mesh,
        in_specs=placed,
        out_specs=(P("pop", None), P("pop", "shard"), P("pop", "shard")),
        check_vma=False,
    )
```

time: 185 us -> 170 us (0.919)
  local copies, waits for them, and re-layouts: 15.2 us -> 5.7 us
  matrix products: 8.4 us -> 0 us
  starting transfers between devices: 28 us -> 31.5 us
  waiting for transfers between devices: 45.1 us -> 48.3 us
  other arithmetic: 9 us -> 6.58 us
    pallas_call x5 -> x4, Pallas kernels: 66.5 us -> 57.3 us  [gated_scores(): pl.pallas_call(kernel, out_shape=shapes, in_specs=specs, out_specs=[pl.Bl...]
    dot_general x2 -> x0, matrix products: 8.4 us -> none  [direction(): lax.dot_general(left, right, (((0,), (0,)), ((), ())), preferred_element_...]
    pallas_call x1 -> x2, Pallas kernels: 3.19 us -> 11.3 us  [the longest x1 8.05 us: update_directions(): pl.pallas_call(kernel, grid=(block_rows // step,), out_shape=[jax.ShapeDt...]
    another operation x12 -> x2, local copies, waits for them, and re-layouts: 6.05 us -> 1.25 us  [numbers(): return jnp.stack([jnp.asarray(value, jnp.int32) for value in values])]
    ppermute x7, waiting for transfers between devices: 13.6 us -> 17.5 us  [across(): return lax.ppermute(value, 'pop', across_pairs)]
    ppermute x8, waiting for transfers between devices: 23.9 us -> 20 us  [outer_permute(): lax.ppermute(value, 'shard', [(s, z * inner + y) for s, z, y in pairs if...]
    ppermute x5, waiting for transfers between devices: 4.4 us -> 7.6 us  [inner_permute(): lax.ppermute(value, 'shard', [(s, z * inner + y) for s, z, y in pairs if...]
    dynamic_slice x2 -> x0, local copies, waits for them, and re-layouts: 1.95 us -> none  [in_half(): return lax.dynamic_slice_in_dim(value, hi * half, half, value.ndim - 1)]
  transfers between devices with their start and end apart: 27 -> 28, of which waited for: 12 -> 15; matrix products, arithmetic and copies ran while one was open for 15% -> 6% of each run, Pallas kernels for 36% -> 36%
where the time goes in v3:
time: 170 us
  Pallas kernels  76.8 us (45%)
  waiting for transfers between devices  48.3 us (28%)
  starting transfers between devices  31.5 us (19%)
  other arithmetic  6.58 us (4%)
  local copies, waits for them, and re-layouts  5.7 us (3%)
    pallas_call x4, Pallas kernels, gated_scores(): pl.pallas_call(kernel, out_shape=shapes, in_specs=specs, out_specs=[pl.Bl...  57.3 us
    ppermute x8, waiting for transfers between devices, outer_permute(): lax.ppermute(value, 'shard', [(s, z * inner + y) for s, z, y in pairs if...  20 us
    ppermute x7, waiting for transfers between devices, across(): return lax.ppermute(value, 'pop', across_pairs)  17.5 us
    ppermute x8, starting transfers between devices, outer_permute(): lax.ppermute(value, 'shard', [(s, z * inner + y) for s, z, y in pairs if...  16.9 us
    pallas_call x1, Pallas kernels, update_directions(): pl.pallas_call(kernel, grid=(block_rows // step,), out_shape=[jax.ShapeDt...  8.05 us
    ppermute x5, waiting for transfers between devices, inner_permute(): lax.ppermute(value, 'shard', [(s, z * inner + y) for s, z, y in pairs if...  7.6 us
    ppermute x7, starting transfers between devices, across(): return lax.ppermute(value, 'pop', across_pairs)  7.23 us
    pallas_call x1, Pallas kernels, own_factors(): pl.pallas_call(kernel, out_shape=[jax.ShapeDtypeStruct((lines, hidden + b...  6.23 us
  transfers between devices with their start and end apart: 28, of which 15 were waited for; matrix products, arithmetic and copies ran while one was open for 6% of the time, Pallas kernels for 36%

profile of v3, /device:TPU:0, one launch (start us, length us, event | category | flops | bytes accessed | tf_op | source)
XLA Modules:
  0.0 169.7 jit_solution(13337908979520116476)
XLA Ops:
  1.2 2.2 %dynamic_slice.6.waited_ref = bf16[240,2048]{1,0:T(8,128)(2,1)} dynamic-slice(bf16[960,4096]{1,0:T(8,128)(2,1)} %bitcast.19, s32[]{:T(128)S(6)} %select_n.100, s32[]{:T(128)S(6)} %select_n.101), dynamic_slice_sizes={240,2048} | dynamic-slice | bytes 1966084 | tf_op jit(solution)/shard_map/dynamic_slice | solution.py:501
  3.5 2.9 %collective-permute-start.4 = (bf16[240,2048]{1,0:T(8,128)(2,1)}, bf16[240,2048]{1,0:T(8,128)(2,1)}, u32[]{:S(2)}, u32[]{:S(2)}) collective-permute-start(bf16[240,2048]{1,0:T(8,128)(2,1)} %dynamic_slice.6.waited_ref), channel_id=1, source_target_pairs={{0,16},{8,24},{16,0},{24,8},{1,17},{9,25},{17,1},{25,9},{2,18},{10... | collective-permute-start | bytes 2949128 | tf_op jit(solution)/shard_map/ppermute | solution.py:485
  6.4 0.6 pad_add_fusion.starts_ref
  7.0 6.2 %shard_map.112 = (bf16[16,5408]{1,0:T(8,128)(2,1)}, bf16[2,48,480]{2,1,0:T(8,128)(2,1)}, bf16[48,1792]{1,0:T(8,128)(2,1)}) custom-call(s32[2]{0:T(128)} %pad_add_fusion.starts_ref, bf16[2,480,4096]{2,1,0:T(8,128)(2,1)} %refs_13_.1, bf16[2,4,4096]{2,1,0:T(4,128)(2,1)} %ag.3, bf16[2,4,4096]{2,1,0:T(4,128)(2,1)} %au.3, bf16[2,4,1792]{2,1,0:T(4,128)(2,1)} %gc.1, ...), custom_call_target="tpu_custom_call" | custom-call | flops 1 | bytes 1 | tf_op jit(solution)/shard_map/pallas_call | solution.py:316
  13.2 3.3 %shard_map.113 = (bf16[1024,512]{1,0:T(8,128)(2,1)}, bf16[1024,512]{1,0:T(8,128)(2,1)}, bf16[1024,512]{1,0:T(8,128)(2,1)}, bf16[1024,256]{1,0:T(8,128)(2,1)}) custom-call(s32[1]{0:T(128)} %bitcast.11.shift_ref, bf16[1024,1792]{1,0:T(8,128)(2,1)} %refs_1_.7, bf16[1024,1792]{1,0:T(8,128)(2,1)} %refs_2_.7, bf16[16,5408]{1,0:T(8,128)(2,1)} %get-tuple-element.24.waited_ref.own_ref), custom_call_target="tpu_custom_call" | custom-call | flops 1 | bytes 1 | tf_op jit(solution)/shard_map/pallas_call | solution.py:443
  16.5 12.7 %collective-permute-done.4.refs_0_ = bf16[240,2048]{1,0:T(8,128)(2,1)} collective-permute-done((bf16[240,2048]{1,0:T(8,128)(2,1)}, bf16[240,2048]{1,0:T(8,128)(2,1)}, u32[]{:S(2)}, u32[]{:S(2)}) %collective-permute-start.4) | collective-permute-done | bytes 983072 | tf_op jit(solution)/shard_map/ppermute | solution.py:485
  29.3 3.2 %collective-permute-done.2.refs_1_.bundle_ref = bf16[16,5408]{1,0:T(8,128)(2,1)} collective-permute-done((bf16[16,5408]{1,0:T(8,128)(2,1)}, bf16[16,5408]{1,0:T(8,128)(2,1)}, u32[]{:S(2)}, u32[]{:S(2)}) %collective-permute-start.2) | collective-permute-done | bytes 173088 | tf_op jit(solution)/shard_map/ppermute | solution.py:485
  32.5 1.7 %collective-permute-start.3 = (bf16[1024,512]{1,0:T(8,128)(2,1)}, bf16[1024,512]{1,0:T(8,128)(2,1)}, u32[]{:S(2)}, u32[]{:S(2)}) collective-permute-start(bf16[1024,512]{1,0:T(8,128)(2,1)} %shard_map.114), channel_id=1, source_target_pairs={{0,16},{8,24},{16,0},{24,8},{1,17},{9,25},{17,1},{25,9},{2,18},{10... | collective-permute-start | bytes 3145736 | tf_op jit(solution)/shard_map/ppermute | solution.py:485
  34.2 1.6 collective-permute-start.5
  35.8 1.5 collective-permute-start.7
  37.3 1.6 collective-permute-start.10
  38.9 0.6 stack.81.starts_ref
  39.5 2.0 %shard_map.116 = (bf16[4,48,240]{2,1,0:T(8,128)(2,1)}, bf16[48,1792]{1,0:T(8,128)(2,1)}, bf16[32,2944]{1,0:T(8,128)(2,1)}, bf16[32,2944]{1,0:T(8,128)(2,1)}) custom-call(s32[5]{0:T(128)} %stack.81.starts_ref, bf16[16,5408]{1,0:T(8,128)(2,1)} %collective-permute-done.2.refs_1_.bundle_ref, bf16[16,5408]{1,0:T(8,128)(2,1)} %get-tuple-element.24.waited_ref.own_ref, ...), custom_call_target="tpu_custom_call" | custom-call | flops 1 | bytes 1 | tf_op jit(solution)/shard_map/pallas_call | solution.py:370
  41.5 1.8 %collective-permute-done.6.refs_1_.refs_2_ = bf16[32,2944]{1,0:T(8,128)(2,1)} collective-permute-done((bf16[32,2944]{1,0:T(8,128)(2,1)}, bf16[32,2944]{1,0:T(8,128)(2,1)}, u32[]{:S(2)}, u32[]{:S(2)}) %collective-permute-start.6) | collective-permute-done | bytes 188448 | tf_op jit(solution)/shard_map/ppermute | solution.py:489
  43.3 8.0 %shard_map.117 = (f32[1024,1792]{1,0:T(8,128)}, f32[1024,1792]{1,0:T(8,128)}) custom-call(bf16[32,2944]{1,0:T(8,128)(2,1)} %get-tuple-element.29.refs_0_.refs_1_, bf16[32,2944]{1,0:T(8,128)(2,1)} %collective-permute-done.6.refs_1_.refs_2_), custom_call_target="tpu_custom_call" | custom-call | flops 1 | bytes 1 | tf_op jit(solution)/shard_map/pallas_call | solution.py:404
  51.3 5.8 %collective-permute-done.5.refs_0_ = bf16[240,2048]{1,0:T(8,128)(2,1)} collective-permute-done((bf16[240,2048]{1,0:T(8,128)(2,1)}, bf16[240,2048]{1,0:T(8,128)(2,1)}, u32[]{:S(2)}, u32[]{:S(2)}) %collective-permute-start.5) | collective-permute-done | bytes 983072 | tf_op jit(solution)/shard_map/ppermute | solution.py:493
  57.2 1.3 collective-permute-done.7.refs_2_.refs_13_.refs_15_.refs_17_.refs_19_
  58.5 4.5 %collective-permute-start.11 = (bf16[240,2048]{1,0:T(8,128)(2,1)}, bf16[240,2048]{1,0:T(8,128)(2,1)}, u32[]{:S(2)}, u32[]{:S(2)}) collective-permute-start(bf16[240,2048]{1,0:T(8,128)(2,1)} %shard_map.122), channel_id=1, source_target_pairs={{0,2},{1,3},{2,0},{3,1},{4,6},{5,7},{6,4},{7,5},{8,10},{9,11},{10,... | collective-permute-start | bytes 2949128 | tf_op jit(solution)/shard_map/ppermute | solution.py:493
  64.0 1.6 collective-permute-start.15
  65.7 0.8 dynamic_slice.7
  67.0 0.6 stack.73.refs_0_
  67.7 11.4 %shard_map.120 = (f32[2,480]{1,0:T(2,128)}, f32[4,240]{1,0:T(4,128)}) custom-call(s32[11]{0:T(128)} %stack.73.refs_0_, bf16[1024,1792]{1,0:T(8,128)(2,1)} %refs_1_.7, bf16[1024,1792]{1,0:T(8,128)(2,1)} %refs_2_.7, bf16[1024,1792]{1,0:T(8,128)(2,1)} %collective-permute-done.refs_5_.refs_3_, bf16[1024,1792]{1,0:T(8,128)(2,1)} %collective-permute-done.1.refs_6_.refs_4_, ...), custom_call_target="tpu_custom_call" | custom-call | flops 1 | bytes 1 | tf_op jit(solution)/shard_map/pallas_call | solution.py:240
  79.1 3.9 %collective-permute-done.11.refs_0_ = bf16[240,2048]{1,0:T(8,128)(2,1)} collective-permute-done((bf16[240,2048]{1,0:T(8,128)(2,1)}, bf16[240,2048]{1,0:T(8,128)(2,1)}, u32[]{:S(2)}, u32[]{:S(2)}) %collective-permute-start.11) | collective-permute-done | bytes 983072 | tf_op jit(solution)/shard_map/ppermute | solution.py:493
  83.0 2.3 %broadcast_select_fusion.1.refs_1_.refs_20_.refs_22_ = bf16[240,2048]{1,0:T(8,128)(2,1)} fusion(bf16[240,2048]{1,0:T(8,128)(2,1)} %shard_map.123, bf16[240,2048]{1,0:T(8,128)(2,1)} %shard_map.122, pred[]{:T(512)S(6)} %or.3), kind=kLoop, calls=%fused_computation.1 | loop fusion | flops 491520 | bytes 2949121 | tf_op jit(solution)/shard_map/jit(_where)/select_n | solution.py:55
  85.3 0.6 collective-permute-done.9.refs_0_
  85.9 3.0 %collective-permute-start.16 = (bf16[240,2048]{1,0:T(8,128)(2,1)}, bf16[240,2048]{1,0:T(8,128)(2,1)}, u32[]{:S(2)}, u32[]{:S(2)}) collective-permute-start(bf16[240,2048]{1,0:T(8,128)(2,1)} %shard_map.127), channel_id=1, source_target_pairs={{0,2},{1,3},{2,0},{3,1},{4,6},{5,7},{6,4},{7,5},{8,10},{9,11},{10,... | collective-permute-start | bytes 2949128 | tf_op jit(solution)/shard_map/ppermute | solution.py:493
  88.9 0.7 collective-permute-start.14
  90.1 14.0 %shard_map.125 = (f32[2,480]{1,0:T(2,128)}, f32[4,240]{1,0:T(4,128)}) custom-call(s32[11]{0:T(128)} %stack.73.refs_0_, bf16[1024,1792]{1,0:T(8,128)(2,1)} %refs_1_.7, bf16[1024,1792]{1,0:T(8,128)(2,1)} %refs_2_.7, bf16[1024,1792]{1,0:T(8,128)(2,1)} %collective-permute-done.refs_5_.refs_3_, bf16[1024,1792]{1,0:T(8,128)(2,1)} %collective-permute-done.1.refs_6_.refs_4_, ...), custom_call_target="tpu_custom_call" | custom-call | flops 1 | bytes 1 | tf_op jit(solution)/shard_map/pallas_call | solution.py:240
  104.1 6.2 %collective-permute-done.16.refs_0_ = bf16[240,2048]{1,0:T(8,128)(2,1)} collective-permute-done((bf16[240,2048]{1,0:T(8,128)(2,1)}, bf16[240,2048]{1,0:T(8,128)(2,1)}, u32[]{:S(2)}, u32[]{:S(2)}) %collective-permute-start.16) | collective-permute-done | bytes 983072 | tf_op jit(solution)/shard_map/ppermute | solution.py:493
  110.4 2.3 %broadcast_select_fusion.refs_1_.refs_24_ = bf16[240,2048]{1,0:T(8,128)(2,1)} fusion(bf16[240,2048]{1,0:T(8,128)(2,1)} %shard_map.128, bf16[240,2048]{1,0:T(8,128)(2,1)} %shard_map.127, pred[]{:T(512)S(6)} %or.3), kind=kLoop, calls=%fused_computation | loop fusion | flops 491520 | bytes 2949121 | tf_op jit(solution)/shard_map/jit(_where)/select_n | solution.py:58
  112.8 0.6 collective-permute-start.19
  113.4 1.2 collective-permute-start.21
  114.5 1.2 collective-permute-done.18.refs_10_
  115.7 16.8 %shard_map.130 = (f32[2,480]{1,0:T(2,128)}, f32[4,240]{1,0:T(4,128)}) custom-call(s32[11]{0:T(128)} %stack.73.refs_0_, bf16[1024,1792]{1,0:T(8,128)(2,1)} %refs_1_.7, bf16[1024,1792]{1,0:T(8,128)(2,1)} %refs_2_.7, bf16[1024,1792]{1,0:T(8,128)(2,1)} %collective-permute-done.refs_5_.refs_3_, bf16[1024,1792]{1,0:T(8,128)(2,1)} %collective-permute-done.1.refs_6_.refs_4_, ...), custom_call_target="tpu_custom_call" | custom-call | flops 1 | bytes 1 | tf_op jit(solution)/shard_map/pallas_call | solution.py:240
  132.7 4.8 %collective-permute-done.21.refs_25_ = bf16[240,2048]{1,0:T(8,128)(2,1)} collective-permute-done((bf16[240,2048]{1,0:T(8,128)(2,1)}, bf16[240,2048]{1,0:T(8,128)(2,1)}, u32[]{:S(2)}, u32[]{:S(2)}) %collective-permute-start.21) | collective-permute-done | bytes 983072 | tf_op jit(solution)/shard_map/ppermute | solution.py:497
  137.5 15.0 %shard_map.133 = (f32[2,480]{1,0:T(2,128)}, f32[4,240]{1,0:T(4,128)}) custom-call(s32[11]{0:T(128)} %stack.73.refs_0_, bf16[1024,1792]{1,0:T(8,128)(2,1)} %refs_1_.7, bf16[1024,1792]{1,0:T(8,128)(2,1)} %refs_2_.7, bf16[1024,1792]{1,0:T(8,128)(2,1)} %collective-permute-done.refs_5_.refs_3_, bf16[1024,1792]{1,0:T(8,128)(2,1)} %collective-permute-done.1.refs_6_.refs_4_, ...), custom_call_target="tpu_custom_call" | custom-call | flops 1 | bytes 1 | tf_op jit(solution)/shard_map/pallas_call | solution.py:240
  152.6 0.7 add_add_fusion.2
  153.3 1.9 %collective-permute-start.24 = (f32[960]{0:T(1024)S(1)}, f32[960]{0:T(1024)S(1)}, u32[]{:S(2)}, u32[]{:S(2)}) collective-permute-start(f32[960]{0:T(1024)S(1)} %add.134), channel_id=1, source_target_pairs={{0,17},{1,16},{2,19},{3,18},{4,21},{5,20},{6,23},{7,22},{8,25},{9,... | collective-permute-start | bytes 11528 | tf_op jit(solution)/shard_map/ppermute | solution.py:650
  155.2 0.7 collective-permute-start.22
  156.0 0.7 add_add_fusion.3
  156.8 0.9 collective-permute-start.23
  157.9 1.0 collective-permute-done.22
  158.8 1.5 collective-permute-done.23
  160.4 3.2 %collective-permute-start.27 = (f32[960]{0:T(1024)S(1)}, f32[960]{0:T(1024)S(1)}, u32[]{:S(2)}, u32[]{:S(2)}) collective-permute-start(f32[960]{0:T(1024)S(1)} %add_add_fusion.1), channel_id=1, source_target_pairs={{0,6},{1,7},{2,0},{3,1},{4,2},{5,3},{6,4},{7,5},{8,14},{9,15},{10,... | collective-permute-start | bytes 11528 | tf_op jit(solution)/shard_map/ppermute | solution.py:493
  163.6 1.4 collective-permute-start.25
  165.0 3.1 %collective-permute-done.26 = f32[960]{0:T(1024)S(1)} collective-permute-done((f32[960]{0:T(1024)S(1)}, f32[960]{0:T(1024)S(1)}, u32[]{:S(2)}, u32[]{:S(2)}) %collective-permute-start.26) | collective-permute-done | bytes 3872 | tf_op jit(solution)/shard_map/ppermute | solution.py:493
  168.1 0.9 collective-permute-done.25
  169.0 0.7 reshape.27
  (45 shorter events, 3.5 us)
Async XLA Ops:
  0.6 28.6 %collective-permute-start = (bf16[1024,1792]{1,0:T(8,128)(2,1)}, bf16[1024,1792]{1,0:T(8,128)(2,1)}, u32[]{:S(2)}, u32[]{:S(2)}) collective-permute-start(bf16[1024,1792]{1,0:T(8,128)(2,1)} %refs_1_.7), channel_id=1, source_target_pairs={{0,8},{8,0},{16,24},{24,16},{1,9},{9,1},{17,25},{25,17},{2,10},{10... | collective-permute-start | bytes 11010056 | tf_op jit(solution)/shard_map/ppermute | solution.py:489
  1.1 28.1 %collective-permute-start.1 = (bf16[1024,1792]{1,0:T(8,128)(2,1)}, bf16[1024,1792]{1,0:T(8,128)(2,1)}, u32[]{:S(2)}, u32[]{:S(2)}) collective-permute-start(bf16[1024,1792]{1,0:T(8,128)(2,1)} %refs_2_.7), channel_id=1, source_target_pairs={{0,8},{8,0},{16,24},{24,16},{1,9},{9,1},{17,25},{25,17},{2,10},{10... | collective-permute-start | bytes 11010056 | tf_op jit(solution)/shard_map/ppermute | solution.py:489
  3.5 25.8 %collective-permute-start.4 = (bf16[240,2048]{1,0:T(8,128)(2,1)}, bf16[240,2048]{1,0:T(8,128)(2,1)}, u32[]{:S(2)}, u32[]{:S(2)}) collective-permute-start(bf16[240,2048]{1,0:T(8,128)(2,1)} %dynamic_slice.6.waited_ref), channel_id=1, source_target_pairs={{0,16},{8,24},{16,0},{24,8},{1,17},{9,25},{17,1},{25,9},{2,18},{10... | collective-permute-start | bytes 2949128 | tf_op jit(solution)/shard_map/ppermute | solution.py:485
  13.2 19.2 %collective-permute-start.2 = (bf16[16,5408]{1,0:T(8,128)(2,1)}, bf16[16,5408]{1,0:T(8,128)(2,1)}, u32[]{:S(2)}, u32[]{:S(2)}) collective-permute-start(bf16[16,5408]{1,0:T(8,128)(2,1)} %get-tuple-element.24.waited_ref.own_ref), channel_id=1, source_target_pairs={{0,16},{8,24},{16,0},{24,8},{1,17},{9,25},{17,1},{25,9},{2,18},{10... | collective-permute-start | bytes 519176 | tf_op jit(solution)/shard_map/ppermute | solution.py:485
  32.5 26.0 %collective-permute-start.3 = (bf16[1024,512]{1,0:T(8,128)(2,1)}, bf16[1024,512]{1,0:T(8,128)(2,1)}, u32[]{:S(2)}, u32[]{:S(2)}) collective-permute-start(bf16[1024,512]{1,0:T(8,128)(2,1)} %shard_map.114), channel_id=1, source_target_pairs={{0,16},{8,24},{16,0},{24,8},{1,17},{9,25},{17,1},{25,9},{2,18},{10... | collective-permute-start | bytes 3145736 | tf_op jit(solution)/shard_map/ppermute | solution.py:485
  34.2 22.9 %collective-permute-start.5 = (bf16[240,2048]{1,0:T(8,128)(2,1)}, bf16[240,2048]{1,0:T(8,128)(2,1)}, u32[]{:S(2)}, u32[]{:S(2)}) collective-permute-start(bf16[240,2048]{1,0:T(8,128)(2,1)} %shard_map.115.refs_12_.refs_14_.refs_16_.refs_18_), channel_id=1, source_target_pairs={{0,2},{1,3},{2,0},{3,1},{4,6},{5,7},{6,4},{7,5},{8,10},{9,11},{10,... | collective-permute-start | bytes 2949128 | tf_op jit(solution)/shard_map/ppermute | solution.py:493
  35.8 22.7 %collective-permute-start.7 = (bf16[240,2048]{1,0:T(8,128)(2,1)}, bf16[240,2048]{1,0:T(8,128)(2,1)}, u32[]{:S(2)}, u32[]{:S(2)}) collective-permute-start(bf16[240,2048]{1,0:T(8,128)(2,1)} %shard_map.115.refs_12_.refs_14_.refs_16_.refs_18_), channel_id=1, source_target_pairs={{0,1},{1,0},{2,3},{3,2},{4,5},{5,4},{6,7},{7,6},{8,9},{9,8},{10,11... | collective-permute-start | bytes 2949128 | tf_op jit(solution)/shard_map/ppermute | solution.py:497
  37.3 21.1 %collective-permute-start.10 = (bf16[240,2048]{1,0:T(8,128)(2,1)}, bf16[240,2048]{1,0:T(8,128)(2,1)}, u32[]{:S(2)}, u32[]{:S(2)}) collective-permute-start(bf16[240,2048]{1,0:T(8,128)(2,1)} %shard_map.115.refs_12_.refs_14_.refs_16_.refs_18_), channel_id=1, source_target_pairs={{2,4},{3,5},{4,2},{5,3},{10,12},{11,13},{12,10},{13,11},{18,20},{1... | collective-permute-start | bytes 2949128 | tf_op jit(solution)/shard_map/ppermute | solution.py:493
  41.5 1.8 %collective-permute-start.6 = (bf16[32,2944]{1,0:T(8,128)(2,1)}, bf16[32,2944]{1,0:T(8,128)(2,1)}, u32[]{:S(2)}, u32[]{:S(2)}) collective-permute-start(bf16[32,2944]{1,0:T(8,128)(2,1)} %get-tuple-element.30), channel_id=1, source_target_pairs={{0,8},{8,0},{16,24},{24,16},{1,9},{9,1},{17,25},{25,17},{2,10},{10... | collective-permute-start | bytes 565256 | tf_op jit(solution)/shard_map/ppermute | solution.py:489
  58.5 9.2 %collective-permute-start.8 = (bf16[1024,512]{1,0:T(8,128)(2,1)}, bf16[1024,512]{1,0:T(8,128)(2,1)}, u32[]{:S(2)}, u32[]{:S(2)}) collective-permute-start(bf16[1024,512]{1,0:T(8,128)(2,1)} %shard_map.119.refs_5_.refs_1_), channel_id=1, source_target_pairs={{0,8},{8,0},{16,24},{24,16},{1,9},{9,1},{17,25},{25,17},{2,10},{10... | collective-permute-start | bytes 3145736 | tf_op jit(solution)/shard_map/ppermute | solution.py:489
  58.5 24.5 %collective-permute-start.11 = (bf16[240,2048]{1,0:T(8,128)(2,1)}, bf16[240,2048]{1,0:T(8,128)(2,1)}, u32[]{:S(2)}, u32[]{:S(2)}) collective-permute-start(bf16[240,2048]{1,0:T(8,128)(2,1)} %shard_map.122), channel_id=1, source_target_pairs={{0,2},{1,3},{2,0},{3,1},{4,6},{5,7},{6,4},{7,5},{8,10},{9,11},{10,... | collective-permute-start | bytes 2949128 | tf_op jit(solution)/shard_map/ppermute | solution.py:493
  63.0 22.9 %collective-permute-start.9 = (bf16[1024,512]{1,0:T(8,128)(2,1)}, bf16[1024,512]{1,0:T(8,128)(2,1)}, u32[]{:S(2)}, u32[]{:S(2)}) collective-permute-start(bf16[1024,512]{1,0:T(8,128)(2,1)} %shard_map.121), channel_id=1, source_target_pairs={{0,16},{8,24},{16,0},{24,8},{1,17},{9,25},{17,1},{25,9},{2,18},{10... | collective-permute-start | bytes 3145736 | tf_op jit(solution)/shard_map/ppermute | solution.py:485
  63.5 22.3 %collective-permute-start.12 = (bf16[240,2048]{1,0:T(8,128)(2,1)}, bf16[240,2048]{1,0:T(8,128)(2,1)}, u32[]{:S(2)}, u32[]{:S(2)}) collective-permute-start(bf16[240,2048]{1,0:T(8,128)(2,1)} %shard_map.118.refs_1_.refs_16_.refs_18_.refs_20_), channel_id=1, source_target_pairs={{0,1},{1,0},{2,3},{3,2},{4,5},{5,4},{6,7},{7,6},{8,9},{9,8},{10,11... | collective-permute-start | bytes 2949128 | tf_op jit(solution)/shard_map/ppermute | solution.py:497
  64.0 21.8 %collective-permute-start.15 = (bf16[240,2048]{1,0:T(8,128)(2,1)}, bf16[240,2048]{1,0:T(8,128)(2,1)}, u32[]{:S(2)}, u32[]{:S(2)}) collective-permute-start(bf16[240,2048]{1,0:T(8,128)(2,1)} %shard_map.118.refs_1_.refs_16_.refs_18_.refs_20_), channel_id=1, source_target_pairs={{2,4},{3,5},{4,2},{5,3},{10,12},{11,13},{12,10},{13,11},{18,20},{1... | collective-permute-start | bytes 2949128 | tf_op jit(solution)/shard_map/ppermute | solution.py:493
  85.9 4.3 %collective-permute-start.13 = (bf16[1024,512]{1,0:T(8,128)(2,1)}, bf16[1024,512]{1,0:T(8,128)(2,1)}, u32[]{:S(2)}, u32[]{:S(2)}) collective-permute-start(bf16[1024,512]{1,0:T(8,128)(2,1)} %shard_map.124.refs_7_.refs_1_), channel_id=1, source_target_pairs={{0,8},{8,0},{16,24},{24,16},{1,9},{9,1},{17,25},{25,17},{2,10},{10... | collective-permute-start | bytes 3145736 | tf_op jit(solution)/shard_map/ppermute | solution.py:489
  85.9 24.5 %collective-permute-start.16 = (bf16[240,2048]{1,0:T(8,128)(2,1)}, bf16[240,2048]{1,0:T(8,128)(2,1)}, u32[]{:S(2)}, u32[]{:S(2)}) collective-permute-start(bf16[240,2048]{1,0:T(8,128)(2,1)} %shard_map.127), channel_id=1, source_target_pairs={{0,2},{1,3},{2,0},{3,1},{4,6},{5,7},{6,4},{7,5},{8,10},{9,11},{10,... | collective-permute-start | bytes 2949128 | tf_op jit(solution)/shard_map/ppermute | solution.py:493
  88.9 23.8 %collective-permute-start.14 = (bf16[1024,512]{1,0:T(8,128)(2,1)}, bf16[1024,512]{1,0:T(8,128)(2,1)}, u32[]{:S(2)}, u32[]{:S(2)}) collective-permute-start(bf16[1024,512]{1,0:T(8,128)(2,1)} %shard_map.126), channel_id=1, source_target_pairs={{0,16},{8,24},{16,0},{24,8},{1,17},{9,25},{17,1},{25,9},{2,18},{10... | collective-permute-start | bytes 3145736 | tf_op jit(solution)/shard_map/ppermute | solution.py:485
  89.6 23.1 %collective-permute-start.17 = (bf16[240,2048]{1,0:T(8,128)(2,1)}, bf16[240,2048]{1,0:T(8,128)(2,1)}, u32[]{:S(2)}, u32[]{:S(2)}) collective-permute-start(bf16[240,2048]{1,0:T(8,128)(2,1)} %broadcast_select_fusion.1.refs_1_.refs_20_.refs_22_), channel_id=1, source_target_pairs={{0,1},{1,0},{2,3},{3,2},{4,5},{5,4},{6,7},{7,6},{8,9},{9,8},{10,11... | collective-permute-start | bytes 2949128 | tf_op jit(solution)/shard_map/ppermute | solution.py:497
  112.7 3.0 %collective-permute-start.18 = (bf16[1024,512]{1,0:T(8,128)(2,1)}, bf16[1024,512]{1,0:T(8,128)(2,1)}, u32[]{:S(2)}, u32[]{:S(2)}) collective-permute-start(bf16[1024,512]{1,0:T(8,128)(2,1)} %shard_map.129.refs_9_), channel_id=1, source_target_pairs={{0,8},{8,0},{16,24},{24,16},{1,9},{9,1},{17,25},{25,17},{2,10},{10... | collective-permute-start | bytes 3145736 | tf_op jit(solution)/shard_map/ppermute | solution.py:489
  112.8 19.7 %collective-permute-start.19 = (bf16[1024,256]{1,0:T(8,128)(2,1)}, bf16[1024,256]{1,0:T(8,128)(2,1)}, u32[]{:S(2)}, u32[]{:S(2)}) collective-permute-start(bf16[1024,256]{1,0:T(8,128)(2,1)} %shard_map.131), channel_id=1, source_target_pairs={{0,16},{8,24},{16,0},{24,8},{1,17},{9,25},{17,1},{25,9},{2,18},{10... | collective-permute-start | bytes 1572872 | tf_op jit(solution)/shard_map/ppermute | solution.py:485
  113.4 24.1 %collective-permute-start.21 = (bf16[240,2048]{1,0:T(8,128)(2,1)}, bf16[240,2048]{1,0:T(8,128)(2,1)}, u32[]{:S(2)}, u32[]{:S(2)}) collective-permute-start(bf16[240,2048]{1,0:T(8,128)(2,1)} %broadcast_select_fusion.refs_1_.refs_24_), channel_id=1, source_target_pairs={{0,1},{1,0},{2,3},{3,2},{4,5},{5,4},{6,7},{7,6},{8,9},{9,8},{10,11... | collective-permute-start | bytes 2949128 | tf_op jit(solution)/shard_map/ppermute | solution.py:497
  132.5 5.0 %collective-permute-start.20 = (bf16[1024,256]{1,0:T(8,128)(2,1)}, bf16[1024,256]{1,0:T(8,128)(2,1)}, u32[]{:S(2)}, u32[]{:S(2)}) collective-permute-start(bf16[1024,256]{1,0:T(8,128)(2,1)} %shard_map.132.refs_11_), channel_id=1, source_target_pairs={{0,8},{8,0},{16,24},{24,16},{1,9},{9,1},{17,25},{25,17},{2,10},{10... | collective-permute-start | bytes 1572872 | tf_op jit(solution)/shard_map/ppermute | solution.py:489
  153.3 4.5 %collective-permute-start.24 = (f32[960]{0:T(1024)S(1)}, f32[960]{0:T(1024)S(1)}, u32[]{:S(2)}, u32[]{:S(2)}) collective-permute-start(f32[960]{0:T(1024)S(1)} %add.134), channel_id=1, source_target_pairs={{0,17},{1,16},{2,19},{3,18},{4,21},{5,20},{6,23},{7,22},{8,25},{9,... | collective-permute-start | bytes 11528 | tf_op jit(solution)/shard_map/ppermute | solution.py:650
  155.2 3.6 %collective-permute-start.22 = (f32[960]{0:T(1024)S(1)}, f32[960]{0:T(1024)S(1)}, u32[]{:S(2)}, u32[]{:S(2)}) collective-permute-start(f32[960]{0:T(1024)S(1)} %add.134), channel_id=1, source_target_pairs={{0,16},{8,24},{16,0},{24,8},{1,17},{9,25},{17,1},{25,9},{2,18},{10... | collective-permute-start | bytes 11528 | tf_op jit(solution)/shard_map/ppermute | solution.py:485
  156.8 3.6 %collective-permute-start.23 = (f32[960]{0:T(1024)S(1)}, f32[960]{0:T(1024)S(1)}, u32[]{:S(2)}, u32[]{:S(2)}) collective-permute-start(f32[960]{0:T(1024)S(1)} %add.130), channel_id=1, source_target_pairs={{0,1},{1,0},{2,3},{3,2},{4,5},{5,4},{6,7},{7,6},{8,9},{9,8},{10,11... | collective-permute-start | bytes 11528 | tf_op jit(solution)/shard_map/ppermute | solution.py:497
  160.4 4.6 %collective-permute-start.27 = (f32[960]{0:T(1024)S(1)}, f32[960]{0:T(1024)S(1)}, u32[]{:S(2)}, u32[]{:S(2)}) collective-permute-start(f32[960]{0:T(1024)S(1)} %add_add_fusion.1), channel_id=1, source_target_pairs={{0,6},{1,7},{2,0},{3,1},{4,2},{5,3},{6,4},{7,5},{8,14},{9,15},{10,... | collective-permute-start | bytes 11528 | tf_op jit(solution)/shard_map/ppermute | solution.py:493
  163.6 4.5 %collective-permute-start.26 = (f32[960]{0:T(1024)S(1)}, f32[960]{0:T(1024)S(1)}, u32[]{:S(2)}, u32[]{:S(2)}) collective-permute-start(f32[960]{0:T(1024)S(1)} %add_add_fusion.1), channel_id=1, source_target_pairs={{0,4},{1,5},{2,6},{3,7},{4,0},{5,1},{6,2},{7,3},{8,12},{9,13},{10,... | collective-permute-start | bytes 11528 | tf_op jit(solution)/shard_map/ppermute | solution.py:493
  163.6 5.4 %collective-permute-start.25 = (f32[960]{0:T(1024)S(1)}, f32[960]{0:T(1024)S(1)}, u32[]{:S(2)}, u32[]{:S(2)}) collective-permute-start(f32[960]{0:T(1024)S(1)} %add_add_fusion.1), channel_id=1, source_target_pairs={{0,2},{1,3},{2,4},{3,5},{4,6},{5,7},{6,0},{7,1},{8,10},{9,11},{10,... | collective-permute-start | bytes 11528 | tf_op jit(solution)/shard_map/ppermute | solution.py:493

commit v4 on v3

--- a/solution.py
+++ b/solution.py
@@ -23,7 +23,14 @@
 
 
 def column_chunks(width):
-    return [[(begin, min(256, width - begin))] for begin in range(0, width, 256)]
+    groups, begin = [], 0
+    while begin < width:
+        end, group = min(begin + (384 if len(groups) == 1 else 256), width), []
+        while begin < end:
+            group.append((begin, min(256, end - begin)))
+            begin += group[-1][1]
+        groups.append(group)
+    return groups
 
 
 def line_sizes(total):
@@ -88,7 +95,7 @@
     )(value, *others)
 
 
-def gated_scores(ids, chunks, own, blocks, parts, readout):
+def gated_scores(ids, chunks, own, blocks, parts, readout, carried):
     arrays, specs, scratch, shapes, copies = [], [], [], [], 0
 
     def add(array, space):
@@ -126,7 +133,7 @@
     if used_tiles:
         own_at, own_out = len(scratch), len(shapes)
         scratch.append(pltpu.VMEM((len(used_tiles) * tile, width), BF16))
-        shapes.append(jax.ShapeDtypeStruct((tiles, tile), F32))
+        shapes.append(jax.ShapeDtypeStruct((place_count, block_rows), F32))
         own_ref, own_lines, own_cols = add(own[0], pltpu.HBM), add_small(own[1]), add_small(own[2])
         copies += len(used_tiles)
     if used_blocks:
@@ -137,6 +144,9 @@
         block_refs = {n: [(add(array, pltpu.HBM), place) for array, place in blocks[0][n][1]] for n in used_blocks}
         copies += sum(len(refs) for refs in block_refs.values())
     readout_at = add_small(readout)
+    carry = [
+        (out, add_small(value)) for out, value in zip((own_out, block_out), carried) if out is not None and value is not None
+    ]
     scratch.append(pltpu.SemaphoreType.DMA((copies + len(small),)))
     inputs, outputs = len(arrays), len(shapes)
 
@@ -187,10 +197,13 @@
         for part in parts[:2]:
             for key in keys(part):
                 fetch(key)
-        for out in outs:
-            out[...] = jnp.zeros(out.shape, F32)
+        for n, out in enumerate(outs):
+            if n not in dict(carry):
+                out[...] = jnp.zeros(out.shape, F32)
         for copy in first_copies:
             copy.wait()
+        for out, place in carry:
+            outs[out][...] = held[place][...]
         for number, part in enumerate(parts):
             for key in keys(part):
                 for copy in pending[key]:
@@ -234,8 +247,12 @@
                     if size % 128 == 0:
                         value = sum(value[:, k : k + 128] for k in range(0, size, 128))
                     line += jnp.sum(value.T, axis=0, keepdims=True)
-                out = outs[own_out if mine else block_out]
-                out[pl.ds(row, 1), :] += line
+                if mine:
+                    for k in range(tile // block_rows):
+                        at_row = row * (tile // block_rows) + k
+                        outs[own_out][at_row : at_row + 1, :] += line[:, k * block_rows : (k + 1) * block_rows]
+                else:
+                    outs[block_out][pl.ds(row, 1), :] += line
 
     results = pl.pallas_call(
         kernel,
@@ -246,7 +263,7 @@
         compiler_params=pltpu.CompilerParams(vmem_limit_bytes=VMEM_BYTES),
         cost_estimate=SMALL,
     )(*arrays)
-    return (results[own_out] if used_tiles else None), (results[block_out] if used_blocks else None)
+    return (results[own_out] if used_tiles else carried[0]), (results[block_out] if used_blocks else carried[1])
 
 
 def noise_columns(gate, up, cuts):
@@ -545,7 +562,7 @@
         kept = jnp.concatenate(pick(hi), 1)
         near = [kept] + [along(kept, step) for step in range(1, lo_size)]
 
-    sent = after(sent, *cut, *jax.tree.leaves(near[1:]))
+    sent = after(sent, other_bundle, *cut, *jax.tree.leaves(near[1:]))
 
     starts = [half_start]
     for step in range(lo_size):
@@ -582,13 +599,13 @@
     steps = line_steps(sent, outer, z, outer_permute)
     held, spread, far, chunk_list = [sent], [line_gather(sent, inner, y, inner_permute)], [], []
     end = len(chunks)
-    passed = [across(after(cut[0], other_bundle))] + [None] * (len(crossing) - 1)
-    own_total = other_total = 0.0
+    passed = [across(cut[0])] + [None] * (len(crossing) - 1)
+    own_total = other_total = None
     done, barrier = [0] * outer, list(directions)
 
     def gather_next():
         next(steps)
-        held.append(steps.send(lambda value: after(value, *barrier)))
+        held.append(steps.send(lambda value: after(value, *barrier) if barrier else value))
         spread.append(line_gather(held[-1], inner, y, inner_permute))
 
     def bring(j):
@@ -603,10 +620,9 @@
             for n, pieces in enumerate(spread)
         ]
         mine, theirs = gated_scores(
-            ids, chunk_list, own, (blocks, far_lines, far_columns), parts, half_readout
+            ids, chunk_list, own, (blocks, far_lines, far_columns), parts, half_readout, (own_total, other_total)
         )
-        own_total = own_total if mine is None else own_total + mine.reshape(-1)
-        other_total = other_total if theirs is None else other_total + theirs.reshape(-1)
+        own_total, other_total = mine, theirs
         return [value for value in (mine, theirs) if value is not None]
 
     for j, group in enumerate(crossing):
@@ -630,19 +646,22 @@
             chunk_list.append((begin, size, sources))
         there = len(chunk_list)
         parts = [(True, t, t + 1, i, i + 1) for i in range(there - len(group), there) for t in range(members)]
-        if j < len(crossing) - 1:
-            ready = min(j + 1, outer - 1)
-            old = [n for n in range(ready) if done[n] == there - 1]
+        ready = min(j + 1, outer - 1)
+        old = [n for n in range(ready) if done[n] == there - len(group)]
+        for i in range(there - len(group), there):
             if old:
-                parts.append((False, old[0], old[-1] + 1, there - 1, there))
-            for n in range(ready):
-                parts += [(False, n, n + 1, i, i + 1) for i in range(done[n], there) if n not in old]
-                done[n] = there
-            barrier = score(parts)
+                parts.append((False, old[0], old[-1] + 1, i, i + 1))
+        for n in range(ready):
+            parts += [(False, n, n + 1, i, i + 1) for i in range(done[n], there) if n not in old]
+            done[n] = there
+        barrier = score(parts)
     while len(held) < outer:
         gather_next()
-    rest = [(False, n, n + 1, i, i + 1) for n in range(outer) for i in range(done[n], end - 1)]
-    score(rest + [(False, 0, outer, end - 1, end)] + parts)
+    rest = []
+    for n in range(outer):
+        cuts_at = list(range(done[n], max(done[n], end - 2))) + [max(done[n], end - 2), end]
+        rest += [(False, n, n + 1, a, b) for a, b in zip(cuts_at, cuts_at[1:]) if a < b]
+    score(rest)
 
     crossed = across(other_total)
     near_own = [inner_permute(own_total, lambda c, s=s: (c + s) % inner) for s in range(1, inner)]

time: 170 us -> 167 us (0.982)
  waiting for transfers between devices: 48.3 us -> 40.2 us
  starting transfers between devices: 31.5 us -> 34.6 us
  Pallas kernels: 76.8 us -> 79.5 us
    ppermute x8, waiting for transfers between devices: 20 us -> 10 us  [outer_permute(): lax.ppermute(value, 'shard', [(s, z * inner + y) for s, z, y in pairs if...]
    pallas_call x4, Pallas kernels: 57.3 us -> 59.9 us  [gated_scores(): pl.pallas_call(kernel, out_shape=shapes, in_specs=specs, out_specs=[pl.Bl...]
    ppermute x5, waiting for transfers between devices: 7.6 us -> 5.19 us  [inner_permute(): lax.ppermute(value, 'shard', [(s, z * inner + y) for s, z, y in pairs if...]
    ppermute x7 -> x6, starting transfers between devices: 7.23 us -> 9.54 us  [across(): return lax.ppermute(value, 'pop', across_pairs)]
    ppermute x1, waiting for transfers between devices: 0.22 us -> 2.39 us  [body(): lax.ppermute(other_total, ('pop', 'shard'), [(p * shard_size + s, (p + lo...]
    ppermute x7 -> x6, waiting for transfers between devices: 17.5 us -> 19.4 us  [across(): return lax.ppermute(value, 'pop', across_pairs)]
  transfers between devices with their start and end apart: 28 -> 26, of which waited for: 15 -> 15; matrix products, arithmetic and copies ran while one was open for 6% -> 6% of each run, Pallas kernels for 36% -> 42%
where the time goes in v4:
time: 167 us; the launch traced here: 166 us
  Pallas kernels  79.5 us (48%)
  waiting for transfers between devices  40.2 us (24%)
  starting transfers between devices  34.6 us (21%)
  other arithmetic  5.91 us (4%)
  local copies, waits for them, and re-layouts  5.55 us (3%)
    pallas_call x4, Pallas kernels, gated_scores(): pl.pallas_call(kernel, out_shape=shapes, in_specs=specs, out_specs=[pl.Bl...  59.9 us
    ppermute x6, waiting for transfers between devices, across(): return lax.ppermute(value, 'pop', across_pairs)  19.4 us
    ppermute x8, starting transfers between devices, outer_permute(): lax.ppermute(value, 'shard', [(s, z * inner + y) for s, z, y in pairs if...  17.4 us
    ppermute x8, waiting for transfers between devices, outer_permute(): lax.ppermute(value, 'shard', [(s, z * inner + y) for s, z, y in pairs if...  10 us
    ppermute x6, starting transfers between devices, across(): return lax.ppermute(value, 'pop', across_pairs)  9.54 us
    pallas_call x1, Pallas kernels, update_directions(): pl.pallas_call(kernel, grid=(block_rows // step,), out_shape=[jax.ShapeDt...  8.05 us
    pallas_call x1, Pallas kernels, own_factors(): pl.pallas_call(kernel, out_shape=[jax.ShapeDtypeStruct((lines, hidden + b...  6.23 us
    ppermute x5, starting transfers between devices, inner_permute(): lax.ppermute(value, 'shard', [(s, z * inner + y) for s, z, y in pairs if...  5.57 us
  transfers between devices with their start and end apart: 26, of which 15 were waited for; matrix products, arithmetic and copies ran while one was open for 6% of the time, Pallas kernels for 42%

profile of v4, /device:TPU:0, one launch (start us, length us, event | category | flops | bytes accessed | tf_op | source)
XLA Modules:
  0.0 166.5 jit_solution(6290759121633213665)
XLA Ops:
  0.6 0.5 collective-permute-start
  1.2 2.2 %dynamic_slice.6.waited_ref = bf16[240,2048]{1,0:T(8,128)(2,1)} dynamic-slice(bf16[960,4096]{1,0:T(8,128)(2,1)} %bitcast.19, s32[]{:T(128)S(6)} %select_n.100, s32[]{:T(128)S(6)} %select_n.101), dynamic_slice_sizes={240,2048} | dynamic-slice | bytes 1966084 | tf_op jit(solution)/shard_map/dynamic_slice | solution.py:518
  3.5 2.9 %collective-permute-start.3 = (bf16[240,2048]{1,0:T(8,128)(2,1)}, bf16[240,2048]{1,0:T(8,128)(2,1)}, u32[]{:S(2)}, u32[]{:S(2)}) collective-permute-start(bf16[240,2048]{1,0:T(8,128)(2,1)} %dynamic_slice.6.waited_ref), channel_id=1, source_target_pairs={{0,16},{8,24},{16,0},{24,8},{1,17},{9,25},{17,1},{25,9},{2,18},{10... | collective-permute-start | bytes 2949128 | tf_op jit(solution)/shard_map/ppermute | solution.py:502
  6.4 0.7 pad_add_fusion.starts_ref
  7.0 6.2 %shard_map.112 = (bf16[16,5408]{1,0:T(8,128)(2,1)}, bf16[2,48,480]{2,1,0:T(8,128)(2,1)}, bf16[48,1792]{1,0:T(8,128)(2,1)}) custom-call(s32[2]{0:T(128)} %pad_add_fusion.starts_ref, bf16[2,480,4096]{2,1,0:T(8,128)(2,1)} %refs_11_.1, bf16[2,4,4096]{2,1,0:T(4,128)(2,1)} %ag.3, bf16[2,4,4096]{2,1,0:T(4,128)(2,1)} %au.3, bf16[2,4,1792]{2,1,0:T(4,128)(2,1)} %gc.1, ...), custom_call_target="tpu_custom_call" | custom-call | flops 1 | bytes 1 | tf_op jit(solution)/shard_map/pallas_call | solution.py:333
  13.3 3.3 %shard_map.113 = (bf16[1024,512]{1,0:T(8,128)(2,1)}, bf16[1024,768]{1,0:T(8,128)(2,1)}, bf16[1024,512]{1,0:T(8,128)(2,1)}) custom-call(s32[1]{0:T(128)} %bitcast.11.shift_ref, bf16[1024,1792]{1,0:T(8,128)(2,1)} %refs_1_.7, bf16[1024,1792]{1,0:T(8,128)(2,1)} %refs_2_.7, bf16[16,5408]{1,0:T(8,128)(2,1)} %get-tuple-element.21.waited_ref.own_ref), custom_call_target="tpu_custom_call" | custom-call | flops 1 | bytes 1 | tf_op jit(solution)/shard_map/pallas_call | solution.py:460
  16.6 2.1 %collective-permute-start.2 = (bf16[1024,512]{1,0:T(8,128)(2,1)}, bf16[1024,512]{1,0:T(8,128)(2,1)}, u32[]{:S(2)}, u32[]{:S(2)}) collective-permute-start(bf16[1024,512]{1,0:T(8,128)(2,1)} %get-tuple-element.22.refs_2_), channel_id=1, source_target_pairs={{0,16},{8,24},{16,0},{24,8},{1,17},{9,25},{17,1},{25,9},{2,18},{10... | collective-permute-start | bytes 3145736 | tf_op jit(solution)/shard_map/ppermute | solution.py:502
  18.7 14.3 %collective-permute-done.4.refs_1_.bundle_ref = bf16[16,5408]{1,0:T(8,128)(2,1)} collective-permute-done((bf16[16,5408]{1,0:T(8,128)(2,1)}, bf16[16,5408]{1,0:T(8,128)(2,1)}, u32[]{:S(2)}, u32[]{:S(2)}) %collective-permute-start.4) | collective-permute-done | bytes 173088 | tf_op jit(solution)/shard_map/ppermute | solution.py:502
  33.1 2.2 %collective-permute-start.5 = (bf16[240,2048]{1,0:T(8,128)(2,1)}, bf16[240,2048]{1,0:T(8,128)(2,1)}, u32[]{:S(2)}, u32[]{:S(2)}) collective-permute-start(bf16[240,2048]{1,0:T(8,128)(2,1)} %shard_map.114.refs_12_.refs_14_.refs_16_), channel_id=1, source_target_pairs={{0,2},{1,3},{2,0},{3,1},{4,6},{5,7},{6,4},{7,5},{8,10},{9,11},{10,... | collective-permute-start | bytes 2949128 | tf_op jit(solution)/shard_map/ppermute | solution.py:510
  35.3 1.5 collective-permute-start.7
  36.8 1.6 collective-permute-start.10
  38.4 0.7 stack.81.starts_ref
  39.1 2.0 %shard_map.115 = (bf16[4,48,240]{2,1,0:T(8,128)(2,1)}, bf16[48,1792]{1,0:T(8,128)(2,1)}, bf16[32,2944]{1,0:T(8,128)(2,1)}, bf16[32,2944]{1,0:T(8,128)(2,1)}) custom-call(s32[5]{0:T(128)} %stack.81.starts_ref, bf16[16,5408]{1,0:T(8,128)(2,1)} %collective-permute-done.4.refs_1_.bundle_ref, bf16[16,5408]{1,0:T(8,128)(2,1)} %get-tuple-element.21.waited_ref.own_ref, ...), custom_call_target="tpu_custom_call" | custom-call | flops 1 | bytes 1 | tf_op jit(solution)/shard_map/pallas_call | solution.py:387
  41.0 1.8 %collective-permute-done.6.refs_1_.refs_2_ = bf16[32,2944]{1,0:T(8,128)(2,1)} collective-permute-done((bf16[32,2944]{1,0:T(8,128)(2,1)}, bf16[32,2944]{1,0:T(8,128)(2,1)}, u32[]{:S(2)}, u32[]{:S(2)}) %collective-permute-start.6) | collective-permute-done | bytes 188448 | tf_op jit(solution)/shard_map/ppermute | solution.py:506
  42.8 1.5 collective-permute-start.9
  44.3 8.0 %shard_map.116 = (f32[1024,1792]{1,0:T(8,128)}, f32[1024,1792]{1,0:T(8,128)}) custom-call(bf16[32,2944]{1,0:T(8,128)(2,1)} %get-tuple-element.25.refs_0_.refs_1_, bf16[32,2944]{1,0:T(8,128)(2,1)} %collective-permute-done.6.refs_1_.refs_2_), custom_call_target="tpu_custom_call" | custom-call | flops 1 | bytes 1 | tf_op jit(solution)/shard_map/pallas_call | solution.py:421
  52.3 3.8 %collective-permute-done.5.refs_0_ = bf16[240,2048]{1,0:T(8,128)(2,1)} collective-permute-done((bf16[240,2048]{1,0:T(8,128)(2,1)}, bf16[240,2048]{1,0:T(8,128)(2,1)}, u32[]{:S(2)}, u32[]{:S(2)}) %collective-permute-start.5) | collective-permute-done | bytes 983072 | tf_op jit(solution)/shard_map/ppermute | solution.py:510
  56.1 1.2 collective-permute-done.7.refs_2_.refs_13_.refs_15_.refs_17_
  57.3 4.5 %collective-permute-start.11 = (bf16[240,2048]{1,0:T(8,128)(2,1)}, bf16[240,2048]{1,0:T(8,128)(2,1)}, u32[]{:S(2)}, u32[]{:S(2)}) collective-permute-start(bf16[240,2048]{1,0:T(8,128)(2,1)} %shard_map.120), channel_id=1, source_target_pairs={{0,2},{1,3},{2,0},{3,1},{4,6},{5,7},{6,4},{7,5},{8,10},{9,11},{10,... | collective-permute-start | bytes 2949128 | tf_op jit(solution)/shard_map/ppermute | solution.py:510
  61.9 0.5 collective-permute-start.12
  62.4 0.8 dynamic_slice.7
  63.2 0.6 broadcast_in_dim.7.refs_14_.refs_18_.refs_22_.refs_15_
  63.7 0.6 stack.73.refs_0_
  64.3 1.6 collective-permute-start.15
  66.0 11.5 %shard_map.121 = (f32[4,240]{1,0:T(4,128)}, f32[4,240]{1,0:T(4,128)}) custom-call(s32[11]{0:T(128)} %stack.73.refs_0_, bf16[1024,1792]{1,0:T(8,128)(2,1)} %refs_1_.7, bf16[1024,1792]{1,0:T(8,128)(2,1)} %refs_2_.7, bf16[1024,1792]{1,0:T(8,128)(2,1)} %collective-permute-done.refs_5_.refs_3_, bf16[1024,1792]{1,0:T(8,128)(2,1)} %collective-permute-done.1.refs_6_.refs_4_, ...), custom_call_target="tpu_custom_call" | custom-call | flops 1 | bytes 1 | tf_op jit(solution)/shard_map/pallas_call | solution.py:257
  77.5 4.3 %collective-permute-done.11.refs_0_ = bf16[240,2048]{1,0:T(8,128)(2,1)} collective-permute-done((bf16[240,2048]{1,0:T(8,128)(2,1)}, bf16[240,2048]{1,0:T(8,128)(2,1)}, u32[]{:S(2)}, u32[]{:S(2)}) %collective-permute-start.11) | collective-permute-done | bytes 983072 | tf_op jit(solution)/shard_map/ppermute | solution.py:510
  81.8 2.3 %broadcast_select_fusion.1.refs_1_.refs_20_ = bf16[240,2048]{1,0:T(8,128)(2,1)} fusion(bf16[240,2048]{1,0:T(8,128)(2,1)} %shard_map.122, bf16[240,2048]{1,0:T(8,128)(2,1)} %shard_map.120, pred[]{:T(512)S(6)} %or.3), kind=kLoop, calls=%fused_computation.1 | loop fusion | flops 491520 | bytes 2949121 | tf_op jit(solution)/shard_map/jit(_where)/select_n | solution.py:62
  84.1 4.5 %collective-permute-done.9.refs_0_ = bf16[1024,768]{1,0:T(8,128)(2,1)} collective-permute-done((bf16[1024,768]{1,0:T(8,128)(2,1)}, bf16[1024,768]{1,0:T(8,128)(2,1)}, u32[]{:S(2)}, u32[]{:S(2)}) %collective-permute-start.9) | collective-permute-done | bytes 1572896 | tf_op jit(solution)/shard_map/ppermute | solution.py:502
  88.7 1.9 %collective-permute-start.16 = (bf16[240,2048]{1,0:T(8,128)(2,1)}, bf16[240,2048]{1,0:T(8,128)(2,1)}, u32[]{:S(2)}, u32[]{:S(2)}) collective-permute-start(bf16[240,2048]{1,0:T(8,128)(2,1)} %shard_map.125), channel_id=1, source_target_pairs={{0,2},{1,3},{2,0},{3,1},{4,6},{5,7},{6,4},{7,5},{8,10},{9,11},{10,... | collective-permute-start | bytes 2949128 | tf_op jit(solution)/shard_map/ppermute | solution.py:510
  90.6 1.5 collective-permute-start.14
  92.1 1.5 collective-permute-start.17
  93.6 19.6 %shard_map.126 = (f32[4,240]{1,0:T(4,128)}, f32[4,240]{1,0:T(4,128)}) custom-call(s32[11]{0:T(128)} %stack.73.refs_0_, bf16[1024,1792]{1,0:T(8,128)(2,1)} %refs_1_.7, bf16[1024,1792]{1,0:T(8,128)(2,1)} %refs_2_.7, bf16[1024,1792]{1,0:T(8,128)(2,1)} %collective-permute-done.refs_5_.refs_3_, bf16[1024,1792]{1,0:T(8,128)(2,1)} %collective-permute-done.1.refs_6_.refs_4_, ...), custom_call_target="tpu_custom_call" | custom-call | flops 1 | bytes 1 | tf_op jit(solution)/shard_map/pallas_call | solution.py:257
  113.2 2.3 %broadcast_select_fusion.refs_1_.refs_13_ = bf16[240,2048]{1,0:T(8,128)(2,1)} fusion(bf16[240,2048]{1,0:T(8,128)(2,1)} %shard_map.127, bf16[240,2048]{1,0:T(8,128)(2,1)} %shard_map.125, pred[]{:T(512)S(6)} %or.3), kind=kLoop, calls=%fused_computation | loop fusion | flops 491520 | bytes 2949121 | tf_op jit(solution)/shard_map/jit(_where)/select_n | solution.py:65
  116.1 1.5 collective-permute-start.19
  117.6 1.5 collective-permute-done.18.refs_10_
  119.1 18.5 %shard_map.129 = (f32[4,240]{1,0:T(4,128)}, f32[4,240]{1,0:T(4,128)}) custom-call(s32[11]{0:T(128)} %stack.73.refs_0_, bf16[1024,1792]{1,0:T(8,128)(2,1)} %refs_1_.7, bf16[1024,1792]{1,0:T(8,128)(2,1)} %refs_2_.7, bf16[1024,1792]{1,0:T(8,128)(2,1)} %collective-permute-done.refs_5_.refs_3_, bf16[1024,1792]{1,0:T(8,128)(2,1)} %collective-permute-done.1.refs_6_.refs_4_, ...), custom_call_target="tpu_custom_call" | custom-call | flops 1 | bytes 1 | tf_op jit(solution)/shard_map/pallas_call | solution.py:257
  137.7 3.0 %collective-permute-done.19.refs_14_ = bf16[240,2048]{1,0:T(8,128)(2,1)} collective-permute-done((bf16[240,2048]{1,0:T(8,128)(2,1)}, bf16[240,2048]{1,0:T(8,128)(2,1)}, u32[]{:S(2)}, u32[]{:S(2)}) %collective-permute-start.19) | collective-permute-done | bytes 983072 | tf_op jit(solution)/shard_map/ppermute | solution.py:514
  140.6 10.2 %shard_map.130 = f32[4,240]{1,0:T(4,128)} custom-call(s32[11]{0:T(128)} %stack.73.refs_0_, bf16[1024,1792]{1,0:T(8,128)(2,1)} %refs_1_.7, bf16[1024,1792]{1,0:T(8,128)(2,1)} %refs_2_.7, bf16[1024,1792]{1,0:T(8,128)(2,1)} %collective-permute-done.refs_5_.refs_3_, bf16[1024,1792]{1,0:T(8,128)(2,1)} %collective-permute-done.1.refs_6_.refs_4_, ...), custom_call_target="tpu_custom_call" | custom-call | flops 1 | bytes 1 | tf_op jit(solution)/shard_map/pallas_call | solution.py:257
  150.8 1.6 collective-permute-start.20
  152.4 1.5 collective-permute-start.22
  154.7 2.4 %collective-permute-done.22 = f32[4,240]{1,0:T(4,128)S(1)} collective-permute-done((f32[4,240]{1,0:T(4,128)}, f32[4,240]{1,0:T(4,128)S(1)}, u32[]{:S(2)}, u32[]{:S(2)}) %collective-permute-start.22) | collective-permute-done | bytes 3872 | tf_op jit(solution)/shard_map/ppermute | solution.py:669
  157.1 0.6 collective-permute-done.21
  157.7 0.7 add_add_fusion.1
  158.4 1.2 collective-permute-start.23
  159.6 2.6 %collective-permute-start.24 = (f32[4,240]{1,0:T(4,128)S(1)}, f32[4,240]{1,0:T(4,128)S(1)}, u32[]{:S(2)}, u32[]{:S(2)}) collective-permute-start(f32[4,240]{1,0:T(4,128)S(1)} %add_add_fusion.1), channel_id=1, source_target_pairs={{0,4},{1,5},{2,6},{3,7},{4,0},{5,1},{6,2},{7,3},{8,12},{9,13},{10,... | collective-permute-start | bytes 11528 | tf_op jit(solution)/shard_map/ppermute | solution.py:510
  162.2 1.7 %collective-permute-start.25 = (f32[4,240]{1,0:T(4,128)S(1)}, f32[4,240]{1,0:T(4,128)S(1)}, u32[]{:S(2)}, u32[]{:S(2)}) collective-permute-start(f32[4,240]{1,0:T(4,128)S(1)} %add_add_fusion.1), channel_id=1, source_target_pairs={{0,6},{1,7},{2,0},{3,1},{4,2},{5,3},{6,4},{7,5},{8,14},{9,15},{10,... | collective-permute-start | bytes 11528 | tf_op jit(solution)/shard_map/ppermute | solution.py:510
  164.1 1.7 %collective-permute-done.25 = f32[4,240]{1,0:T(4,128)S(1)} collective-permute-done((f32[4,240]{1,0:T(4,128)S(1)}, f32[4,240]{1,0:T(4,128)S(1)}, u32[]{:S(2)}, u32[]{:S(2)}) %collective-permute-start.25) | collective-permute-done | bytes 3872 | tf_op jit(solution)/shard_map/ppermute | solution.py:510
  165.8 0.7 reshape.13
  (34 shorter events, 1.8 us)
Async XLA Ops:
  0.6 32.4 %collective-permute-start = (bf16[1024,1792]{1,0:T(8,128)(2,1)}, bf16[1024,1792]{1,0:T(8,128)(2,1)}, u32[]{:S(2)}, u32[]{:S(2)}) collective-permute-start(bf16[1024,1792]{1,0:T(8,128)(2,1)} %refs_1_.7), channel_id=1, source_target_pairs={{0,8},{8,0},{16,24},{24,16},{1,9},{9,1},{17,25},{25,17},{2,10},{10... | collective-permute-start | bytes 11010056 | tf_op jit(solution)/shard_map/ppermute | solution.py:506
  1.1 31.9 %collective-permute-start.1 = (bf16[1024,1792]{1,0:T(8,128)(2,1)}, bf16[1024,1792]{1,0:T(8,128)(2,1)}, u32[]{:S(2)}, u32[]{:S(2)}) collective-permute-start(bf16[1024,1792]{1,0:T(8,128)(2,1)} %refs_2_.7), channel_id=1, source_target_pairs={{0,8},{8,0},{16,24},{24,16},{1,9},{9,1},{17,25},{25,17},{2,10},{10... | collective-permute-start | bytes 11010056 | tf_op jit(solution)/shard_map/ppermute | solution.py:506
  3.5 29.6 %collective-permute-start.3 = (bf16[240,2048]{1,0:T(8,128)(2,1)}, bf16[240,2048]{1,0:T(8,128)(2,1)}, u32[]{:S(2)}, u32[]{:S(2)}) collective-permute-start(bf16[240,2048]{1,0:T(8,128)(2,1)} %dynamic_slice.6.waited_ref), channel_id=1, source_target_pairs={{0,16},{8,24},{16,0},{24,8},{1,17},{9,25},{17,1},{25,9},{2,18},{10... | collective-permute-start | bytes 2949128 | tf_op jit(solution)/shard_map/ppermute | solution.py:502
  13.3 19.8 %collective-permute-start.4 = (bf16[16,5408]{1,0:T(8,128)(2,1)}, bf16[16,5408]{1,0:T(8,128)(2,1)}, u32[]{:S(2)}, u32[]{:S(2)}) collective-permute-start(bf16[16,5408]{1,0:T(8,128)(2,1)} %get-tuple-element.21.waited_ref.own_ref), channel_id=1, source_target_pairs={{0,16},{8,24},{16,0},{24,8},{1,17},{9,25},{17,1},{25,9},{2,18},{10... | collective-permute-start | bytes 519176 | tf_op jit(solution)/shard_map/ppermute | solution.py:502
  16.6 39.5 %collective-permute-start.2 = (bf16[1024,512]{1,0:T(8,128)(2,1)}, bf16[1024,512]{1,0:T(8,128)(2,1)}, u32[]{:S(2)}, u32[]{:S(2)}) collective-permute-start(bf16[1024,512]{1,0:T(8,128)(2,1)} %get-tuple-element.22.refs_2_), channel_id=1, source_target_pairs={{0,16},{8,24},{16,0},{24,8},{1,17},{9,25},{17,1},{25,9},{2,18},{10... | collective-permute-start | bytes 3145736 | tf_op jit(solution)/shard_map/ppermute | solution.py:502
  33.1 23.1 %collective-permute-start.5 = (bf16[240,2048]{1,0:T(8,128)(2,1)}, bf16[240,2048]{1,0:T(8,128)(2,1)}, u32[]{:S(2)}, u32[]{:S(2)}) collective-permute-start(bf16[240,2048]{1,0:T(8,128)(2,1)} %shard_map.114.refs_12_.refs_14_.refs_16_), channel_id=1, source_target_pairs={{0,2},{1,3},{2,0},{3,1},{4,6},{5,7},{6,4},{7,5},{8,10},{9,11},{10,... | collective-permute-start | bytes 2949128 | tf_op jit(solution)/shard_map/ppermute | solution.py:510
  35.3 22.1 %collective-permute-start.7 = (bf16[240,2048]{1,0:T(8,128)(2,1)}, bf16[240,2048]{1,0:T(8,128)(2,1)}, u32[]{:S(2)}, u32[]{:S(2)}) collective-permute-start(bf16[240,2048]{1,0:T(8,128)(2,1)} %shard_map.114.refs_12_.refs_14_.refs_16_), channel_id=1, source_target_pairs={{0,1},{1,0},{2,3},{3,2},{4,5},{5,4},{6,7},{7,6},{8,9},{9,8},{10,11... | collective-permute-start | bytes 2949128 | tf_op jit(solution)/shard_map/ppermute | solution.py:514
  36.8 20.6 %collective-permute-start.10 = (bf16[240,2048]{1,0:T(8,128)(2,1)}, bf16[240,2048]{1,0:T(8,128)(2,1)}, u32[]{:S(2)}, u32[]{:S(2)}) collective-permute-start(bf16[240,2048]{1,0:T(8,128)(2,1)} %shard_map.114.refs_12_.refs_14_.refs_16_), channel_id=1, source_target_pairs={{2,4},{3,5},{4,2},{5,3},{10,12},{11,13},{12,10},{13,11},{18,20},{1... | collective-permute-start | bytes 2949128 | tf_op jit(solution)/shard_map/ppermute | solution.py:510
  41.0 1.8 %collective-permute-start.6 = (bf16[32,2944]{1,0:T(8,128)(2,1)}, bf16[32,2944]{1,0:T(8,128)(2,1)}, u32[]{:S(2)}, u32[]{:S(2)}) collective-permute-start(bf16[32,2944]{1,0:T(8,128)(2,1)} %get-tuple-element.26), channel_id=1, source_target_pairs={{0,8},{8,0},{16,24},{24,16},{1,9},{9,1},{17,25},{25,17},{2,10},{10... | collective-permute-start | bytes 565256 | tf_op jit(solution)/shard_map/ppermute | solution.py:506
  42.8 45.8 %collective-permute-start.9 = (bf16[1024,768]{1,0:T(8,128)(2,1)}, bf16[1024,768]{1,0:T(8,128)(2,1)}, u32[]{:S(2)}, u32[]{:S(2)}) collective-permute-start(bf16[1024,768]{1,0:T(8,128)(2,1)} %shard_map.119), channel_id=1, source_target_pairs={{0,16},{8,24},{16,0},{24,8},{1,17},{9,25},{17,1},{25,9},{2,18},{10... | collective-permute-start | bytes 4718600 | tf_op jit(solution)/shard_map/ppermute | solution.py:502
  57.3 8.6 %collective-permute-start.8 = (bf16[1024,512]{1,0:T(8,128)(2,1)}, bf16[1024,512]{1,0:T(8,128)(2,1)}, u32[]{:S(2)}, u32[]{:S(2)}) collective-permute-start(bf16[1024,512]{1,0:T(8,128)(2,1)} %shard_map.118.refs_5_.refs_1_), channel_id=1, source_target_pairs={{0,8},{8,0},{16,24},{24,16},{1,9},{9,1},{17,25},{25,17},{2,10},{10... | collective-permute-start | bytes 3145736 | tf_op jit(solution)/shard_map/ppermute | solution.py:506
  57.3 24.5 %collective-permute-start.11 = (bf16[240,2048]{1,0:T(8,128)(2,1)}, bf16[240,2048]{1,0:T(8,128)(2,1)}, u32[]{:S(2)}, u32[]{:S(2)}) collective-permute-start(bf16[240,2048]{1,0:T(8,128)(2,1)} %shard_map.120), channel_id=1, source_target_pairs={{0,2},{1,3},{2,0},{3,1},{4,6},{5,7},{6,4},{7,5},{8,10},{9,11},{10,... | collective-permute-start | bytes 2949128 | tf_op jit(solution)/shard_map/ppermute | solution.py:510
  61.9 26.8 %collective-permute-start.12 = (bf16[240,2048]{1,0:T(8,128)(2,1)}, bf16[240,2048]{1,0:T(8,128)(2,1)}, u32[]{:S(2)}, u32[]{:S(2)}) collective-permute-start(bf16[240,2048]{1,0:T(8,128)(2,1)} %shard_map.117.refs_1_.refs_16_.refs_18_), channel_id=1, source_target_pairs={{0,1},{1,0},{2,3},{3,2},{4,5},{5,4},{6,7},{7,6},{8,9},{9,8},{10,11... | collective-permute-start | bytes 2949128 | tf_op jit(solution)/shard_map/ppermute | solution.py:514
  64.3 24.3 %collective-permute-start.15 = (bf16[240,2048]{1,0:T(8,128)(2,1)}, bf16[240,2048]{1,0:T(8,128)(2,1)}, u32[]{:S(2)}, u32[]{:S(2)}) collective-permute-start(bf16[240,2048]{1,0:T(8,128)(2,1)} %shard_map.117.refs_1_.refs_16_.refs_18_), channel_id=1, source_target_pairs={{2,4},{3,5},{4,2},{5,3},{10,12},{11,13},{12,10},{13,11},{18,20},{1... | collective-permute-start | bytes 2949128 | tf_op jit(solution)/shard_map/ppermute | solution.py:510
  88.7 4.9 %collective-permute-start.13 = (bf16[1024,768]{1,0:T(8,128)(2,1)}, bf16[1024,768]{1,0:T(8,128)(2,1)}, u32[]{:S(2)}, u32[]{:S(2)}) collective-permute-start(bf16[1024,768]{1,0:T(8,128)(2,1)} %shard_map.123.refs_7_), channel_id=1, source_target_pairs={{0,8},{8,0},{16,24},{24,16},{1,9},{9,1},{17,25},{25,17},{2,10},{10... | collective-permute-start | bytes 4718600 | tf_op jit(solution)/shard_map/ppermute | solution.py:506
  88.7 24.6 %collective-permute-start.16 = (bf16[240,2048]{1,0:T(8,128)(2,1)}, bf16[240,2048]{1,0:T(8,128)(2,1)}, u32[]{:S(2)}, u32[]{:S(2)}) collective-permute-start(bf16[240,2048]{1,0:T(8,128)(2,1)} %shard_map.125), channel_id=1, source_target_pairs={{0,2},{1,3},{2,0},{3,1},{4,6},{5,7},{6,4},{7,5},{8,10},{9,11},{10,... | collective-permute-start | bytes 2949128 | tf_op jit(solution)/shard_map/ppermute | solution.py:510
  90.6 25.5 %collective-permute-start.14 = (bf16[1024,512]{1,0:T(8,128)(2,1)}, bf16[1024,512]{1,0:T(8,128)(2,1)}, u32[]{:S(2)}, u32[]{:S(2)}) collective-permute-start(bf16[1024,512]{1,0:T(8,128)(2,1)} %shard_map.124), channel_id=1, source_target_pairs={{0,16},{8,24},{16,0},{24,8},{1,17},{9,25},{17,1},{25,9},{2,18},{10... | collective-permute-start | bytes 3145736 | tf_op jit(solution)/shard_map/ppermute | solution.py:502
  92.1 23.9 %collective-permute-start.17 = (bf16[240,2048]{1,0:T(8,128)(2,1)}, bf16[240,2048]{1,0:T(8,128)(2,1)}, u32[]{:S(2)}, u32[]{:S(2)}) collective-permute-start(bf16[240,2048]{1,0:T(8,128)(2,1)} %broadcast_select_fusion.1.refs_1_.refs_20_), channel_id=1, source_target_pairs={{0,1},{1,0},{2,3},{3,2},{4,5},{5,4},{6,7},{7,6},{8,9},{9,8},{10,11... | collective-permute-start | bytes 2949128 | tf_op jit(solution)/shard_map/ppermute | solution.py:514
  116.1 3.0 %collective-permute-start.18 = (bf16[1024,512]{1,0:T(8,128)(2,1)}, bf16[1024,512]{1,0:T(8,128)(2,1)}, u32[]{:S(2)}, u32[]{:S(2)}) collective-permute-start(bf16[1024,512]{1,0:T(8,128)(2,1)} %shard_map.128.refs_9_), channel_id=1, source_target_pairs={{0,8},{8,0},{16,24},{24,16},{1,9},{9,1},{17,25},{25,17},{2,10},{10... | collective-permute-start | bytes 3145736 | tf_op jit(solution)/shard_map/ppermute | solution.py:506
  116.1 24.5 %collective-permute-start.19 = (bf16[240,2048]{1,0:T(8,128)(2,1)}, bf16[240,2048]{1,0:T(8,128)(2,1)}, u32[]{:S(2)}, u32[]{:S(2)}) collective-permute-start(bf16[240,2048]{1,0:T(8,128)(2,1)} %broadcast_select_fusion.refs_1_.refs_13_), channel_id=1, source_target_pairs={{0,1},{1,0},{2,3},{3,2},{4,5},{5,4},{6,7},{7,6},{8,9},{9,8},{10,11... | collective-permute-start | bytes 2949128 | tf_op jit(solution)/shard_map/ppermute | solution.py:514
  150.8 3.9 %collective-permute-start.20 = (f32[4,240]{1,0:T(4,128)}, f32[4,240]{1,0:T(4,128)S(1)}, u32[]{:S(2)}, u32[]{:S(2)}) collective-permute-start(f32[4,240]{1,0:T(4,128)} %shard_map.130), channel_id=1, source_target_pairs={{0,16},{8,24},{16,0},{24,8},{1,17},{9,25},{17,1},{25,9},{2,18},{10... | collective-permute-start | bytes 11528 | tf_op jit(solution)/shard_map/ppermute | solution.py:502
  152.4 4.7 %collective-permute-start.22 = (f32[4,240]{1,0:T(4,128)}, f32[4,240]{1,0:T(4,128)S(1)}, u32[]{:S(2)}, u32[]{:S(2)}) collective-permute-start(f32[4,240]{1,0:T(4,128)} %shard_map.130), channel_id=1, source_target_pairs={{0,17},{1,16},{2,19},{3,18},{4,21},{5,20},{6,23},{7,22},{8,25},{9,... | collective-permute-start | bytes 11528 | tf_op jit(solution)/shard_map/ppermute | solution.py:669
  153.9 3.8 %collective-permute-start.21 = (f32[4,240]{1,0:T(4,128)}, f32[4,240]{1,0:T(4,128)S(1)}, u32[]{:S(2)}, u32[]{:S(2)}) collective-permute-start(f32[4,240]{1,0:T(4,128)} %get-tuple-element.37), channel_id=1, source_target_pairs={{0,1},{1,0},{2,3},{3,2},{4,5},{5,4},{6,7},{7,6},{8,9},{9,8},{10,11... | collective-permute-start | bytes 11528 | tf_op jit(solution)/shard_map/ppermute | solution.py:514
  158.4 5.5 %collective-permute-start.23 = (f32[4,240]{1,0:T(4,128)S(1)}, f32[4,240]{1,0:T(4,128)S(1)}, u32[]{:S(2)}, u32[]{:S(2)}) collective-permute-start(f32[4,240]{1,0:T(4,128)S(1)} %add_add_fusion.1), channel_id=1, source_target_pairs={{0,2},{1,3},{2,4},{3,5},{4,6},{5,7},{6,0},{7,1},{8,10},{9,11},{10,... | collective-permute-start | bytes 11528 | tf_op jit(solution)/shard_map/ppermute | solution.py:510
  159.6 4.5 %collective-permute-start.24 = (f32[4,240]{1,0:T(4,128)S(1)}, f32[4,240]{1,0:T(4,128)S(1)}, u32[]{:S(2)}, u32[]{:S(2)}) collective-permute-start(f32[4,240]{1,0:T(4,128)S(1)} %add_add_fusion.1), channel_id=1, source_target_pairs={{0,4},{1,5},{2,6},{3,7},{4,0},{5,1},{6,2},{7,3},{8,12},{9,13},{10,... | collective-permute-start | bytes 11528 | tf_op jit(solution)/shard_map/ppermute | solution.py:510
  162.2 3.6 %collective-permute-start.25 = (f32[4,240]{1,0:T(4,128)S(1)}, f32[4,240]{1,0:T(4,128)S(1)}, u32[]{:S(2)}, u32[]{:S(2)}) collective-permute-start(f32[4,240]{1,0:T(4,128)S(1)} %add_add_fusion.1), channel_id=1, source_target_pairs={{0,6},{1,7},{2,0},{3,1},{4,2},{5,3},{6,4},{7,5},{8,14},{9,15},{10,... | collective-permute-start | bytes 11528 | tf_op jit(solution)/shard_map/ppermute | solution.py:510

commit v5 on v4

--- a/solution.py
+++ b/solution.py
@@ -143,6 +143,11 @@
         far_lines, far_cols = add_small(blocks[1]), add_small(blocks[2])
         block_refs = {n: [(add(array, pltpu.HBM), place) for array, place in blocks[0][n][1]] for n in used_blocks}
         copies += sum(len(refs) for refs in block_refs.values())
+    sums_at = {}
+    for mine, used, height in ((True, used_tiles, tile), (False, used_blocks, block_rows)):
+        if used:
+            sums_at[mine] = len(scratch)
+            scratch.append(pltpu.VMEM((len(used) * height, 128), F32))
     readout_at = add_small(readout)
     carry = [
         (out, add_small(value)) for out, value in zip((own_out, block_out), carried) if out is not None and value is not None
@@ -204,6 +209,16 @@
             copy.wait()
         for out, place in carry:
             outs[out][...] = held[place][...]
+        summed = set()
+
+        def add_line(mine, row, line):
+            if not mine:
+                outs[block_out][pl.ds(row, 1), :] += line
+                return
+            for k in range(tile // block_rows):
+                at_row = row * (tile // block_rows) + k
+                outs[own_out][at_row : at_row + 1, :] += line[:, k * block_rows : (k + 1) * block_rows]
+
         for number, part in enumerate(parts):
             for key in keys(part):
                 for copy in pending[key]:
@@ -238,21 +253,31 @@
                     (((0,), (0,)), ((), ())),
                     preferred_element_type=F32,
                 )
-                line = 0.0
+                folded, lone = None, None
                 for j in range(first, last):
                     start, size, _ = chunks[j]
                     lane = lane_at[j] - lane_at[first]
                     gate, up = part_total[:, lane : lane + size], part_total[:, lane + size : lane + 2 * size]
                     value = gate / (1.0 + jnp.exp(-gate)) * up * readout_ref[:, start : start + size]
                     if size % 128 == 0:
-                        value = sum(value[:, k : k + 128] for k in range(0, size, 128))
-                    line += jnp.sum(value.T, axis=0, keepdims=True)
-                if mine:
-                    for k in range(tile // block_rows):
-                        at_row = row * (tile // block_rows) + k
-                        outs[own_out][at_row : at_row + 1, :] += line[:, k * block_rows : (k + 1) * block_rows]
-                else:
-                    outs[block_out][pl.ds(row, 1), :] += line
+                        for k in range(0, size, 128):
+                            block = value[:, k : k + 128]
+                            folded = block if folded is None else folded + block
+                    else:
+                        line = jnp.sum(value.T, axis=0, keepdims=True)
+                        lone = line if lone is None else lone + line
+                if folded is not None:
+                    there = held[sums_at[mine]].at[(at + t) * height : (at + t + 1) * height, :]
+                    key = (mine, begin + t)
+                    there[...] = folded + there[...] if key in summed else folded
+                    summed.add(key)
+                if lone is not None:
+                    add_line(mine, row, lone)
+        for mine, n in sorted(summed):
+            height, used = (tile, used_tiles) if mine else (block_rows, used_blocks)
+            value = held[sums_at[mine]][used.index(n) * height : (used.index(n) + 1) * height, :]
+            row = n if mine else ids_ref[blocks[0][n][0]]
+            add_line(mine, row, jnp.sum(value.T, axis=0, keepdims=True))
 
     results = pl.pallas_call(
         kernel,

time: 167 us -> 167 us (level)
  transfers between devices with their start and end apart: 26 -> 26, of which waited for: 15 -> 16; matrix products, arithmetic and copies ran while one was open for 6% -> 6% of each run, Pallas kernels for 42% -> 41%
where the time goes in v5:
time: 167 us; the launch traced here: 166 us
  Pallas kernels  78.4 us (47%)
  waiting for transfers between devices  41.3 us (25%)
  starting transfers between devices  34.6 us (21%)
  other arithmetic  5.9 us (4%)
  local copies, waits for them, and re-layouts  5.55 us (3%)
    pallas_call x4, Pallas kernels, gated_scores(): pl.pallas_call(kernel, out_shape=shapes, in_specs=specs, out_specs=[pl.Bl...  58.9 us
    ppermute x6, waiting for transfers between devices, across(): return lax.ppermute(value, 'pop', across_pairs)  19.4 us
    ppermute x8, starting transfers between devices, outer_permute(): lax.ppermute(value, 'shard', [(s, z * inner + y) for s, z, y in pairs if...  17.4 us
    ppermute x8, waiting for transfers between devices, outer_permute(): lax.ppermute(value, 'shard', [(s, z * inner + y) for s, z, y in pairs if...  10.6 us
    ppermute x6, starting transfers between devices, across(): return lax.ppermute(value, 'pop', across_pairs)  9.54 us
    pallas_call x1, Pallas kernels, update_directions(): pl.pallas_call(kernel, grid=(block_rows // step,), out_shape=[jax.ShapeDt...  8.05 us
    pallas_call x1, Pallas kernels, own_factors(): pl.pallas_call(kernel, out_shape=[jax.ShapeDtypeStruct((lines, hidden + b...  6.23 us
    ppermute x5, waiting for transfers between devices, inner_permute(): lax.ppermute(value, 'shard', [(s, z * inner + y) for s, z, y in pairs if...  5.62 us
  transfers between devices with their start and end apart: 26, of which 16 were waited for; matrix products, arithmetic and copies ran while one was open for 6% of the time, Pallas kernels for 41%

profile of v5, /device:TPU:0, one launch (start us, length us, event | category | flops | bytes accessed | tf_op | source)
XLA Modules:
  0.0 166.5 jit_solution(15351952623451459080)
XLA Ops:
  0.6 0.5 collective-permute-start
  1.2 2.2 %dynamic_slice.6.waited_ref = bf16[240,2048]{1,0:T(8,128)(2,1)} dynamic-slice(bf16[960,4096]{1,0:T(8,128)(2,1)} %bitcast.19, s32[]{:T(128)S(6)} %select_n.100, s32[]{:T(128)S(6)} %select_n.101), dynamic_slice_sizes={240,2048} | dynamic-slice | bytes 1966084 | tf_op jit(solution)/shard_map/dynamic_slice | solution.py:543
  3.5 2.9 %collective-permute-start.3 = (bf16[240,2048]{1,0:T(8,128)(2,1)}, bf16[240,2048]{1,0:T(8,128)(2,1)}, u32[]{:S(2)}, u32[]{:S(2)}) collective-permute-start(bf16[240,2048]{1,0:T(8,128)(2,1)} %dynamic_slice.6.waited_ref), channel_id=1, source_target_pairs={{0,16},{8,24},{16,0},{24,8},{1,17},{9,25},{17,1},{25,9},{2,18},{10... | collective-permute-start | bytes 2949128 | tf_op jit(solution)/shard_map/ppermute | solution.py:527
  6.4 0.7 pad_add_fusion.starts_ref
  7.0 6.2 %shard_map.112 = (bf16[16,5408]{1,0:T(8,128)(2,1)}, bf16[2,48,480]{2,1,0:T(8,128)(2,1)}, bf16[48,1792]{1,0:T(8,128)(2,1)}) custom-call(s32[2]{0:T(128)} %pad_add_fusion.starts_ref, bf16[2,480,4096]{2,1,0:T(8,128)(2,1)} %refs_11_.1, bf16[2,4,4096]{2,1,0:T(4,128)(2,1)} %ag.3, bf16[2,4,4096]{2,1,0:T(4,128)(2,1)} %au.3, bf16[2,4,1792]{2,1,0:T(4,128)(2,1)} %gc.1, ...), custom_call_target="tpu_custom_call" | custom-call | flops 1 | bytes 1 | tf_op jit(solution)/shard_map/pallas_call | solution.py:358
  13.3 3.3 %shard_map.113 = (bf16[1024,512]{1,0:T(8,128)(2,1)}, bf16[1024,768]{1,0:T(8,128)(2,1)}, bf16[1024,512]{1,0:T(8,128)(2,1)}) custom-call(s32[1]{0:T(128)} %bitcast.11.shift_ref, bf16[1024,1792]{1,0:T(8,128)(2,1)} %refs_1_.7, bf16[1024,1792]{1,0:T(8,128)(2,1)} %refs_2_.7, bf16[16,5408]{1,0:T(8,128)(2,1)} %get-tuple-element.21.waited_ref.own_ref), custom_call_target="tpu_custom_call" | custom-call | flops 1 | bytes 1 | tf_op jit(solution)/shard_map/pallas_call | solution.py:485
  16.6 2.1 %collective-permute-start.2 = (bf16[1024,512]{1,0:T(8,128)(2,1)}, bf16[1024,512]{1,0:T(8,128)(2,1)}, u32[]{:S(2)}, u32[]{:S(2)}) collective-permute-start(bf16[1024,512]{1,0:T(8,128)(2,1)} %get-tuple-element.22.refs_2_), channel_id=1, source_target_pairs={{0,16},{8,24},{16,0},{24,8},{1,17},{9,25},{17,1},{25,9},{2,18},{10... | collective-permute-start | bytes 3145736 | tf_op jit(solution)/shard_map/ppermute | solution.py:527
  18.7 14.3 %collective-permute-done.4.refs_1_.bundle_ref = bf16[16,5408]{1,0:T(8,128)(2,1)} collective-permute-done((bf16[16,5408]{1,0:T(8,128)(2,1)}, bf16[16,5408]{1,0:T(8,128)(2,1)}, u32[]{:S(2)}, u32[]{:S(2)}) %collective-permute-start.4) | collective-permute-done | bytes 173088 | tf_op jit(solution)/shard_map/ppermute | solution.py:527
  33.1 2.2 %collective-permute-start.5 = (bf16[240,2048]{1,0:T(8,128)(2,1)}, bf16[240,2048]{1,0:T(8,128)(2,1)}, u32[]{:S(2)}, u32[]{:S(2)}) collective-permute-start(bf16[240,2048]{1,0:T(8,128)(2,1)} %shard_map.114.refs_12_.refs_14_.refs_16_), channel_id=1, source_target_pairs={{0,2},{1,3},{2,0},{3,1},{4,6},{5,7},{6,4},{7,5},{8,10},{9,11},{10,... | collective-permute-start | bytes 2949128 | tf_op jit(solution)/shard_map/ppermute | solution.py:535
  35.3 1.5 collective-permute-start.7
  36.8 1.6 collective-permute-start.10
  38.4 0.7 stack.81.starts_ref
  39.1 2.0 %shard_map.115 = (bf16[4,48,240]{2,1,0:T(8,128)(2,1)}, bf16[48,1792]{1,0:T(8,128)(2,1)}, bf16[32,2944]{1,0:T(8,128)(2,1)}, bf16[32,2944]{1,0:T(8,128)(2,1)}) custom-call(s32[5]{0:T(128)} %stack.81.starts_ref, bf16[16,5408]{1,0:T(8,128)(2,1)} %collective-permute-done.4.refs_1_.bundle_ref, bf16[16,5408]{1,0:T(8,128)(2,1)} %get-tuple-element.21.waited_ref.own_ref, ...), custom_call_target="tpu_custom_call" | custom-call | flops 1 | bytes 1 | tf_op jit(solution)/shard_map/pallas_call | solution.py:412
  41.0 1.8 %collective-permute-done.6.refs_1_.refs_2_ = bf16[32,2944]{1,0:T(8,128)(2,1)} collective-permute-done((bf16[32,2944]{1,0:T(8,128)(2,1)}, bf16[32,2944]{1,0:T(8,128)(2,1)}, u32[]{:S(2)}, u32[]{:S(2)}) %collective-permute-start.6) | collective-permute-done | bytes 188448 | tf_op jit(solution)/shard_map/ppermute | solution.py:531
  42.8 1.5 collective-permute-start.9
  44.3 8.0 %shard_map.116 = (f32[1024,1792]{1,0:T(8,128)}, f32[1024,1792]{1,0:T(8,128)}) custom-call(bf16[32,2944]{1,0:T(8,128)(2,1)} %get-tuple-element.25.refs_0_.refs_1_, bf16[32,2944]{1,0:T(8,128)(2,1)} %collective-permute-done.6.refs_1_.refs_2_), custom_call_target="tpu_custom_call" | custom-call | flops 1 | bytes 1 | tf_op jit(solution)/shard_map/pallas_call | solution.py:446
  52.3 3.8 %collective-permute-done.5.refs_0_ = bf16[240,2048]{1,0:T(8,128)(2,1)} collective-permute-done((bf16[240,2048]{1,0:T(8,128)(2,1)}, bf16[240,2048]{1,0:T(8,128)(2,1)}, u32[]{:S(2)}, u32[]{:S(2)}) %collective-permute-start.5) | collective-permute-done | bytes 983072 | tf_op jit(solution)/shard_map/ppermute | solution.py:535
  56.1 1.2 collective-permute-done.7.refs_2_.refs_13_.refs_15_.refs_17_
  57.3 4.5 %collective-permute-start.11 = (bf16[240,2048]{1,0:T(8,128)(2,1)}, bf16[240,2048]{1,0:T(8,128)(2,1)}, u32[]{:S(2)}, u32[]{:S(2)}) collective-permute-start(bf16[240,2048]{1,0:T(8,128)(2,1)} %shard_map.120), channel_id=1, source_target_pairs={{0,2},{1,3},{2,0},{3,1},{4,6},{5,7},{6,4},{7,5},{8,10},{9,11},{10,... | collective-permute-start | bytes 2949128 | tf_op jit(solution)/shard_map/ppermute | solution.py:535
  61.9 0.5 collective-permute-start.12
  62.4 0.8 dynamic_slice.7
  63.2 0.6 broadcast_in_dim.7.refs_14_.refs_18_.refs_22_.refs_15_
  63.7 0.6 stack.73.refs_0_
  64.3 1.6 collective-permute-start.15
  66.0 11.3 %shard_map.121 = (f32[4,240]{1,0:T(4,128)}, f32[4,240]{1,0:T(4,128)}) custom-call(s32[11]{0:T(128)} %stack.73.refs_0_, bf16[1024,1792]{1,0:T(8,128)(2,1)} %refs_1_.7, bf16[1024,1792]{1,0:T(8,128)(2,1)} %refs_2_.7, bf16[1024,1792]{1,0:T(8,128)(2,1)} %collective-permute-done.refs_5_.refs_3_, bf16[1024,1792]{1,0:T(8,128)(2,1)} %collective-permute-done.1.refs_6_.refs_4_, ...), custom_call_target="tpu_custom_call" | custom-call | flops 1 | bytes 1 | tf_op jit(solution)/shard_map/pallas_call | solution.py:282
  77.3 4.5 %collective-permute-done.11.refs_0_ = bf16[240,2048]{1,0:T(8,128)(2,1)} collective-permute-done((bf16[240,2048]{1,0:T(8,128)(2,1)}, bf16[240,2048]{1,0:T(8,128)(2,1)}, u32[]{:S(2)}, u32[]{:S(2)}) %collective-permute-start.11) | collective-permute-done | bytes 983072 | tf_op jit(solution)/shard_map/ppermute | solution.py:535
  81.8 2.3 %broadcast_select_fusion.1.refs_1_.refs_20_ = bf16[240,2048]{1,0:T(8,128)(2,1)} fusion(bf16[240,2048]{1,0:T(8,128)(2,1)} %shard_map.122, bf16[240,2048]{1,0:T(8,128)(2,1)} %shard_map.120, pred[]{:T(512)S(6)} %or.3), kind=kLoop, calls=%fused_computation.1 | loop fusion | flops 491520 | bytes 2949121 | tf_op jit(solution)/shard_map/jit(_where)/select_n | solution.py:62
  84.1 4.5 %collective-permute-done.9.refs_0_ = bf16[1024,768]{1,0:T(8,128)(2,1)} collective-permute-done((bf16[1024,768]{1,0:T(8,128)(2,1)}, bf16[1024,768]{1,0:T(8,128)(2,1)}, u32[]{:S(2)}, u32[]{:S(2)}) %collective-permute-start.9) | collective-permute-done | bytes 1572896 | tf_op jit(solution)/shard_map/ppermute | solution.py:527
  88.7 1.9 %collective-permute-start.16 = (bf16[240,2048]{1,0:T(8,128)(2,1)}, bf16[240,2048]{1,0:T(8,128)(2,1)}, u32[]{:S(2)}, u32[]{:S(2)}) collective-permute-start(bf16[240,2048]{1,0:T(8,128)(2,1)} %shard_map.125), channel_id=1, source_target_pairs={{0,2},{1,3},{2,0},{3,1},{4,6},{5,7},{6,4},{7,5},{8,10},{9,11},{10,... | collective-permute-start | bytes 2949128 | tf_op jit(solution)/shard_map/ppermute | solution.py:535
  90.6 1.5 collective-permute-start.14
  92.1 1.5 collective-permute-start.17
  93.6 19.2 %shard_map.126 = (f32[4,240]{1,0:T(4,128)}, f32[4,240]{1,0:T(4,128)}) custom-call(s32[11]{0:T(128)} %stack.73.refs_0_, bf16[1024,1792]{1,0:T(8,128)(2,1)} %refs_1_.7, bf16[1024,1792]{1,0:T(8,128)(2,1)} %refs_2_.7, bf16[1024,1792]{1,0:T(8,128)(2,1)} %collective-permute-done.refs_5_.refs_3_, bf16[1024,1792]{1,0:T(8,128)(2,1)} %collective-permute-done.1.refs_6_.refs_4_, ...), custom_call_target="tpu_custom_call" | custom-call | flops 1 | bytes 1 | tf_op jit(solution)/shard_map/pallas_call | solution.py:282
  113.2 2.3 %broadcast_select_fusion.refs_1_.refs_13_ = bf16[240,2048]{1,0:T(8,128)(2,1)} fusion(bf16[240,2048]{1,0:T(8,128)(2,1)} %shard_map.127, bf16[240,2048]{1,0:T(8,128)(2,1)} %shard_map.125, pred[]{:T(512)S(6)} %or.3), kind=kLoop, calls=%fused_computation | loop fusion | flops 491520 | bytes 2949121 | tf_op jit(solution)/shard_map/jit(_where)/select_n | solution.py:65
  116.1 1.5 collective-permute-start.19
  117.6 1.5 collective-permute-done.18.refs_10_
  119.1 18.1 %shard_map.129 = (f32[4,240]{1,0:T(4,128)}, f32[4,240]{1,0:T(4,128)}) custom-call(s32[11]{0:T(128)} %stack.73.refs_0_, bf16[1024,1792]{1,0:T(8,128)(2,1)} %refs_1_.7, bf16[1024,1792]{1,0:T(8,128)(2,1)} %refs_2_.7, bf16[1024,1792]{1,0:T(8,128)(2,1)} %collective-permute-done.refs_5_.refs_3_, bf16[1024,1792]{1,0:T(8,128)(2,1)} %collective-permute-done.1.refs_6_.refs_4_, ...), custom_call_target="tpu_custom_call" | custom-call | flops 1 | bytes 1 | tf_op jit(solution)/shard_map/pallas_call | solution.py:282
  137.2 3.4 %collective-permute-done.19.refs_14_ = bf16[240,2048]{1,0:T(8,128)(2,1)} collective-permute-done((bf16[240,2048]{1,0:T(8,128)(2,1)}, bf16[240,2048]{1,0:T(8,128)(2,1)}, u32[]{:S(2)}, u32[]{:S(2)}) %collective-permute-start.19) | collective-permute-done | bytes 983072 | tf_op jit(solution)/shard_map/ppermute | solution.py:539
  140.6 10.2 %shard_map.130 = f32[4,240]{1,0:T(4,128)} custom-call(s32[11]{0:T(128)} %stack.73.refs_0_, bf16[1024,1792]{1,0:T(8,128)(2,1)} %refs_1_.7, bf16[1024,1792]{1,0:T(8,128)(2,1)} %refs_2_.7, bf16[1024,1792]{1,0:T(8,128)(2,1)} %collective-permute-done.refs_5_.refs_3_, bf16[1024,1792]{1,0:T(8,128)(2,1)} %collective-permute-done.1.refs_6_.refs_4_, ...), custom_call_target="tpu_custom_call" | custom-call | flops 1 | bytes 1 | tf_op jit(solution)/shard_map/pallas_call | solution.py:282
  150.8 1.6 collective-permute-start.20
  152.4 1.5 collective-permute-start.22
  154.7 2.4 %collective-permute-done.22 = f32[4,240]{1,0:T(4,128)S(1)} collective-permute-done((f32[4,240]{1,0:T(4,128)}, f32[4,240]{1,0:T(4,128)S(1)}, u32[]{:S(2)}, u32[]{:S(2)}) %collective-permute-start.22) | collective-permute-done | bytes 3872 | tf_op jit(solution)/shard_map/ppermute | solution.py:694
  157.1 0.6 collective-permute-done.21
  157.7 0.7 add_add_fusion.1
  158.4 1.2 collective-permute-start.23
  159.6 2.6 %collective-permute-start.24 = (f32[4,240]{1,0:T(4,128)S(1)}, f32[4,240]{1,0:T(4,128)S(1)}, u32[]{:S(2)}, u32[]{:S(2)}) collective-permute-start(f32[4,240]{1,0:T(4,128)S(1)} %add_add_fusion.1), channel_id=1, source_target_pairs={{0,4},{1,5},{2,6},{3,7},{4,0},{5,1},{6,2},{7,3},{8,12},{9,13},{10,... | collective-permute-start | bytes 11528 | tf_op jit(solution)/shard_map/ppermute | solution.py:535
  162.2 1.7 %collective-permute-start.25 = (f32[4,240]{1,0:T(4,128)S(1)}, f32[4,240]{1,0:T(4,128)S(1)}, u32[]{:S(2)}, u32[]{:S(2)}) collective-permute-start(f32[4,240]{1,0:T(4,128)S(1)} %add_add_fusion.1), channel_id=1, source_target_pairs={{0,6},{1,7},{2,0},{3,1},{4,2},{5,3},{6,4},{7,5},{8,14},{9,15},{10,... | collective-permute-start | bytes 11528 | tf_op jit(solution)/shard_map/ppermute | solution.py:535
  164.1 1.7 %collective-permute-done.25 = f32[4,240]{1,0:T(4,128)S(1)} collective-permute-done((f32[4,240]{1,0:T(4,128)S(1)}, f32[4,240]{1,0:T(4,128)S(1)}, u32[]{:S(2)}, u32[]{:S(2)}) %collective-permute-start.25) | collective-permute-done | bytes 3872 | tf_op jit(solution)/shard_map/ppermute | solution.py:535
  165.8 0.7 reshape.13
  (34 shorter events, 2.2 us)
Async XLA Ops:
  0.6 32.4 %collective-permute-start = (bf16[1024,1792]{1,0:T(8,128)(2,1)}, bf16[1024,1792]{1,0:T(8,128)(2,1)}, u32[]{:S(2)}, u32[]{:S(2)}) collective-permute-start(bf16[1024,1792]{1,0:T(8,128)(2,1)} %refs_1_.7), channel_id=1, source_target_pairs={{0,8},{8,0},{16,24},{24,16},{1,9},{9,1},{17,25},{25,17},{2,10},{10... | collective-permute-start | bytes 11010056 | tf_op jit(solution)/shard_map/ppermute | solution.py:531
  1.1 31.9 %collective-permute-start.1 = (bf16[1024,1792]{1,0:T(8,128)(2,1)}, bf16[1024,1792]{1,0:T(8,128)(2,1)}, u32[]{:S(2)}, u32[]{:S(2)}) collective-permute-start(bf16[1024,1792]{1,0:T(8,128)(2,1)} %refs_2_.7), channel_id=1, source_target_pairs={{0,8},{8,0},{16,24},{24,16},{1,9},{9,1},{17,25},{25,17},{2,10},{10... | collective-permute-start | bytes 11010056 | tf_op jit(solution)/shard_map/ppermute | solution.py:531
  3.5 29.6 %collective-permute-start.3 = (bf16[240,2048]{1,0:T(8,128)(2,1)}, bf16[240,2048]{1,0:T(8,128)(2,1)}, u32[]{:S(2)}, u32[]{:S(2)}) collective-permute-start(bf16[240,2048]{1,0:T(8,128)(2,1)} %dynamic_slice.6.waited_ref), channel_id=1, source_target_pairs={{0,16},{8,24},{16,0},{24,8},{1,17},{9,25},{17,1},{25,9},{2,18},{10... | collective-permute-start | bytes 2949128 | tf_op jit(solution)/shard_map/ppermute | solution.py:527
  13.3 19.8 %collective-permute-start.4 = (bf16[16,5408]{1,0:T(8,128)(2,1)}, bf16[16,5408]{1,0:T(8,128)(2,1)}, u32[]{:S(2)}, u32[]{:S(2)}) collective-permute-start(bf16[16,5408]{1,0:T(8,128)(2,1)} %get-tuple-element.21.waited_ref.own_ref), channel_id=1, source_target_pairs={{0,16},{8,24},{16,0},{24,8},{1,17},{9,25},{17,1},{25,9},{2,18},{10... | collective-permute-start | bytes 519176 | tf_op jit(solution)/shard_map/ppermute | solution.py:527
  16.6 39.5 %collective-permute-start.2 = (bf16[1024,512]{1,0:T(8,128)(2,1)}, bf16[1024,512]{1,0:T(8,128)(2,1)}, u32[]{:S(2)}, u32[]{:S(2)}) collective-permute-start(bf16[1024,512]{1,0:T(8,128)(2,1)} %get-tuple-element.22.refs_2_), channel_id=1, source_target_pairs={{0,16},{8,24},{16,0},{24,8},{1,17},{9,25},{17,1},{25,9},{2,18},{10... | collective-permute-start | bytes 3145736 | tf_op jit(solution)/shard_map/ppermute | solution.py:527
  33.1 23.1 %collective-permute-start.5 = (bf16[240,2048]{1,0:T(8,128)(2,1)}, bf16[240,2048]{1,0:T(8,128)(2,1)}, u32[]{:S(2)}, u32[]{:S(2)}) collective-permute-start(bf16[240,2048]{1,0:T(8,128)(2,1)} %shard_map.114.refs_12_.refs_14_.refs_16_), channel_id=1, source_target_pairs={{0,2},{1,3},{2,0},{3,1},{4,6},{5,7},{6,4},{7,5},{8,10},{9,11},{10,... | collective-permute-start | bytes 2949128 | tf_op jit(solution)/shard_map/ppermute | solution.py:535
  35.3 22.1 %collective-permute-start.7 = (bf16[240,2048]{1,0:T(8,128)(2,1)}, bf16[240,2048]{1,0:T(8,128)(2,1)}, u32[]{:S(2)}, u32[]{:S(2)}) collective-permute-start(bf16[240,2048]{1,0:T(8,128)(2,1)} %shard_map.114.refs_12_.refs_14_.refs_16_), channel_id=1, source_target_pairs={{0,1},{1,0},{2,3},{3,2},{4,5},{5,4},{6,7},{7,6},{8,9},{9,8},{10,11... | collective-permute-start | bytes 2949128 | tf_op jit(solution)/shard_map/ppermute | solution.py:539
  36.8 20.6 %collective-permute-start.10 = (bf16[240,2048]{1,0:T(8,128)(2,1)}, bf16[240,2048]{1,0:T(8,128)(2,1)}, u32[]{:S(2)}, u32[]{:S(2)}) collective-permute-start(bf16[240,2048]{1,0:T(8,128)(2,1)} %shard_map.114.refs_12_.refs_14_.refs_16_), channel_id=1, source_target_pairs={{2,4},{3,5},{4,2},{5,3},{10,12},{11,13},{12,10},{13,11},{18,20},{1... | collective-permute-start | bytes 2949128 | tf_op jit(solution)/shard_map/ppermute | solution.py:535
  41.0 1.8 %collective-permute-start.6 = (bf16[32,2944]{1,0:T(8,128)(2,1)}, bf16[32,2944]{1,0:T(8,128)(2,1)}, u32[]{:S(2)}, u32[]{:S(2)}) collective-permute-start(bf16[32,2944]{1,0:T(8,128)(2,1)} %get-tuple-element.26), channel_id=1, source_target_pairs={{0,8},{8,0},{16,24},{24,16},{1,9},{9,1},{17,25},{25,17},{2,10},{10... | collective-permute-start | bytes 565256 | tf_op jit(solution)/shard_map/ppermute | solution.py:531
  42.8 45.8 %collective-permute-start.9 = (bf16[1024,768]{1,0:T(8,128)(2,1)}, bf16[1024,768]{1,0:T(8,128)(2,1)}, u32[]{:S(2)}, u32[]{:S(2)}) collective-permute-start(bf16[1024,768]{1,0:T(8,128)(2,1)} %shard_map.119), channel_id=1, source_target_pairs={{0,16},{8,24},{16,0},{24,8},{1,17},{9,25},{17,1},{25,9},{2,18},{10... | collective-permute-start | bytes 4718600 | tf_op jit(solution)/shard_map/ppermute | solution.py:527
  57.3 8.6 %collective-permute-start.8 = (bf16[1024,512]{1,0:T(8,128)(2,1)}, bf16[1024,512]{1,0:T(8,128)(2,1)}, u32[]{:S(2)}, u32[]{:S(2)}) collective-permute-start(bf16[1024,512]{1,0:T(8,128)(2,1)} %shard_map.118.refs_5_.refs_1_), channel_id=1, source_target_pairs={{0,8},{8,0},{16,24},{24,16},{1,9},{9,1},{17,25},{25,17},{2,10},{10... | collective-permute-start | bytes 3145736 | tf_op jit(solution)/shard_map/ppermute | solution.py:531
  57.3 24.5 %collective-permute-start.11 = (bf16[240,2048]{1,0:T(8,128)(2,1)}, bf16[240,2048]{1,0:T(8,128)(2,1)}, u32[]{:S(2)}, u32[]{:S(2)}) collective-permute-start(bf16[240,2048]{1,0:T(8,128)(2,1)} %shard_map.120), channel_id=1, source_target_pairs={{0,2},{1,3},{2,0},{3,1},{4,6},{5,7},{6,4},{7,5},{8,10},{9,11},{10,... | collective-permute-start | bytes 2949128 | tf_op jit(solution)/shard_map/ppermute | solution.py:535
  61.9 26.8 %collective-permute-start.12 = (bf16[240,2048]{1,0:T(8,128)(2,1)}, bf16[240,2048]{1,0:T(8,128)(2,1)}, u32[]{:S(2)}, u32[]{:S(2)}) collective-permute-start(bf16[240,2048]{1,0:T(8,128)(2,1)} %shard_map.117.refs_1_.refs_16_.refs_18_), channel_id=1, source_target_pairs={{0,1},{1,0},{2,3},{3,2},{4,5},{5,4},{6,7},{7,6},{8,9},{9,8},{10,11... | collective-permute-start | bytes 2949128 | tf_op jit(solution)/shard_map/ppermute | solution.py:539
  64.3 24.3 %collective-permute-start.15 = (bf16[240,2048]{1,0:T(8,128)(2,1)}, bf16[240,2048]{1,0:T(8,128)(2,1)}, u32[]{:S(2)}, u32[]{:S(2)}) collective-permute-start(bf16[240,2048]{1,0:T(8,128)(2,1)} %shard_map.117.refs_1_.refs_16_.refs_18_), channel_id=1, source_target_pairs={{2,4},{3,5},{4,2},{5,3},{10,12},{11,13},{12,10},{13,11},{18,20},{1... | collective-permute-start | bytes 2949128 | tf_op jit(solution)/shard_map/ppermute | solution.py:535
  88.7 4.9 %collective-permute-start.13 = (bf16[1024,768]{1,0:T(8,128)(2,1)}, bf16[1024,768]{1,0:T(8,128)(2,1)}, u32[]{:S(2)}, u32[]{:S(2)}) collective-permute-start(bf16[1024,768]{1,0:T(8,128)(2,1)} %shard_map.123.refs_7_), channel_id=1, source_target_pairs={{0,8},{8,0},{16,24},{24,16},{1,9},{9,1},{17,25},{25,17},{2,10},{10... | collective-permute-start | bytes 4718600 | tf_op jit(solution)/shard_map/ppermute | solution.py:531
  88.7 24.6 %collective-permute-start.16 = (bf16[240,2048]{1,0:T(8,128)(2,1)}, bf16[240,2048]{1,0:T(8,128)(2,1)}, u32[]{:S(2)}, u32[]{:S(2)}) collective-permute-start(bf16[240,2048]{1,0:T(8,128)(2,1)} %shard_map.125), channel_id=1, source_target_pairs={{0,2},{1,3},{2,0},{3,1},{4,6},{5,7},{6,4},{7,5},{8,10},{9,11},{10,... | collective-permute-start | bytes 2949128 | tf_op jit(solution)/shard_map/ppermute | solution.py:535
  90.6 25.5 %collective-permute-start.14 = (bf16[1024,512]{1,0:T(8,128)(2,1)}, bf16[1024,512]{1,0:T(8,128)(2,1)}, u32[]{:S(2)}, u32[]{:S(2)}) collective-permute-start(bf16[1024,512]{1,0:T(8,128)(2,1)} %shard_map.124), channel_id=1, source_target_pairs={{0,16},{8,24},{16,0},{24,8},{1,17},{9,25},{17,1},{25,9},{2,18},{10... | collective-permute-start | bytes 3145736 | tf_op jit(solution)/shard_map/ppermute | solution.py:527
  92.1 23.9 %collective-permute-start.17 = (bf16[240,2048]{1,0:T(8,128)(2,1)}, bf16[240,2048]{1,0:T(8,128)(2,1)}, u32[]{:S(2)}, u32[]{:S(2)}) collective-permute-start(bf16[240,2048]{1,0:T(8,128)(2,1)} %broadcast_select_fusion.1.refs_1_.refs_20_), channel_id=1, source_target_pairs={{0,1},{1,0},{2,3},{3,2},{4,5},{5,4},{6,7},{7,6},{8,9},{9,8},{10,11... | collective-permute-start | bytes 2949128 | tf_op jit(solution)/shard_map/ppermute | solution.py:539
  116.1 3.0 %collective-permute-start.18 = (bf16[1024,512]{1,0:T(8,128)(2,1)}, bf16[1024,512]{1,0:T(8,128)(2,1)}, u32[]{:S(2)}, u32[]{:S(2)}) collective-permute-start(bf16[1024,512]{1,0:T(8,128)(2,1)} %shard_map.128.refs_9_), channel_id=1, source_target_pairs={{0,8},{8,0},{16,24},{24,16},{1,9},{9,1},{17,25},{25,17},{2,10},{10... | collective-permute-start | bytes 3145736 | tf_op jit(solution)/shard_map/ppermute | solution.py:531
  116.1 24.5 %collective-permute-start.19 = (bf16[240,2048]{1,0:T(8,128)(2,1)}, bf16[240,2048]{1,0:T(8,128)(2,1)}, u32[]{:S(2)}, u32[]{:S(2)}) collective-permute-start(bf16[240,2048]{1,0:T(8,128)(2,1)} %broadcast_select_fusion.refs_1_.refs_13_), channel_id=1, source_target_pairs={{0,1},{1,0},{2,3},{3,2},{4,5},{5,4},{6,7},{7,6},{8,9},{9,8},{10,11... | collective-permute-start | bytes 2949128 | tf_op jit(solution)/shard_map/ppermute | solution.py:539
  150.8 3.9 %collective-permute-start.20 = (f32[4,240]{1,0:T(4,128)}, f32[4,240]{1,0:T(4,128)S(1)}, u32[]{:S(2)}, u32[]{:S(2)}) collective-permute-start(f32[4,240]{1,0:T(4,128)} %shard_map.130), channel_id=1, source_target_pairs={{0,16},{8,24},{16,0},{24,8},{1,17},{9,25},{17,1},{25,9},{2,18},{10... | collective-permute-start | bytes 11528 | tf_op jit(solution)/shard_map/ppermute | solution.py:527
  152.4 4.7 %collective-permute-start.22 = (f32[4,240]{1,0:T(4,128)}, f32[4,240]{1,0:T(4,128)S(1)}, u32[]{:S(2)}, u32[]{:S(2)}) collective-permute-start(f32[4,240]{1,0:T(4,128)} %shard_map.130), channel_id=1, source_target_pairs={{0,17},{1,16},{2,19},{3,18},{4,21},{5,20},{6,23},{7,22},{8,25},{9,... | collective-permute-start | bytes 11528 | tf_op jit(solution)/shard_map/ppermute | solution.py:694
  153.9 3.8 %collective-permute-start.21 = (f32[4,240]{1,0:T(4,128)}, f32[4,240]{1,0:T(4,128)S(1)}, u32[]{:S(2)}, u32[]{:S(2)}) collective-permute-start(f32[4,240]{1,0:T(4,128)} %get-tuple-element.37), channel_id=1, source_target_pairs={{0,1},{1,0},{2,3},{3,2},{4,5},{5,4},{6,7},{7,6},{8,9},{9,8},{10,11... | collective-permute-start | bytes 11528 | tf_op jit(solution)/shard_map/ppermute | solution.py:539
  158.4 5.5 %collective-permute-start.23 = (f32[4,240]{1,0:T(4,128)S(1)}, f32[4,240]{1,0:T(4,128)S(1)}, u32[]{:S(2)}, u32[]{:S(2)}) collective-permute-start(f32[4,240]{1,0:T(4,128)S(1)} %add_add_fusion.1), channel_id=1, source_target_pairs={{0,2},{1,3},{2,4},{3,5},{4,6},{5,7},{6,0},{7,1},{8,10},{9,11},{10,... | collective-permute-start | bytes 11528 | tf_op jit(solution)/shard_map/ppermute | solution.py:535
  159.6 4.5 %collective-permute-start.24 = (f32[4,240]{1,0:T(4,128)S(1)}, f32[4,240]{1,0:T(4,128)S(1)}, u32[]{:S(2)}, u32[]{:S(2)}) collective-permute-start(f32[4,240]{1,0:T(4,128)S(1)} %add_add_fusion.1), channel_id=1, source_target_pairs={{0,4},{1,5},{2,6},{3,7},{4,0},{5,1},{6,2},{7,3},{8,12},{9,13},{10,... | collective-permute-start | bytes 11528 | tf_op jit(solution)/shard_map/ppermute | solution.py:535
  162.2 3.6 %collective-permute-start.25 = (f32[4,240]{1,0:T(4,128)S(1)}, f32[4,240]{1,0:T(4,128)S(1)}, u32[]{:S(2)}, u32[]{:S(2)}) collective-permute-start(f32[4,240]{1,0:T(4,128)S(1)} %add_add_fusion.1), channel_id=1, source_target_pairs={{0,6},{1,7},{2,0},{3,1},{4,2},{5,3},{6,4},{7,5},{8,14},{9,15},{10,... | collective-permute-start | bytes 11528 | tf_op jit(solution)/shard_map/ppermute | solution.py:535

commit v6 on v5

--- a/solution.py
+++ b/solution.py
@@ -686,10 +686,12 @@
     for n in range(outer):
         cuts_at = list(range(done[n], max(done[n], end - 2))) + [max(done[n], end - 2), end]
         rest += [(False, n, n + 1, a, b) for a, b in zip(cuts_at, cuts_at[1:]) if a < b]
+    near_own = [inner_permute(own_total, lambda c, s=s: (c + s) % inner) for s in range(1, inner)]
+    if near_own:
+        other_total = after(other_total, *near_own)
     score(rest)
 
     crossed = across(other_total)
-    near_own = [inner_permute(own_total, lambda c, s=s: (c + s) % inner) for s in range(1, inner)]
     near_other = [
         lax.ppermute(
             other_total,

time: 167 us -> 167 us (level)
  transfers between devices with their start and end apart: 26 -> 26, of which waited for: 16 -> 15; matrix products, arithmetic and copies ran while one was open for 6% -> 6% of each run, Pallas kernels for 41% -> 41%
where the time goes in v6:
time: 167 us
  Pallas kernels  78.4 us (47%)
  waiting for transfers between devices  40.2 us (24%)
  starting transfers between devices  35.7 us (21%)
  other arithmetic  5.93 us (4%)
  local copies, waits for them, and re-layouts  5.55 us (3%)
    pallas_call x4, Pallas kernels, gated_scores(): pl.pallas_call(kernel, out_shape=shapes, in_specs=specs, out_specs=[pl.Bl...  58.9 us
    ppermute x6, waiting for transfers between devices, across(): return lax.ppermute(value, 'pop', across_pairs)  19.9 us
    ppermute x8, starting transfers between devices, outer_permute(): lax.ppermute(value, 'shard', [(s, z * inner + y) for s, z, y in pairs if...  17.4 us
    ppermute x8, waiting for transfers between devices, outer_permute(): lax.ppermute(value, 'shard', [(s, z * inner + y) for s, z, y in pairs if...  10.6 us
    ppermute x6, starting transfers between devices, across(): return lax.ppermute(value, 'pop', across_pairs)  9.54 us
    pallas_call x1, Pallas kernels, update_directions(): pl.pallas_call(kernel, grid=(block_rows // step,), out_shape=[jax.ShapeDt...  8.05 us
    ppermute x5, starting transfers between devices, inner_permute(): lax.ppermute(value, 'shard', [(s, z * inner + y) for s, z, y in pairs if...  6.65 us
    pallas_call x1, Pallas kernels, own_factors(): pl.pallas_call(kernel, out_shape=[jax.ShapeDtypeStruct((lines, hidden + b...  6.23 us
  transfers between devices with their start and end apart: 26, of which 15 were waited for; matrix products, arithmetic and copies ran while one was open for 6% of the time, Pallas kernels for 41%

profile of v6, /device:TPU:0, one launch (start us, length us, event | category | flops | bytes accessed | tf_op | source)
XLA Modules:
  0.0 166.5 jit_solution(3756779269213139981)
XLA Ops:
  0.6 0.5 collective-permute-start
  1.2 2.2 %dynamic_slice.6.waited_ref = bf16[240,2048]{1,0:T(8,128)(2,1)} dynamic-slice(bf16[960,4096]{1,0:T(8,128)(2,1)} %bitcast.19, s32[]{:T(128)S(6)} %select_n.100, s32[]{:T(128)S(6)} %select_n.101), dynamic_slice_sizes={240,2048} | dynamic-slice | bytes 1966084 | tf_op jit(solution)/shard_map/dynamic_slice | solution.py:543
  3.5 2.9 %collective-permute-start.3 = (bf16[240,2048]{1,0:T(8,128)(2,1)}, bf16[240,2048]{1,0:T(8,128)(2,1)}, u32[]{:S(2)}, u32[]{:S(2)}) collective-permute-start(bf16[240,2048]{1,0:T(8,128)(2,1)} %dynamic_slice.6.waited_ref), channel_id=1, source_target_pairs={{0,16},{8,24},{16,0},{24,8},{1,17},{9,25},{17,1},{25,9},{2,18},{10... | collective-permute-start | bytes 2949128 | tf_op jit(solution)/shard_map/ppermute | solution.py:527
  6.4 0.7 pad_add_fusion.starts_ref
  7.0 6.2 %shard_map.112 = (bf16[16,5408]{1,0:T(8,128)(2,1)}, bf16[2,48,480]{2,1,0:T(8,128)(2,1)}, bf16[48,1792]{1,0:T(8,128)(2,1)}) custom-call(s32[2]{0:T(128)} %pad_add_fusion.starts_ref, bf16[2,480,4096]{2,1,0:T(8,128)(2,1)} %refs_11_.1, bf16[2,4,4096]{2,1,0:T(4,128)(2,1)} %ag.3, bf16[2,4,4096]{2,1,0:T(4,128)(2,1)} %au.3, bf16[2,4,1792]{2,1,0:T(4,128)(2,1)} %gc.1, ...), custom_call_target="tpu_custom_call" | custom-call | flops 1 | bytes 1 | tf_op jit(solution)/shard_map/pallas_call | solution.py:358
  13.3 3.3 %shard_map.113 = (bf16[1024,512]{1,0:T(8,128)(2,1)}, bf16[1024,768]{1,0:T(8,128)(2,1)}, bf16[1024,512]{1,0:T(8,128)(2,1)}) custom-call(s32[1]{0:T(128)} %bitcast.11.shift_ref, bf16[1024,1792]{1,0:T(8,128)(2,1)} %refs_1_.7, bf16[1024,1792]{1,0:T(8,128)(2,1)} %refs_2_.7, bf16[16,5408]{1,0:T(8,128)(2,1)} %get-tuple-element.21.waited_ref.own_ref), custom_call_target="tpu_custom_call" | custom-call | flops 1 | bytes 1 | tf_op jit(solution)/shard_map/pallas_call | solution.py:485
  16.6 2.1 %collective-permute-start.2 = (bf16[1024,512]{1,0:T(8,128)(2,1)}, bf16[1024,512]{1,0:T(8,128)(2,1)}, u32[]{:S(2)}, u32[]{:S(2)}) collective-permute-start(bf16[1024,512]{1,0:T(8,128)(2,1)} %get-tuple-element.22.refs_2_), channel_id=1, source_target_pairs={{0,16},{8,24},{16,0},{24,8},{1,17},{9,25},{17,1},{25,9},{2,18},{10... | collective-permute-start | bytes 3145736 | tf_op jit(solution)/shard_map/ppermute | solution.py:527
  18.7 14.3 %collective-permute-done.4.refs_1_.bundle_ref = bf16[16,5408]{1,0:T(8,128)(2,1)} collective-permute-done((bf16[16,5408]{1,0:T(8,128)(2,1)}, bf16[16,5408]{1,0:T(8,128)(2,1)}, u32[]{:S(2)}, u32[]{:S(2)}) %collective-permute-start.4) | collective-permute-done | bytes 173088 | tf_op jit(solution)/shard_map/ppermute | solution.py:527
  33.1 2.2 %collective-permute-start.5 = (bf16[240,2048]{1,0:T(8,128)(2,1)}, bf16[240,2048]{1,0:T(8,128)(2,1)}, u32[]{:S(2)}, u32[]{:S(2)}) collective-permute-start(bf16[240,2048]{1,0:T(8,128)(2,1)} %shard_map.114.refs_12_.refs_14_.refs_16_), channel_id=1, source_target_pairs={{0,2},{1,3},{2,0},{3,1},{4,6},{5,7},{6,4},{7,5},{8,10},{9,11},{10,... | collective-permute-start | bytes 2949128 | tf_op jit(solution)/shard_map/ppermute | solution.py:535
  35.3 1.5 collective-permute-start.7
  36.8 1.6 collective-permute-start.10
  38.4 0.7 stack.81.starts_ref
  39.1 2.0 %shard_map.115 = (bf16[4,48,240]{2,1,0:T(8,128)(2,1)}, bf16[48,1792]{1,0:T(8,128)(2,1)}, bf16[32,2944]{1,0:T(8,128)(2,1)}, bf16[32,2944]{1,0:T(8,128)(2,1)}) custom-call(s32[5]{0:T(128)} %stack.81.starts_ref, bf16[16,5408]{1,0:T(8,128)(2,1)} %collective-permute-done.4.refs_1_.bundle_ref, bf16[16,5408]{1,0:T(8,128)(2,1)} %get-tuple-element.21.waited_ref.own_ref, ...), custom_call_target="tpu_custom_call" | custom-call | flops 1 | bytes 1 | tf_op jit(solution)/shard_map/pallas_call | solution.py:412
  41.0 1.8 %collective-permute-done.6.refs_1_.refs_2_ = bf16[32,2944]{1,0:T(8,128)(2,1)} collective-permute-done((bf16[32,2944]{1,0:T(8,128)(2,1)}, bf16[32,2944]{1,0:T(8,128)(2,1)}, u32[]{:S(2)}, u32[]{:S(2)}) %collective-permute-start.6) | collective-permute-done | bytes 188448 | tf_op jit(solution)/shard_map/ppermute | solution.py:531
  42.8 1.5 collective-permute-start.9
  44.3 8.0 %shard_map.116 = (f32[1024,1792]{1,0:T(8,128)}, f32[1024,1792]{1,0:T(8,128)}) custom-call(bf16[32,2944]{1,0:T(8,128)(2,1)} %get-tuple-element.25.refs_0_.refs_1_, bf16[32,2944]{1,0:T(8,128)(2,1)} %collective-permute-done.6.refs_1_.refs_2_), custom_call_target="tpu_custom_call" | custom-call | flops 1 | bytes 1 | tf_op jit(solution)/shard_map/pallas_call | solution.py:446
  52.3 3.8 %collective-permute-done.5.refs_0_ = bf16[240,2048]{1,0:T(8,128)(2,1)} collective-permute-done((bf16[240,2048]{1,0:T(8,128)(2,1)}, bf16[240,2048]{1,0:T(8,128)(2,1)}, u32[]{:S(2)}, u32[]{:S(2)}) %collective-permute-start.5) | collective-permute-done | bytes 983072 | tf_op jit(solution)/shard_map/ppermute | solution.py:535
  56.1 1.2 collective-permute-done.7.refs_2_.refs_13_.refs_15_.refs_17_
  57.3 4.5 %collective-permute-start.11 = (bf16[240,2048]{1,0:T(8,128)(2,1)}, bf16[240,2048]{1,0:T(8,128)(2,1)}, u32[]{:S(2)}, u32[]{:S(2)}) collective-permute-start(bf16[240,2048]{1,0:T(8,128)(2,1)} %shard_map.120), channel_id=1, source_target_pairs={{0,2},{1,3},{2,0},{3,1},{4,6},{5,7},{6,4},{7,5},{8,10},{9,11},{10,... | collective-permute-start | bytes 2949128 | tf_op jit(solution)/shard_map/ppermute | solution.py:535
  62.4 0.8 dynamic_slice.7
  63.2 0.6 broadcast_in_dim.7.refs_14_.refs_18_.refs_22_.refs_15_
  63.7 0.6 stack.73.refs_0_
  64.3 1.6 collective-permute-start.15
  66.0 11.3 %shard_map.121 = (f32[4,240]{1,0:T(4,128)}, f32[4,240]{1,0:T(4,128)}) custom-call(s32[11]{0:T(128)} %stack.73.refs_0_, bf16[1024,1792]{1,0:T(8,128)(2,1)} %refs_1_.7, bf16[1024,1792]{1,0:T(8,128)(2,1)} %refs_2_.7, bf16[1024,1792]{1,0:T(8,128)(2,1)} %collective-permute-done.refs_5_.refs_3_, bf16[1024,1792]{1,0:T(8,128)(2,1)} %collective-permute-done.1.refs_6_.refs_4_, ...), custom_call_target="tpu_custom_call" | custom-call | flops 1 | bytes 1 | tf_op jit(solution)/shard_map/pallas_call | solution.py:282
  77.3 4.5 %collective-permute-done.11.refs_0_ = bf16[240,2048]{1,0:T(8,128)(2,1)} collective-permute-done((bf16[240,2048]{1,0:T(8,128)(2,1)}, bf16[240,2048]{1,0:T(8,128)(2,1)}, u32[]{:S(2)}, u32[]{:S(2)}) %collective-permute-start.11) | collective-permute-done | bytes 983072 | tf_op jit(solution)/shard_map/ppermute | solution.py:535
  81.8 2.3 %broadcast_select_fusion.1.refs_1_.refs_20_ = bf16[240,2048]{1,0:T(8,128)(2,1)} fusion(bf16[240,2048]{1,0:T(8,128)(2,1)} %shard_map.122, bf16[240,2048]{1,0:T(8,128)(2,1)} %shard_map.120, pred[]{:T(512)S(6)} %or.3), kind=kLoop, calls=%fused_computation.1 | loop fusion | flops 491520 | bytes 2949121 | tf_op jit(solution)/shard_map/jit(_where)/select_n | solution.py:62
  84.1 4.5 %collective-permute-done.9.refs_0_ = bf16[1024,768]{1,0:T(8,128)(2,1)} collective-permute-done((bf16[1024,768]{1,0:T(8,128)(2,1)}, bf16[1024,768]{1,0:T(8,128)(2,1)}, u32[]{:S(2)}, u32[]{:S(2)}) %collective-permute-start.9) | collective-permute-done | bytes 1572896 | tf_op jit(solution)/shard_map/ppermute | solution.py:527
  88.7 1.9 %collective-permute-start.16 = (bf16[240,2048]{1,0:T(8,128)(2,1)}, bf16[240,2048]{1,0:T(8,128)(2,1)}, u32[]{:S(2)}, u32[]{:S(2)}) collective-permute-start(bf16[240,2048]{1,0:T(8,128)(2,1)} %shard_map.125), channel_id=1, source_target_pairs={{0,2},{1,3},{2,0},{3,1},{4,6},{5,7},{6,4},{7,5},{8,10},{9,11},{10,... | collective-permute-start | bytes 2949128 | tf_op jit(solution)/shard_map/ppermute | solution.py:535
  90.6 1.5 collective-permute-start.14
  92.1 1.5 collective-permute-start.17
  93.6 19.2 %shard_map.126 = (f32[4,240]{1,0:T(4,128)}, f32[4,240]{1,0:T(4,128)}) custom-call(s32[11]{0:T(128)} %stack.73.refs_0_, bf16[1024,1792]{1,0:T(8,128)(2,1)} %refs_1_.7, bf16[1024,1792]{1,0:T(8,128)(2,1)} %refs_2_.7, bf16[1024,1792]{1,0:T(8,128)(2,1)} %collective-permute-done.refs_5_.refs_3_, bf16[1024,1792]{1,0:T(8,128)(2,1)} %collective-permute-done.1.refs_6_.refs_4_, ...), custom_call_target="tpu_custom_call" | custom-call | flops 1 | bytes 1 | tf_op jit(solution)/shard_map/pallas_call | solution.py:282
  113.2 2.3 %broadcast_select_fusion.refs_1_.refs_13_ = bf16[240,2048]{1,0:T(8,128)(2,1)} fusion(bf16[240,2048]{1,0:T(8,128)(2,1)} %shard_map.127, bf16[240,2048]{1,0:T(8,128)(2,1)} %shard_map.125, pred[]{:T(512)S(6)} %or.3), kind=kLoop, calls=%fused_computation | loop fusion | flops 491520 | bytes 2949121 | tf_op jit(solution)/shard_map/jit(_where)/select_n | solution.py:65
  116.1 1.5 collective-permute-start.19
  117.6 1.5 collective-permute-done.18.refs_10_
  119.1 18.1 %shard_map.129 = (f32[4,240]{1,0:T(4,128)}, f32[4,240]{1,0:T(4,128)}) custom-call(s32[11]{0:T(128)} %stack.73.refs_0_, bf16[1024,1792]{1,0:T(8,128)(2,1)} %refs_1_.7, bf16[1024,1792]{1,0:T(8,128)(2,1)} %refs_2_.7, bf16[1024,1792]{1,0:T(8,128)(2,1)} %collective-permute-done.refs_5_.refs_3_, bf16[1024,1792]{1,0:T(8,128)(2,1)} %collective-permute-done.1.refs_6_.refs_4_, ...), custom_call_target="tpu_custom_call" | custom-call | flops 1 | bytes 1 | tf_op jit(solution)/shard_map/pallas_call | solution.py:282
  137.2 1.6 collective-permute-start.20
  138.8 2.4 %collective-permute-done.20.refs_1_ = f32[4,240]{1,0:T(4,128)} collective-permute-done((f32[4,240]{1,0:T(4,128)}, f32[4,240]{1,0:T(4,128)}, u32[]{:S(2)}, u32[]{:S(2)}) %collective-permute-start.20) | collective-permute-done | bytes 3872 | tf_op jit(solution)/shard_map/ppermute | solution.py:539
  141.2 10.2 %shard_map.131 = f32[4,240]{1,0:T(4,128)} custom-call(s32[11]{0:T(128)} %stack.73.refs_0_, bf16[1024,1792]{1,0:T(8,128)(2,1)} %refs_1_.7, bf16[1024,1792]{1,0:T(8,128)(2,1)} %refs_2_.7, bf16[1024,1792]{1,0:T(8,128)(2,1)} %collective-permute-done.refs_5_.refs_3_, bf16[1024,1792]{1,0:T(8,128)(2,1)} %collective-permute-done.1.refs_6_.refs_4_, ...), custom_call_target="tpu_custom_call" | custom-call | flops 1 | bytes 1 | tf_op jit(solution)/shard_map/pallas_call | solution.py:282
  151.4 1.6 collective-permute-start.21
  153.0 1.5 collective-permute-start.22
  154.5 0.8 collective-permute-done.21
  155.3 2.4 %collective-permute-done.22 = f32[4,240]{1,0:T(4,128)S(1)} collective-permute-done((f32[4,240]{1,0:T(4,128)}, f32[4,240]{1,0:T(4,128)S(1)}, u32[]{:S(2)}, u32[]{:S(2)}) %collective-permute-start.22) | collective-permute-done | bytes 3872 | tf_op jit(solution)/shard_map/ppermute | solution.py:696
  157.7 0.7 add_add_fusion.1
  158.4 1.2 collective-permute-start.23
  159.6 2.6 %collective-permute-start.24 = (f32[4,240]{1,0:T(4,128)S(1)}, f32[4,240]{1,0:T(4,128)S(1)}, u32[]{:S(2)}, u32[]{:S(2)}) collective-permute-start(f32[4,240]{1,0:T(4,128)S(1)} %add_add_fusion.1), channel_id=1, source_target_pairs={{0,4},{1,5},{2,6},{3,7},{4,0},{5,1},{6,2},{7,3},{8,12},{9,13},{10,... | collective-permute-start | bytes 11528 | tf_op jit(solution)/shard_map/ppermute | solution.py:535
  162.2 1.7 %collective-permute-start.25 = (f32[4,240]{1,0:T(4,128)S(1)}, f32[4,240]{1,0:T(4,128)S(1)}, u32[]{:S(2)}, u32[]{:S(2)}) collective-permute-start(f32[4,240]{1,0:T(4,128)S(1)} %add_add_fusion.1), channel_id=1, source_target_pairs={{0,6},{1,7},{2,0},{3,1},{4,2},{5,3},{6,4},{7,5},{8,14},{9,15},{10,... | collective-permute-start | bytes 11528 | tf_op jit(solution)/shard_map/ppermute | solution.py:535
  164.2 1.7 %collective-permute-done.25 = f32[4,240]{1,0:T(4,128)S(1)} collective-permute-done((f32[4,240]{1,0:T(4,128)S(1)}, f32[4,240]{1,0:T(4,128)S(1)}, u32[]{:S(2)}, u32[]{:S(2)}) %collective-permute-start.25) | collective-permute-done | bytes 3872 | tf_op jit(solution)/shard_map/ppermute | solution.py:535
  165.8 0.7 reshape.13
  (35 shorter events, 1.9 us)
Async XLA Ops:
  0.6 32.4 %collective-permute-start = (bf16[1024,1792]{1,0:T(8,128)(2,1)}, bf16[1024,1792]{1,0:T(8,128)(2,1)}, u32[]{:S(2)}, u32[]{:S(2)}) collective-permute-start(bf16[1024,1792]{1,0:T(8,128)(2,1)} %refs_1_.7), channel_id=1, source_target_pairs={{0,8},{8,0},{16,24},{24,16},{1,9},{9,1},{17,25},{25,17},{2,10},{10... | collective-permute-start | bytes 11010056 | tf_op jit(solution)/shard_map/ppermute | solution.py:531
  1.1 31.9 %collective-permute-start.1 = (bf16[1024,1792]{1,0:T(8,128)(2,1)}, bf16[1024,1792]{1,0:T(8,128)(2,1)}, u32[]{:S(2)}, u32[]{:S(2)}) collective-permute-start(bf16[1024,1792]{1,0:T(8,128)(2,1)} %refs_2_.7), channel_id=1, source_target_pairs={{0,8},{8,0},{16,24},{24,16},{1,9},{9,1},{17,25},{25,17},{2,10},{10... | collective-permute-start | bytes 11010056 | tf_op jit(solution)/shard_map/ppermute | solution.py:531
  3.5 29.6 %collective-permute-start.3 = (bf16[240,2048]{1,0:T(8,128)(2,1)}, bf16[240,2048]{1,0:T(8,128)(2,1)}, u32[]{:S(2)}, u32[]{:S(2)}) collective-permute-start(bf16[240,2048]{1,0:T(8,128)(2,1)} %dynamic_slice.6.waited_ref), channel_id=1, source_target_pairs={{0,16},{8,24},{16,0},{24,8},{1,17},{9,25},{17,1},{25,9},{2,18},{10... | collective-permute-start | bytes 2949128 | tf_op jit(solution)/shard_map/ppermute | solution.py:527
  13.3 19.8 %collective-permute-start.4 = (bf16[16,5408]{1,0:T(8,128)(2,1)}, bf16[16,5408]{1,0:T(8,128)(2,1)}, u32[]{:S(2)}, u32[]{:S(2)}) collective-permute-start(bf16[16,5408]{1,0:T(8,128)(2,1)} %get-tuple-element.21.waited_ref.own_ref), channel_id=1, source_target_pairs={{0,16},{8,24},{16,0},{24,8},{1,17},{9,25},{17,1},{25,9},{2,18},{10... | collective-permute-start | bytes 519176 | tf_op jit(solution)/shard_map/ppermute | solution.py:527
  16.6 39.5 %collective-permute-start.2 = (bf16[1024,512]{1,0:T(8,128)(2,1)}, bf16[1024,512]{1,0:T(8,128)(2,1)}, u32[]{:S(2)}, u32[]{:S(2)}) collective-permute-start(bf16[1024,512]{1,0:T(8,128)(2,1)} %get-tuple-element.22.refs_2_), channel_id=1, source_target_pairs={{0,16},{8,24},{16,0},{24,8},{1,17},{9,25},{17,1},{25,9},{2,18},{10... | collective-permute-start | bytes 3145736 | tf_op jit(solution)/shard_map/ppermute | solution.py:527
  33.1 23.1 %collective-permute-start.5 = (bf16[240,2048]{1,0:T(8,128)(2,1)}, bf16[240,2048]{1,0:T(8,128)(2,1)}, u32[]{:S(2)}, u32[]{:S(2)}) collective-permute-start(bf16[240,2048]{1,0:T(8,128)(2,1)} %shard_map.114.refs_12_.refs_14_.refs_16_), channel_id=1, source_target_pairs={{0,2},{1,3},{2,0},{3,1},{4,6},{5,7},{6,4},{7,5},{8,10},{9,11},{10,... | collective-permute-start | bytes 2949128 | tf_op jit(solution)/shard_map/ppermute | solution.py:535
  35.3 22.1 %collective-permute-start.7 = (bf16[240,2048]{1,0:T(8,128)(2,1)}, bf16[240,2048]{1,0:T(8,128)(2,1)}, u32[]{:S(2)}, u32[]{:S(2)}) collective-permute-start(bf16[240,2048]{1,0:T(8,128)(2,1)} %shard_map.114.refs_12_.refs_14_.refs_16_), channel_id=1, source_target_pairs={{0,1},{1,0},{2,3},{3,2},{4,5},{5,4},{6,7},{7,6},{8,9},{9,8},{10,11... | collective-permute-start | bytes 2949128 | tf_op jit(solution)/shard_map/ppermute | solution.py:539
  36.8 20.6 %collective-permute-start.10 = (bf16[240,2048]{1,0:T(8,128)(2,1)}, bf16[240,2048]{1,0:T(8,128)(2,1)}, u32[]{:S(2)}, u32[]{:S(2)}) collective-permute-start(bf16[240,2048]{1,0:T(8,128)(2,1)} %shard_map.114.refs_12_.refs_14_.refs_16_), channel_id=1, source_target_pairs={{2,4},{3,5},{4,2},{5,3},{10,12},{11,13},{12,10},{13,11},{18,20},{1... | collective-permute-start | bytes 2949128 | tf_op jit(solution)/shard_map/ppermute | solution.py:535
  41.0 1.8 %collective-permute-start.6 = (bf16[32,2944]{1,0:T(8,128)(2,1)}, bf16[32,2944]{1,0:T(8,128)(2,1)}, u32[]{:S(2)}, u32[]{:S(2)}) collective-permute-start(bf16[32,2944]{1,0:T(8,128)(2,1)} %get-tuple-element.26), channel_id=1, source_target_pairs={{0,8},{8,0},{16,24},{24,16},{1,9},{9,1},{17,25},{25,17},{2,10},{10... | collective-permute-start | bytes 565256 | tf_op jit(solution)/shard_map/ppermute | solution.py:531
  42.8 45.8 %collective-permute-start.9 = (bf16[1024,768]{1,0:T(8,128)(2,1)}, bf16[1024,768]{1,0:T(8,128)(2,1)}, u32[]{:S(2)}, u32[]{:S(2)}) collective-permute-start(bf16[1024,768]{1,0:T(8,128)(2,1)} %shard_map.119), channel_id=1, source_target_pairs={{0,16},{8,24},{16,0},{24,8},{1,17},{9,25},{17,1},{25,9},{2,18},{10... | collective-permute-start | bytes 4718600 | tf_op jit(solution)/shard_map/ppermute | solution.py:527
  57.3 8.6 %collective-permute-start.8 = (bf16[1024,512]{1,0:T(8,128)(2,1)}, bf16[1024,512]{1,0:T(8,128)(2,1)}, u32[]{:S(2)}, u32[]{:S(2)}) collective-permute-start(bf16[1024,512]{1,0:T(8,128)(2,1)} %shard_map.118.refs_5_.refs_1_), channel_id=1, source_target_pairs={{0,8},{8,0},{16,24},{24,16},{1,9},{9,1},{17,25},{25,17},{2,10},{10... | collective-permute-start | bytes 3145736 | tf_op jit(solution)/shard_map/ppermute | solution.py:531
  57.3 24.5 %collective-permute-start.11 = (bf16[240,2048]{1,0:T(8,128)(2,1)}, bf16[240,2048]{1,0:T(8,128)(2,1)}, u32[]{:S(2)}, u32[]{:S(2)}) collective-permute-start(bf16[240,2048]{1,0:T(8,128)(2,1)} %shard_map.120), channel_id=1, source_target_pairs={{0,2},{1,3},{2,0},{3,1},{4,6},{5,7},{6,4},{7,5},{8,10},{9,11},{10,... | collective-permute-start | bytes 2949128 | tf_op jit(solution)/shard_map/ppermute | solution.py:535
  61.9 26.8 %collective-permute-start.12 = (bf16[240,2048]{1,0:T(8,128)(2,1)}, bf16[240,2048]{1,0:T(8,128)(2,1)}, u32[]{:S(2)}, u32[]{:S(2)}) collective-permute-start(bf16[240,2048]{1,0:T(8,128)(2,1)} %shard_map.117.refs_1_.refs_16_.refs_18_), channel_id=1, source_target_pairs={{0,1},{1,0},{2,3},{3,2},{4,5},{5,4},{6,7},{7,6},{8,9},{9,8},{10,11... | collective-permute-start | bytes 2949128 | tf_op jit(solution)/shard_map/ppermute | solution.py:539
  64.3 24.3 %collective-permute-start.15 = (bf16[240,2048]{1,0:T(8,128)(2,1)}, bf16[240,2048]{1,0:T(8,128)(2,1)}, u32[]{:S(2)}, u32[]{:S(2)}) collective-permute-start(bf16[240,2048]{1,0:T(8,128)(2,1)} %shard_map.117.refs_1_.refs_16_.refs_18_), channel_id=1, source_target_pairs={{2,4},{3,5},{4,2},{5,3},{10,12},{11,13},{12,10},{13,11},{18,20},{1... | collective-permute-start | bytes 2949128 | tf_op jit(solution)/shard_map/ppermute | solution.py:535
  88.7 4.9 %collective-permute-start.13 = (bf16[1024,768]{1,0:T(8,128)(2,1)}, bf16[1024,768]{1,0:T(8,128)(2,1)}, u32[]{:S(2)}, u32[]{:S(2)}) collective-permute-start(bf16[1024,768]{1,0:T(8,128)(2,1)} %shard_map.123.refs_7_), channel_id=1, source_target_pairs={{0,8},{8,0},{16,24},{24,16},{1,9},{9,1},{17,25},{25,17},{2,10},{10... | collective-permute-start | bytes 4718600 | tf_op jit(solution)/shard_map/ppermute | solution.py:531
  88.7 24.6 %collective-permute-start.16 = (bf16[240,2048]{1,0:T(8,128)(2,1)}, bf16[240,2048]{1,0:T(8,128)(2,1)}, u32[]{:S(2)}, u32[]{:S(2)}) collective-permute-start(bf16[240,2048]{1,0:T(8,128)(2,1)} %shard_map.125), channel_id=1, source_target_pairs={{0,2},{1,3},{2,0},{3,1},{4,6},{5,7},{6,4},{7,5},{8,10},{9,11},{10,... | collective-permute-start | bytes 2949128 | tf_op jit(solution)/shard_map/ppermute | solution.py:535
  90.6 25.5 %collective-permute-start.14 = (bf16[1024,512]{1,0:T(8,128)(2,1)}, bf16[1024,512]{1,0:T(8,128)(2,1)}, u32[]{:S(2)}, u32[]{:S(2)}) collective-permute-start(bf16[1024,512]{1,0:T(8,128)(2,1)} %shard_map.124), channel_id=1, source_target_pairs={{0,16},{8,24},{16,0},{24,8},{1,17},{9,25},{17,1},{25,9},{2,18},{10... | collective-permute-start | bytes 3145736 | tf_op jit(solution)/shard_map/ppermute | solution.py:527
  92.1 23.9 %collective-permute-start.17 = (bf16[240,2048]{1,0:T(8,128)(2,1)}, bf16[240,2048]{1,0:T(8,128)(2,1)}, u32[]{:S(2)}, u32[]{:S(2)}) collective-permute-start(bf16[240,2048]{1,0:T(8,128)(2,1)} %broadcast_select_fusion.1.refs_1_.refs_20_), channel_id=1, source_target_pairs={{0,1},{1,0},{2,3},{3,2},{4,5},{5,4},{6,7},{7,6},{8,9},{9,8},{10,11... | collective-permute-start | bytes 2949128 | tf_op jit(solution)/shard_map/ppermute | solution.py:539
  116.1 3.0 %collective-permute-start.18 = (bf16[1024,512]{1,0:T(8,128)(2,1)}, bf16[1024,512]{1,0:T(8,128)(2,1)}, u32[]{:S(2)}, u32[]{:S(2)}) collective-permute-start(bf16[1024,512]{1,0:T(8,128)(2,1)} %shard_map.128.refs_9_), channel_id=1, source_target_pairs={{0,8},{8,0},{16,24},{24,16},{1,9},{9,1},{17,25},{25,17},{2,10},{10... | collective-permute-start | bytes 3145736 | tf_op jit(solution)/shard_map/ppermute | solution.py:531
  116.1 25.1 %collective-permute-start.19 = (bf16[240,2048]{1,0:T(8,128)(2,1)}, bf16[240,2048]{1,0:T(8,128)(2,1)}, u32[]{:S(2)}, u32[]{:S(2)}) collective-permute-start(bf16[240,2048]{1,0:T(8,128)(2,1)} %broadcast_select_fusion.refs_1_.refs_13_), channel_id=1, source_target_pairs={{0,1},{1,0},{2,3},{3,2},{4,5},{5,4},{6,7},{7,6},{8,9},{9,8},{10,11... | collective-permute-start | bytes 2949128 | tf_op jit(solution)/shard_map/ppermute | solution.py:539
  137.2 4.0 %collective-permute-start.20 = (f32[4,240]{1,0:T(4,128)}, f32[4,240]{1,0:T(4,128)}, u32[]{:S(2)}, u32[]{:S(2)}) collective-permute-start(f32[4,240]{1,0:T(4,128)} %get-tuple-element.37), channel_id=1, source_target_pairs={{0,1},{1,0},{2,3},{3,2},{4,5},{5,4},{6,7},{7,6},{8,9},{9,8},{10,11... | collective-permute-start | bytes 11528 | tf_op jit(solution)/shard_map/ppermute | solution.py:539
  151.4 3.9 %collective-permute-start.21 = (f32[4,240]{1,0:T(4,128)}, f32[4,240]{1,0:T(4,128)S(1)}, u32[]{:S(2)}, u32[]{:S(2)}) collective-permute-start(f32[4,240]{1,0:T(4,128)} %shard_map.131), channel_id=1, source_target_pairs={{0,16},{8,24},{16,0},{24,8},{1,17},{9,25},{17,1},{25,9},{2,18},{10... | collective-permute-start | bytes 11528 | tf_op jit(solution)/shard_map/ppermute | solution.py:527
  153.0 4.7 %collective-permute-start.22 = (f32[4,240]{1,0:T(4,128)}, f32[4,240]{1,0:T(4,128)S(1)}, u32[]{:S(2)}, u32[]{:S(2)}) collective-permute-start(f32[4,240]{1,0:T(4,128)} %shard_map.131), channel_id=1, source_target_pairs={{0,17},{1,16},{2,19},{3,18},{4,21},{5,20},{6,23},{7,22},{8,25},{9,... | collective-permute-start | bytes 11528 | tf_op jit(solution)/shard_map/ppermute | solution.py:696
  158.4 5.5 %collective-permute-start.23 = (f32[4,240]{1,0:T(4,128)S(1)}, f32[4,240]{1,0:T(4,128)S(1)}, u32[]{:S(2)}, u32[]{:S(2)}) collective-permute-start(f32[4,240]{1,0:T(4,128)S(1)} %add_add_fusion.1), channel_id=1, source_target_pairs={{0,2},{1,3},{2,4},{3,5},{4,6},{5,7},{6,0},{7,1},{8,10},{9,11},{10,... | collective-permute-start | bytes 11528 | tf_op jit(solution)/shard_map/ppermute | solution.py:535
  159.6 4.5 %collective-permute-start.24 = (f32[4,240]{1,0:T(4,128)S(1)}, f32[4,240]{1,0:T(4,128)S(1)}, u32[]{:S(2)}, u32[]{:S(2)}) collective-permute-start(f32[4,240]{1,0:T(4,128)S(1)} %add_add_fusion.1), channel_id=1, source_target_pairs={{0,4},{1,5},{2,6},{3,7},{4,0},{5,1},{6,2},{7,3},{8,12},{9,13},{10,... | collective-permute-start | bytes 11528 | tf_op jit(solution)/shard_map/ppermute | solution.py:535
  162.2 3.6 %collective-permute-start.25 = (f32[4,240]{1,0:T(4,128)S(1)}, f32[4,240]{1,0:T(4,128)S(1)}, u32[]{:S(2)}, u32[]{:S(2)}) collective-permute-start(f32[4,240]{1,0:T(4,128)S(1)} %add_add_fusion.1), channel_id=1, source_target_pairs={{0,6},{1,7},{2,0},{3,1},{4,2},{5,3},{6,4},{7,5},{8,14},{9,15},{10,... | collective-permute-start | bytes 11528 | tf_op jit(solution)/shard_map/ppermute | solution.py:535
